TPU v7x, 256 devices: a whole 4x4x8 slice. The times are simulated.
256 devices in a mesh: seq: 32 (over z, y_hi, core), tp: 8 (over x, y_lo).
Axes of the slice: x: 4, y: 4 (y_hi: 2, y_lo: 2; y = y_hi * 2 + y_lo), z: 8, core: 2. Of those that a mesh axis runs over, the one named last changes fastest.
Arguments:
- queries: bfloat16 [8192, 8192], P('seq', 'tp'), may hold values from -128 to 128
- keys: bfloat16 [8192, 1024], P('seq', 'tp'), may hold values from -4 to 4
- values: bfloat16 [8192, 1024], P('seq', 'tp'), may hold values from -4 to 4
- out_weight: bfloat16 [8192, 4096], P('tp'), may hold values from -0.25 to 0.25
- step_queries: bfloat16 [32, 8192], P('seq', 'tp'), may hold values from -128 to 128
- new_keys: bfloat16 [32, 1024], P('seq', 'tp'), may hold values from -4 to 4
- new_values: bfloat16 [32, 1024], P('seq', 'tp'), may hold values from -4 to 4
- key_cache: bfloat16 [32, 4096, 1024], P('seq', None, 'tp'), may hold values from -4 to 4
- value_cache: bfloat16 [32, 4096, 1024], P('seq', None, 'tp'), may hold values from -4 to 4
- cache_lens: int32 [32], P('seq'), may hold values from 2 to 4096
Outputs:
- prefill_out: bfloat16 [8192, 4096], P(('seq', 'tp'))
- decode_out: bfloat16 [32, 4096], P('seq', 'tp')
All inputs are finite; a program needn't handle non-finite values.
Results may differ from a plain program's by a relative error of at most 0.019.
Values may be sent and summed in bfloat16 or wider, within the bound.
No kernel may reach another device: no remote copies, remote signals or barrier semaphores. Data moves between devices by JAX's collectives and lax.ppermute only.
A program may use at most 192 MiB of HBM per device.

v0:
```python
import functools
import math

import jax
import jax.numpy as jnp
from jax import lax
from jax.experimental import pallas as pl
from jax.experimental.pallas import tpu as pltpu
from jax.sharding import PartitionSpec as P

HEAD = 128
SCALE = HEAD ** -0.5 * math.log2(math.e)
LOW = -1e30
STEP_ROWS = 16
STEP_ROWS = 16
NT = (((1,), (1,)), ((), ()))
EDGES, HALF, OWN, OTHER = 0, 4, 4, 7
Z, YH, CORE = 8, 2, 2


def seq_pairs(move):
    pairs = []
    for z in range(Z):
        for yh in range(YH):
            for c in range(CORE):
                z2, yh2, c2 = move(z, yh, c)
                pairs.append(((z * YH + yh) * CORE + c, ((z2 % Z) * YH + yh2) * CORE + c2))
    return pairs


SWAP_Y = seq_pairs(lambda z, yh, c: (z, 1 - yh, c))
SWAP_CORE = seq_pairs(lambda z, yh, c: (z, yh, 1 - c))
SWAP_BOTH = seq_pairs(lambda z, yh, c: (z, 1 - yh, 1 - c))
FAR = seq_pairs(lambda z, yh, c: (z + Z // 2, yh, c))
RING = seq_pairs(lambda z, yh, c: (z + 1 if c == 0 else z - 1, yh, c))


def split_queries(q_ref, q2_ref, rows, heads):
    for h in range(heads):
        scaled = q_ref[:, h * HEAD:(h + 1) * HEAD].astype(jnp.float32) * SCALE
        high = scaled.astype(jnp.bfloat16)
        low = (scaled - high.astype(jnp.float32)).astype(jnp.bfloat16)
        q2_ref[h * rows:(h + 1) * rows, :HEAD] = high
        q2_ref[h * rows:(h + 1) * rows, HEAD:] = low


def spread(sources, k2_ref, v2_ref, at, rows):
    for src in sources:
        for b in range(src.shape[0] // (2 * rows)):
            k = src[2 * b * rows:(2 * b + 1) * rows, :]
            v = src[(2 * b + 1) * rows:(2 * b + 2) * rows, :]
            k2_ref[at:at + rows, :HEAD] = k
            k2_ref[at:at + rows, HEAD:] = k
            v2_ref[at:at + rows, :HEAD] = v
            v2_ref[at:at + rows, HEAD:] = jnp.ones_like(v)
            at += rows


def attend(q2_ref, k2_ref, v2_ref, n, m_ref, acc_ref, m_out, acc_out, rows, heads, mask=None):
    first = m_ref is None
    together = heads // 2 if heads % 2 == 0 else heads

    def some_heads(i, _):
        parts = [pl.ds(pl.multiple_of((i * together + j) * rows, rows), rows) for j in range(together)]
        scores = [
            lax.dot_general(q2_ref[part, :], k2_ref[:n, :], NT, preferred_element_type=jnp.float32) for part in parts
        ]
        for part, s in zip(parts, scores):
            if mask is not None:
                s = jnp.where(mask, s, LOW)
            peak = jnp.max(s, axis=1, keepdims=True)
            if not first:
                old = m_ref[part, :1]
                peak = jnp.maximum(old, peak)
            p = jnp.exp2(s - peak).astype(jnp.bfloat16)
            mixed = jnp.dot(p, v2_ref[:n, :], preferred_element_type=jnp.float32)
            if not first:
                mixed = mixed + acc_ref[part, :] * jnp.exp2(old - peak)
            acc_out[part, :] = mixed
            m_out[part, :] = jnp.broadcast_to(peak, (rows, HEAD))
        return 0

    lax.fori_loop(0, heads // together, some_heads, 0)


def local_kernel(flag_ref, q_ref, kv_ref, q2_ref, m_ref, acc_ref, k2_ref, v2_ref, *, rows, heads):
    split_queries(q_ref, q2_ref, rows, heads)
    spread([kv_ref], k2_ref, v2_ref, 0, rows)
    row = lax.broadcasted_iota(jnp.int32, (rows, rows), 0)
    col = lax.broadcasted_iota(jnp.int32, (rows, rows), 1)
    mask = jnp.concatenate([(row - col) >= flag_ref[EDGES + b] for b in range(4)], axis=1)
    attend(q2_ref, k2_ref, v2_ref, 4 * rows, None, None, m_ref, acc_ref, rows, heads, mask)


def attend_live(flag_ref, at, q2_ref, groups, k2_ref, v2_ref, m_in, acc_in, m_ref, acc_ref, rows, heads):
    n = 4 * rows
    live = [flag_ref[i] == 1 for i in at]
    if len(groups) == 1:
        some, one = live[0], live[0]
    else:
        some, one = jnp.logical_or(*live), jnp.logical_xor(*live)

        @pl.when(jnp.logical_and(*live))
        def _():
            spread(groups[0], k2_ref, v2_ref, 0, rows)
            spread(groups[1], k2_ref, v2_ref, n, rows)
            attend(q2_ref, k2_ref, v2_ref, 2 * n, m_in, acc_in, m_ref, acc_ref, rows, heads)

    @pl.when(one)
    def _():
        for here, group in zip(live, groups):
            @pl.when(here)
            def _():
                spread(group, k2_ref, v2_ref, 0, rows)

        attend(q2_ref, k2_ref, v2_ref, n, m_in, acc_in, m_ref, acc_ref, rows, heads)

    @pl.when(jnp.logical_not(some))
    def _():
        m_ref[...] = m_in[...]
        acc_ref[...] = acc_in[...]


def step_kernel(flag_ref, q2_ref, *refs, rows, heads, at, counts):
    groups = [refs[:counts[0]], refs[counts[0]:sum(counts)]]
    m_in, acc_in, m_ref, acc_ref, k2_ref, v2_ref = refs[sum(counts):]
    attend_live(flag_ref, at, q2_ref, groups, k2_ref, v2_ref, m_in, acc_in, m_ref, acc_ref, rows, heads)


def last_kernel(flag_ref, q2_ref, other_ref, m_in, acc_in, step_ref, w_hbm, out_ref, att_ref,
                acc_ref, m_ref, k2_ref, v2_ref, w_ref, w_sem, *, rows, heads, n_tp):
    w_copy = pltpu.make_async_copy(w_hbm, w_ref, w_sem)
    w_copy.start()
    attend_live(flag_ref, (OTHER + 3,), q2_ref, [[other_ref]], k2_ref, v2_ref,
                m_in, acc_in, m_ref, acc_ref, rows, heads)
    for h in range(heads):
        cols = slice(h * HEAD, (h + 1) * HEAD)
        acc = acc_ref[h * rows:(h + 1) * rows, :]
        att_ref[:rows, cols] = (acc[:, :HEAD] / acc[:, HEAD:]).astype(jnp.bfloat16)
        att_ref[rows:, cols] = jnp.broadcast_to(step_ref[h:h + 1, :], (STEP_ROWS, HEAD)).astype(jnp.bfloat16)
    w_copy.wait()
    each, wide = rows // n_tp, w_ref.shape[1] // n_tp
    for g in range(n_tp):
        part = jnp.dot(att_ref[...], w_ref[:, g * wide:(g + 1) * wide], preferred_element_type=jnp.float32)
        part = part.astype(jnp.bfloat16)
        for t in range(n_tp):
            out_ref[t, g * each:(g + 1) * each, :] = part[t * each:(t + 1) * each, :]
        out_ref[g, rows:, :] = part[rows:, :]


def sum_kernel(parts_ref, out_ref, step_ref, *, n_tp):
    each, wide = out_ref.shape[0], parts_ref.shape[2]
    rows = parts_ref.shape[1] - STEP_ROWS
    for g in range(n_tp):
        total = parts_ref[0, g * each:(g + 1) * each, :].astype(jnp.float32)
        for t in range(1, n_tp):
            total = total + parts_ref[t, g * each:(g + 1) * each, :].astype(jnp.float32)
        out_ref[:, g * wide:(g + 1) * wide] = total.astype(jnp.bfloat16)
    total = parts_ref[0, rows:, :].astype(jnp.float32)
    for t in range(1, n_tp):
        total = total + parts_ref[t, rows:, :].astype(jnp.float32)
    step_ref[...] = total[:1, :].astype(jnp.bfloat16)


def decode_kernel(len_ref, q_ref, nk_ref, nv_ref, k_hbm, v_hbm, out_ref, k_ref, v_ref, k_sem, v_sem, *, heads):
    k_copy = pltpu.make_async_copy(k_hbm.at[0], k_ref, k_sem)
    v_copy = pltpu.make_async_copy(v_hbm.at[0], v_ref, v_sem)
    k_copy.start()
    v_copy.start()
    query = jnp.concatenate([q_ref[:, h * HEAD:(h + 1) * HEAD] for h in range(heads)], axis=0).astype(jnp.float32)
    scaled = query * SCALE
    high = scaled.astype(jnp.bfloat16)
    low = (scaled - high.astype(jnp.float32)).astype(jnp.bfloat16)
    both = jnp.concatenate([high, low], axis=0)
    own = jnp.sum(query * nk_ref[...].astype(jnp.float32), axis=1, keepdims=True) * SCALE
    k_copy.wait()
    s = lax.dot_general(both, k_ref[...], NT, preferred_element_type=jnp.float32)
    s = s[:heads, :] + s[heads:, :]
    slot = lax.broadcasted_iota(jnp.int32, s.shape, 1)
    s = jnp.where(slot < len_ref[0], s, LOW)
    peak = jnp.maximum(jnp.max(s, axis=1, keepdims=True), own)
    p = jnp.exp2(s - peak)
    own = jnp.exp2(own - peak)
    total = jnp.sum(p, axis=1, keepdims=True) + own
    v_copy.wait()
    mixed = jnp.dot(p.astype(jnp.bfloat16), v_ref[...], preferred_element_type=jnp.float32)
    mixed = mixed + own.astype(jnp.bfloat16).astype(jnp.float32) * nv_ref[...].astype(jnp.float32)
    out_ref[...] = mixed / total


def pack_own_kernel(k_hbm, v_hbm, out_ref, k_sem, v_sem):
    rows = k_hbm.shape[0]
    k_copy = pltpu.make_async_copy(k_hbm, out_ref.at[pl.ds(0, rows)], k_sem)
    v_copy = pltpu.make_async_copy(v_hbm, out_ref.at[pl.ds(rows, rows)], v_sem)
    k_copy.start()
    v_copy.start()
    k_copy.wait()
    v_copy.wait()


def pack_here_kernel(own_ref, both_ref, core_ref, far_ref, y_ref, _, here_ref, far_out_ref):
    at = 0
    for ref in (own_ref, y_ref, core_ref, both_ref):
        here_ref[at:at + ref.shape[0], :] = ref[...]
        at += ref.shape[0]
    far_out_ref[...] = far_ref[...]


def gate_kernel(*_):
    pass


def after(block, *others):
    anywhere = pl.BlockSpec(memory_space=pl.ANY)
    return pl.pallas_call(
        gate_kernel,
        in_specs=[anywhere] * (1 + len(others)),
        out_specs=anywhere,
        out_shape=jax.ShapeDtypeStruct(block.shape, block.dtype),
        input_output_aliases={0: 0},
        compiler_params=pltpu.CompilerParams(vmem_limit_bytes=2**20),
        name="gate",
    )(block, *others)


def body(queries, keys, values, out_weight, step_queries, new_keys, new_values, key_cache, value_cache, cache_lens):
    rows = queries.shape[0]
    heads = queries.shape[1] // HEAD
    n_tp = lax.axis_size("tp")
    width = out_weight.shape[1]
    seq = lax.axis_index("seq")
    z, yh, core = seq // (YH * CORE), seq // CORE % YH, seq % CORE
    vmem = pl.BlockSpec(memory_space=pltpu.VMEM)
    smem = pl.BlockSpec(memory_space=pltpu.SMEM)
    anywhere = pl.BlockSpec(memory_space=pl.ANY)

    def params(mib):
        return pltpu.CompilerParams(vmem_limit_bytes=mib * 2**20)

    def cost(keys_seen, more_flops=0):
        return pl.CostEstimate(
            flops=4 * heads * rows * keys_seen * 256 + more_flops,
            bytes_accessed=2**20,
            transcendentals=heads * rows * keys_seen,
        )

    def send(block, pairs):
        return lax.ppermute(block, "seq", pairs)

    own_ring = [jnp.where(core == 0, z >= k, z + k >= Z) for k in range(1, 4)]
    other_ring = [jnp.where(core == 0, z + k >= Z, z >= k) for k in range(1, 4)]
    edges = [jnp.int32(0)] + [jnp.where(c == 1, -rows, rows) for c in (yh, core, yh)]
    flags = jnp.stack([x.astype(jnp.int32) for x in edges + [z >= Z // 2] + own_ring + other_ring])

    own = pl.pallas_call(
        pack_own_kernel,
        in_specs=[anywhere] * 2,
        out_specs=vmem,
        out_shape=jax.ShapeDtypeStruct((2 * rows, HEAD), jnp.bfloat16),
        scratch_shapes=[pltpu.SemaphoreType.DMA] * 2,
        compiler_params=params(60),
        name="pack_own",
    )(keys, values)
    by_core, far, by_y = (send(own, p) for p in (SWAP_CORE, FAR, SWAP_Y))
    step_attention = pl.pallas_call(
        functools.partial(decode_kernel, heads=heads),
        in_specs=[smem] + [vmem] * 3 + [anywhere] * 2,
        out_specs=vmem,
        out_shape=jax.ShapeDtypeStruct((heads, HEAD), jnp.float32),
        scratch_shapes=[pltpu.VMEM(key_cache.shape[1:], jnp.bfloat16)] * 2 + [pltpu.SemaphoreType.DMA] * 2,
        compiler_params=params(60),
        cost_estimate=pl.CostEstimate(flops=10**9, bytes_accessed=2 * 2**20, transcendentals=heads * key_cache.shape[1]),
        name="decode",
    )(cache_lens, step_queries, new_keys, new_values, key_cache, value_cache)
    by_y = after(by_y, step_attention)
    by_both = send(by_y, SWAP_CORE)
    here, far = pl.pallas_call(
        pack_here_kernel,
        in_specs=[vmem] * 5 + [smem],
        out_specs=[vmem] * 2,
        out_shape=[jax.ShapeDtypeStruct((n * rows, HEAD), jnp.bfloat16) for n in (8, 2)],
        compiler_params=params(4),
        name="pack_here",
    )(own, by_both, by_core, far, by_y, flags)
    ring_1 = send(here, RING)
    fars = [far] + [send(far, p) for p in (SWAP_CORE, SWAP_BOTH, SWAP_Y)]

    state = (
        jax.ShapeDtypeStruct((heads * rows, HEAD), jnp.float32),
        jax.ShapeDtypeStruct((heads * rows, 2 * HEAD), jnp.float32),
    )
    q2, m, acc = pl.pallas_call(
        functools.partial(local_kernel, rows=rows, heads=heads),
        in_specs=[smem, vmem, vmem],
        out_specs=[vmem] * 3,
        out_shape=(jax.ShapeDtypeStruct((heads * rows, 2 * HEAD), jnp.bfloat16),) + state,
        scratch_shapes=[pltpu.VMEM((4 * rows, 2 * HEAD), jnp.bfloat16)] * 2,
        compiler_params=params(36),
        cost_estimate=cost(4 * rows),
        name="attend_local",
    )(flags, queries, here)

    def step(name, at, groups, m, acc):
        counts = [len(group) for group in groups]
        n = sum(counts)
        return pl.pallas_call(
            functools.partial(step_kernel, rows=rows, heads=heads, at=at, counts=counts),
            in_specs=[smem] + [vmem] * (3 + n),
            out_specs=[vmem] * 2,
            out_shape=state,
            input_output_aliases={2 + n: 0, 3 + n: 1},
            scratch_shapes=[pltpu.VMEM((8 * rows, 2 * HEAD), jnp.bfloat16)] * 2,
            compiler_params=params(36),
            cost_estimate=cost(8 * rows),
            name=name,
        )(flags, q2, *groups[0], *groups[1], m, acc)

    ring_1 = after(ring_1, m)
    ring_2, other_1 = send(ring_1, RING), send(ring_1, SWAP_CORE)
    m, acc = step("attend_1", (OWN + 1, HALF), [[ring_1], fars], m, acc)
    ring_2 = after(ring_2, m)
    ring_3, other_2 = send(ring_2, RING), send(ring_2, SWAP_CORE)
    m, acc = step("attend_2", (OTHER + 1, OWN + 2), [[other_1], [ring_2]], m, acc)
    ring_3 = after(ring_3, m)
    other_3 = send(ring_3, SWAP_CORE)
    m, acc = step("attend_3", (OTHER + 2, OWN + 3), [[other_2], [ring_3]], m, acc)

    partial = pl.pallas_call(
        functools.partial(last_kernel, rows=rows, heads=heads, n_tp=n_tp),
        in_specs=[smem] + [vmem] * 5 + [anywhere],
        out_specs=vmem,
        out_shape=jax.ShapeDtypeStruct((n_tp, rows + STEP_ROWS, width // n_tp), jnp.bfloat16),
        scratch_shapes=[
            pltpu.VMEM((rows + STEP_ROWS, heads * HEAD), jnp.bfloat16),
            pltpu.VMEM(state[1].shape, jnp.float32),
            pltpu.VMEM(state[0].shape, jnp.float32),
            pltpu.VMEM((4 * rows, 2 * HEAD), jnp.bfloat16),
            pltpu.VMEM((4 * rows, 2 * HEAD), jnp.bfloat16),
            pltpu.VMEM(out_weight.shape, jnp.bfloat16),
            pltpu.SemaphoreType.DMA,
        ],
        compiler_params=params(44),
        cost_estimate=cost(4 * rows, 2 * rows * heads * HEAD * width),
        name="attend_project",
    )(flags, q2, other_3, m, acc, step_attention, out_weight)
    swapped = lax.all_to_all(partial, "tp", 0, 0)
    prefill_out, decode_out = pl.pallas_call(
        functools.partial(sum_kernel, n_tp=n_tp),
        in_specs=[vmem],
        out_specs=[vmem] * 2,
        out_shape=(
            jax.ShapeDtypeStruct((rows // n_tp, width), jnp.bfloat16),
            jax.ShapeDtypeStruct((1, width // n_tp), jnp.bfloat16),
        ),
        compiler_params=params(24),
        name="sum_parts",
    )(swapped)
    return prefill_out, decode_out


def solution(mesh):
    return jax.shard_map(
        body,
        mesh=mesh,
        in_specs=(
            P("seq", "tp"),
            P("seq", "tp"),
            P("seq", "tp"),
            P("tp", None),
            P("seq", "tp"),
            P("seq", "tp"),
            P("seq", "tp"),
            P("seq", None, "tp"),
            P("seq", None, "tp"),
            P("seq"),
        ),
        out_specs=(P(("seq", "tp"), None), P("seq", "tp")),
        check_vma=False,
    )
```

profile of v0, /device:TPU:128, one launch (start us, length us, event | category | flops | bytes accessed | tf_op | source)
XLA Modules:
  0.0 93.4 jit_solution(15620032840927985647)
XLA Ops:
  0.6 1.5 %pack_own.1.own_ref = bf16[512,128]{1,0:T(8,128)(2,1)} custom-call(bf16[256,128]{1,0:T(8,128)(2,1)} %k_hbm.2, bf16[256,128]{1,0:T(8,128)(2,1)} %v_hbm.2), custom_call_target="tpu_custom_call" | custom-call | tf_op jit(solution)/shard_map/pack_own/pallas_call | solution.py:255
  2.2 0.0 copy-start
  2.2 3.3 %collective-permute-start = (bf16[512,128]{1,0:T(8,128)(2,1)}, bf16[512,128]{1,0:T(8,128)(2,1)S(1)}, u32[]{:S(2)}, u32[]{:S(2)}) collective-permute-start(bf16[512,128]{1,0:T(8,128)(2,1)} %pack_own.1.own_ref), channel_id=1, source_target_pairs={{0,16},{8,24},{16,0},{24,8},{32,48},{40,56},{48,32},{56,40},{64,80... | collective-permute-start | bytes 393224 | tf_op jit(solution)/shard_map/ppermute | solution.py:248
  5.5 0.0 collective-permute-start.3
  5.5 0.0 collective-permute-start.2
  6.1 0.0 copy-start.3
  6.1 3.4 %decode.1.__1_.step_ref = f32[8,128]{1,0:T(8,128)} custom-call(s32[1]{0:T(128)S(6)} %copy.32.len_ref, bf16[1,1024]{1,0:T(2,128)(2,1)} %q_ref.2, bf16[1,128]{1,0:T(2,128)(2,1)} %nk_ref.1, bf16[1,128]{1,0:T(2,128)(2,1)} %nv_ref.1, bf16[1,4096,128]{2,1,0:T(8,128)(2,1)} %k_hbm.3, bf16[1,4096,128]{2,1,0:T(8,128)(2,1)} %v_hbm.3), custom_call_target="tpu_custom_call" | custom-call | flops 1000000000 | bytes 2097152 | tf_op jit(solution)/shard_map/decode/pallas_call | solution.py:265
  9.6 0.0 collective-permute-done.__0_
  9.6 0.0 copy-start.1
  9.6 0.7 copy-done.1
  10.3 0.5 collective-permute-start.1
  10.8 0.1 stack.68._.flag_ref
  10.9 5.8 %collective-permute-done.3.far_ref = bf16[512,128]{1,0:T(8,128)(2,1)S(1)} collective-permute-done((bf16[512,128]{1,0:T(8,128)(2,1)}, bf16[512,128]{1,0:T(8,128)(2,1)S(1)}, u32[]{:S(2)}, u32[]{:S(2)}) %collective-permute-start.3) | collective-permute-done | bytes 131104 | tf_op jit(solution)/shard_map/ppermute | solution.py:248
  16.6 0.0 collective-permute-done.2.core_ref
  16.6 0.0 collective-permute-done.1.both_ref
  16.6 0.0 copy-done
  16.7 0.6 pack_here.1
  17.2 1.8 %collective-permute-start.4 = (bf16[2048,128]{1,0:T(8,128)(2,1)S(1)}, bf16[2048,128]{1,0:T(8,128)(2,1)S(1)}, u32[]{:S(2)}, u32[]{:S(2)}) collective-permute-start(bf16[2048,128]{1,0:T(8,128)(2,1)S(1)} %get-tuple-element.13.kv_ref), channel_id=1, source_target_pairs={{0,32},{8,232},{16,48},{24,248},{32,64},{40,8},{48,80},{56,24},{64... | collective-permute-start | bytes 1572872 | tf_op jit(solution)/shard_map/ppermute | solution.py:248
  19.1 0.4 collective-permute-start.8
  19.4 0.5 collective-permute-start.7
  20.0 2.7 %collective-permute-start.6 = (bf16[512,128]{1,0:T(8,128)(2,1)S(1)}, bf16[512,128]{1,0:T(8,128)(2,1)S(1)}, u32[]{:S(2)}, u32[]{:S(2)}) collective-permute-start(bf16[512,128]{1,0:T(8,128)(2,1)S(1)} %get-tuple-element.16.refs_1_), channel_id=1, source_target_pairs={{0,8},{8,0},{16,24},{24,16},{32,40},{40,32},{48,56},{56,48},{64,72... | collective-permute-start | bytes 393224 | tf_op jit(solution)/shard_map/ppermute | solution.py:248
  22.7 0.0 copy-done.3
  22.7 4.3 %attend_local.1 = (bf16[2048,256]{1,0:T(8,128)(2,1)S(1)}, f32[2048,128]{1,0:T(8,128)S(1)}, f32[2048,256]{1,0:T(8,128)S(1)}) custom-call(s32[11]{0:T(128)S(1)} %stack.68._.flag_ref, bf16[256,1024]{1,0:T(8,128)(2,1)S(1)} %copy-done.3, bf16[2048,128]{1,0:T(8,128)(2,1)S(1)} %get-tuple-element.13.kv_ref), custom_call_target="tpu_custom_call" | custom-call | flops 2147483648 | bytes 1048576 | tf_op jit(solution)/shard_map/attend_local/pallas_call | solution.py:292
  27.1 0.7 collective-permute-done.4.__0_
  27.7 0.5 collective-permute-start.5
  28.2 0.1 collective-permute-start.10
  28.4 0.0 collective-permute-done.8.refs_4_
  28.4 0.0 collective-permute-done.7.refs_3_
  28.4 0.0 collective-permute-done.6.refs_2_
  28.4 6.4 %attend_1.1 = (f32[2048,128]{1,0:T(8,128)S(1)}, f32[2048,256]{1,0:T(8,128)S(1)}) custom-call(s32[11]{0:T(128)S(1)} %stack.68._.flag_ref, bf16[2048,256]{1,0:T(8,128)(2,1)S(1)} %get-tuple-element.14.q2_ref, bf16[2048,128]{1,0:T(8,128)(2,1)S(1)} %gate.5.refs_0_, ...), custom_call_target="tpu_custom_call", output_to_operand_aliasing={{0}: (7, {}), {1}: (8, {})} | custom-call | flops 4294967296 | bytes 1048576 | tf_op jit(solution)/shard_map/attend_1/pallas_call | solution.py:306
  34.8 3.3 %collective-permute-done.5.__0_ = bf16[2048,128]{1,0:T(8,128)(2,1)S(1)} collective-permute-done((bf16[2048,128]{1,0:T(8,128)(2,1)S(1)}, bf16[2048,128]{1,0:T(8,128)(2,1)S(1)}, u32[]{:S(2)}, u32[]{:S(2)}) %collective-permute-start.5) | collective-permute-done | bytes 524320 | tf_op jit(solution)/shard_map/ppermute | solution.py:248
  38.1 0.0 collective-permute-start.9
  38.1 0.0 collective-permute-start.12
  38.1 0.0 collective-permute-done.10.refs_0_
  38.1 4.0 %attend_2.1 = (f32[2048,128]{1,0:T(8,128)S(1)}, f32[2048,256]{1,0:T(8,128)S(1)}) custom-call(s32[11]{0:T(128)S(1)} %stack.68._.flag_ref, bf16[2048,256]{1,0:T(8,128)(2,1)S(1)} %get-tuple-element.14.q2_ref, bf16[2048,128]{1,0:T(8,128)(2,1)S(1)} %collective-permute-done.10.refs_0_, ...), custom_call_target="tpu_custom_call", output_to_operand_aliasing={{0}: (4, {}), {1}: (5, {})} | custom-call | flops 4294967296 | bytes 1048576 | tf_op jit(solution)/shard_map/attend_2/pallas_call | solution.py:306
  42.2 6.3 %collective-permute-done.9.__0_ = bf16[2048,128]{1,0:T(8,128)(2,1)S(1)} collective-permute-done((bf16[2048,128]{1,0:T(8,128)(2,1)S(1)}, bf16[2048,128]{1,0:T(8,128)(2,1)S(1)}, u32[]{:S(2)}, u32[]{:S(2)}) %collective-permute-start.9) | collective-permute-done | bytes 524320 | tf_op jit(solution)/shard_map/ppermute | solution.py:248
  48.5 0.0 collective-permute-start.11
  48.5 0.0 collective-permute-done.12.refs_0_
  48.5 0.0 copy-start.2
  48.5 4.3 %attend_3.1 = (f32[2048,128]{1,0:T(8,128)S(1)}, f32[2048,256]{1,0:T(8,128)S(1)}) custom-call(s32[11]{0:T(128)S(1)} %stack.68._.flag_ref, bf16[2048,256]{1,0:T(8,128)(2,1)S(1)} %get-tuple-element.14.q2_ref, bf16[2048,128]{1,0:T(8,128)(2,1)S(1)} %collective-permute-done.12.refs_0_, ...), custom_call_target="tpu_custom_call", output_to_operand_aliasing={{0}: (4, {}), {1}: (5, {})} | custom-call | flops 4294967296 | bytes 1048576 | tf_op jit(solution)/shard_map/attend_3/pallas_call | solution.py:306
  52.8 0.0 collective-permute-done.11.other_ref
  52.8 0.0 copy-done.2
  52.8 6.4 %attend_project.1 = bf16[8,272,512]{2,1,0:T(8,128)(2,1)S(1)} custom-call(s32[11]{0:T(128)S(1)} %stack.68._.flag_ref, bf16[2048,256]{1,0:T(8,128)(2,1)S(1)} %get-tuple-element.14.q2_ref, bf16[2048,128]{1,0:T(8,128)(2,1)S(1)} %collective-permute-done.11.other_ref, f32[2048,128]{1,0:T(8,128)S(1)} %get-tuple-element.22.m_in, ...), custom_call_target="tpu_custom_call" | custom-call | flops 4294967296 | bytes 1048576 | tf_op jit(solution)/shard_map/attend_project/pallas_call | solution.py:328
  59.2 33.2 %all_to_all.5.parts_ref = bf16[8,272,512]{2,1,0:T(8,128)(2,1)S(1)} all-to-all(bf16[8,272,512]{2,1,0:T(8,128)(2,1)S(1)} %attend_project.1), channel_id=1, replica_groups=mesh['seq'=32,'tp'=8] {'tp'}, dimensions={0} | all-to-all | bytes 4456448 | tf_op jit(solution)/shard_map/all_to_all | solution.py:346
  92.5 1.0 %sum_parts.1 = (bf16[32,4096]{1,0:T(8,128)(2,1)}, bf16[1,512]{1,0:T(2,128)(2,1)}) custom-call(bf16[8,272,512]{2,1,0:T(8,128)(2,1)S(1)} %all_to_all.5.parts_ref), custom_call_target="tpu_custom_call" | custom-call | tf_op jit(solution)/shard_map/sum_parts/pallas_call | solution.py:347
  (4 shorter events, 0.0 us)
Async XLA Ops:
  2.2 14.5 %copy-start = (bf16[512,128]{1,0:T(8,128)(2,1)S(1)}, bf16[512,128]{1,0:T(8,128)(2,1)}, u32[]{:S(2)}) copy-start(bf16[512,128]{1,0:T(8,128)(2,1)} %pack_own.1.own_ref) | copy-start | bytes 393220
  2.2 7.4 %collective-permute-start = (bf16[512,128]{1,0:T(8,128)(2,1)}, bf16[512,128]{1,0:T(8,128)(2,1)S(1)}, u32[]{:S(2)}, u32[]{:S(2)}) collective-permute-start(bf16[512,128]{1,0:T(8,128)(2,1)} %pack_own.1.own_ref), channel_id=1, source_target_pairs={{0,16},{8,24},{16,0},{24,8},{32,48},{40,56},{48,32},{56,40},{64,80... | collective-permute-start | bytes 393224 | tf_op jit(solution)/shard_map/ppermute | solution.py:248
  5.5 11.2 %collective-permute-start.3 = (bf16[512,128]{1,0:T(8,128)(2,1)}, bf16[512,128]{1,0:T(8,128)(2,1)S(1)}, u32[]{:S(2)}, u32[]{:S(2)}) collective-permute-start(bf16[512,128]{1,0:T(8,128)(2,1)} %pack_own.1.own_ref), channel_id=1, source_target_pairs={{0,128},{8,136},{16,144},{24,152},{32,160},{40,168},{48,176},{56,1... | collective-permute-start | bytes 393224 | tf_op jit(solution)/shard_map/ppermute | solution.py:248
  5.5 11.2 %collective-permute-start.2 = (bf16[512,128]{1,0:T(8,128)(2,1)}, bf16[512,128]{1,0:T(8,128)(2,1)S(1)}, u32[]{:S(2)}, u32[]{:S(2)}) collective-permute-start(bf16[512,128]{1,0:T(8,128)(2,1)} %pack_own.1.own_ref), channel_id=1, source_target_pairs={{0,8},{8,0},{16,24},{24,16},{32,40},{40,32},{48,56},{56,48},{64,72... | collective-permute-start | bytes 393224 | tf_op jit(solution)/shard_map/ppermute | solution.py:248
  6.1 16.6 %copy-start.3 = (bf16[256,1024]{1,0:T(8,128)(2,1)S(1)}, bf16[256,1024]{1,0:T(8,128)(2,1)}, u32[]{:S(2)}) copy-start(bf16[256,1024]{1,0:T(8,128)(2,1)} %q_ref.3) | copy-start | bytes 1572868
  9.6 0.7 copy-start.1
  10.3 6.4 %collective-permute-start.1 = (bf16[512,128]{1,0:T(8,128)(2,1)S(1)}, bf16[512,128]{1,0:T(8,128)(2,1)S(1)}, u32[]{:S(2)}, u32[]{:S(2)}) collective-permute-start(bf16[512,128]{1,0:T(8,128)(2,1)S(1)} %gate.4.y_ref), channel_id=1, source_target_pairs={{0,8},{8,0},{16,24},{24,16},{32,40},{40,32},{48,56},{56,48},{64,72... | collective-permute-start | bytes 393224 | tf_op jit(solution)/shard_map/ppermute | solution.py:248
  17.2 10.5 %collective-permute-start.4 = (bf16[2048,128]{1,0:T(8,128)(2,1)S(1)}, bf16[2048,128]{1,0:T(8,128)(2,1)S(1)}, u32[]{:S(2)}, u32[]{:S(2)}) collective-permute-start(bf16[2048,128]{1,0:T(8,128)(2,1)S(1)} %get-tuple-element.13.kv_ref), channel_id=1, source_target_pairs={{0,32},{8,232},{16,48},{24,248},{32,64},{40,8},{48,80},{56,24},{64... | collective-permute-start | bytes 1572872 | tf_op jit(solution)/shard_map/ppermute | solution.py:248
  19.1 9.3 %collective-permute-start.8 = (bf16[512,128]{1,0:T(8,128)(2,1)S(1)}, bf16[512,128]{1,0:T(8,128)(2,1)S(1)}, u32[]{:S(2)}, u32[]{:S(2)}) collective-permute-start(bf16[512,128]{1,0:T(8,128)(2,1)S(1)} %get-tuple-element.16.refs_1_), channel_id=1, source_target_pairs={{0,16},{8,24},{16,0},{24,8},{32,48},{40,56},{48,32},{56,40},{64,80... | collective-permute-start | bytes 393224 | tf_op jit(solution)/shard_map/ppermute | solution.py:248
  19.4 8.9 %collective-permute-start.7 = (bf16[512,128]{1,0:T(8,128)(2,1)S(1)}, bf16[512,128]{1,0:T(8,128)(2,1)S(1)}, u32[]{:S(2)}, u32[]{:S(2)}) collective-permute-start(bf16[512,128]{1,0:T(8,128)(2,1)S(1)} %get-tuple-element.16.refs_1_), channel_id=1, source_target_pairs={{0,24},{8,16},{16,8},{24,0},{32,56},{40,48},{48,40},{56,32},{64,88... | collective-permute-start | bytes 393224 | tf_op jit(solution)/shard_map/ppermute | solution.py:248
  20.0 8.4 %collective-permute-start.6 = (bf16[512,128]{1,0:T(8,128)(2,1)S(1)}, bf16[512,128]{1,0:T(8,128)(2,1)S(1)}, u32[]{:S(2)}, u32[]{:S(2)}) collective-permute-start(bf16[512,128]{1,0:T(8,128)(2,1)S(1)} %get-tuple-element.16.refs_1_), channel_id=1, source_target_pairs={{0,8},{8,0},{16,24},{24,16},{32,40},{40,32},{48,56},{56,48},{64,72... | collective-permute-start | bytes 393224 | tf_op jit(solution)/shard_map/ppermute | solution.py:248
  27.7 10.4 %collective-permute-start.5 = (bf16[2048,128]{1,0:T(8,128)(2,1)S(1)}, bf16[2048,128]{1,0:T(8,128)(2,1)S(1)}, u32[]{:S(2)}, u32[]{:S(2)}) collective-permute-start(bf16[2048,128]{1,0:T(8,128)(2,1)S(1)} %gate.5.refs_0_), channel_id=1, source_target_pairs={{0,32},{8,232},{16,48},{24,248},{32,64},{40,8},{48,80},{56,24},{64... | collective-permute-start | bytes 1572872 | tf_op jit(solution)/shard_map/ppermute | solution.py:248
  28.2 9.9 %collective-permute-start.10 = (bf16[2048,128]{1,0:T(8,128)(2,1)S(1)}, bf16[2048,128]{1,0:T(8,128)(2,1)S(1)}, u32[]{:S(2)}, u32[]{:S(2)}) collective-permute-start(bf16[2048,128]{1,0:T(8,128)(2,1)S(1)} %gate.5.refs_0_), channel_id=1, source_target_pairs={{0,8},{8,0},{16,24},{24,16},{32,40},{40,32},{48,56},{56,48},{64,72... | collective-permute-start | bytes 1572872 | tf_op jit(solution)/shard_map/ppermute | solution.py:248
  38.1 10.4 %collective-permute-start.9 = (bf16[2048,128]{1,0:T(8,128)(2,1)S(1)}, bf16[2048,128]{1,0:T(8,128)(2,1)S(1)}, u32[]{:S(2)}, u32[]{:S(2)}) collective-permute-start(bf16[2048,128]{1,0:T(8,128)(2,1)S(1)} %gate.6.refs_1_), channel_id=1, source_target_pairs={{0,32},{8,232},{16,48},{24,248},{32,64},{40,8},{48,80},{56,24},{64... | collective-permute-start | bytes 1572872 | tf_op jit(solution)/shard_map/ppermute | solution.py:248
  38.1 10.4 %collective-permute-start.12 = (bf16[2048,128]{1,0:T(8,128)(2,1)S(1)}, bf16[2048,128]{1,0:T(8,128)(2,1)S(1)}, u32[]{:S(2)}, u32[]{:S(2)}) collective-permute-start(bf16[2048,128]{1,0:T(8,128)(2,1)S(1)} %gate.6.refs_1_), channel_id=1, source_target_pairs={{0,8},{8,0},{16,24},{24,16},{32,40},{40,32},{48,56},{56,48},{64,72... | collective-permute-start | bytes 1572872 | tf_op jit(solution)/shard_map/ppermute | solution.py:248
  48.5 4.3 %collective-permute-start.11 = (bf16[2048,128]{1,0:T(8,128)(2,1)S(1)}, bf16[2048,128]{1,0:T(8,128)(2,1)S(1)}, u32[]{:S(2)}, u32[]{:S(2)}) collective-permute-start(bf16[2048,128]{1,0:T(8,128)(2,1)S(1)} %gate.7.refs_1_), channel_id=1, source_target_pairs={{0,8},{8,0},{16,24},{24,16},{32,40},{40,32},{48,56},{56,48},{64,72... | collective-permute-start | bytes 1572872 | tf_op jit(solution)/shard_map/ppermute | solution.py:248
  48.5 4.3 %copy-start.2 = (f32[8,128]{1,0:T(8,128)S(1)}, f32[8,128]{1,0:T(8,128)}, u32[]{:S(2)}) copy-start(f32[8,128]{1,0:T(8,128)} %decode.1.__1_.step_ref) | copy-start | bytes 12292
where the time goes:
time: 93.7 us; the launch traced here: 93.4 us
  blocking collectives  33.2 us (35%)
  Pallas kernels  32 us (34%)
  waiting for transfers between devices  16.1 us (17%)
  starting transfers between devices  9.9 us (11%)
  between operations  1.42 us (2%)
    all_to_all x1, blocking collectives, body(): swapped = lax.all_to_all(partial, 'tp', 0, 0)  33.2 us
    ppermute x13, waiting for transfers between devices, send(): return lax.ppermute(block, 'seq', pairs)  16.1 us
    pallas_call x3, Pallas kernels, step(): pl.pallas_call(functools.partial(step_kernel, rows=rows, heads=heads, at=...  14.7 us
    ppermute x13, starting transfers between devices, send(): return lax.ppermute(block, 'seq', pairs)  9.9 us
    pallas_call x1, Pallas kernels, body(): pl.pallas_call(functools.partial(last_kernel, rows=rows, heads=heads, n_t...  6.4 us
    pallas_call x1, Pallas kernels, body(): pl.pallas_call(functools.partial(local_kernel, rows=rows, heads=heads), i...  4.34 us
    pallas_call x1, Pallas kernels, body(): pl.pallas_call(functools.partial(decode_kernel, heads=heads), in_specs=[s...  3.44 us
  transfers between devices with their start and end apart: 13, of which 4 were waited for; matrix products, arithmetic and copies ran while one was open for 0% of the time, Pallas kernels for 24%

commit v1 on v0

--- a/solution.py
+++ b/solution.py
@@ -11,10 +11,12 @@
 HEAD = 128
 SCALE = HEAD ** -0.5 * math.log2(math.e)
 LOW = -1e30
+LANES = 128
 STEP_ROWS = 16
+LANES = 128
 STEP_ROWS = 16
 NT = (((1,), (1,)), ((), ()))
-EDGES, HALF, OWN, OTHER = 0, 4, 4, 7
+EDGES, HALF, OWN, OTHER, START = 0, 4, 4, 7, 11
 Z, YH, CORE = 8, 2, 2
 
 
@@ -35,13 +37,25 @@
 RING = seq_pairs(lambda z, yh, c: (z + 1 if c == 0 else z - 1, yh, c))
 
 
-def split_queries(q_ref, q2_ref, rows, heads):
-    for h in range(heads):
-        scaled = q_ref[:, h * HEAD:(h + 1) * HEAD].astype(jnp.float32) * SCALE
-        high = scaled.astype(jnp.bfloat16)
-        low = (scaled - high.astype(jnp.float32)).astype(jnp.bfloat16)
-        q2_ref[h * rows:(h + 1) * rows, :HEAD] = high
-        q2_ref[h * rows:(h + 1) * rows, HEAD:] = low
+X, YL = 4, 2
+OVER_Y = [(x * YL + y, x * YL + 1 - y) for x in range(X) for y in range(YL)]
+
+
+def over_x_pairs(dx):
+    return [(x * YL + y, (x + dx) % X * YL + y) for x in range(X) for y in range(YL)]
+
+
+def split_queries(flag_ref, q_ref, q2_ref, rows, heads, n_tp):
+    each = rows // n_tp
+    for i in range(n_tp):
+        start = pl.multiple_of(flag_ref[START + i], each)
+        for h in range(heads):
+            scaled = q_ref[pl.ds(start, each), h * HEAD:(h + 1) * HEAD].astype(jnp.float32) * SCALE
+            high = scaled.astype(jnp.bfloat16)
+            low = (scaled - high.astype(jnp.float32)).astype(jnp.bfloat16)
+            at = h * rows + i * each
+            q2_ref[at:at + each, :HEAD] = high
+            q2_ref[at:at + each, HEAD:] = low
 
 
 def spread(sources, k2_ref, v2_ref, at, rows):
@@ -83,10 +97,15 @@
     lax.fori_loop(0, heads // together, some_heads, 0)
 
 
-def local_kernel(flag_ref, q_ref, kv_ref, q2_ref, m_ref, acc_ref, k2_ref, v2_ref, *, rows, heads):
-    split_queries(q_ref, q2_ref, rows, heads)
+def local_kernel(flag_ref, q_ref, kv_ref, q2_ref, m_ref, acc_ref, k2_ref, v2_ref, *, rows, heads, n_tp):
+    split_queries(flag_ref, q_ref, q2_ref, rows, heads, n_tp)
     spread([kv_ref], k2_ref, v2_ref, 0, rows)
-    row = lax.broadcasted_iota(jnp.int32, (rows, rows), 0)
+    each = rows // n_tp
+    place = lax.broadcasted_iota(jnp.int32, (rows, rows), 0)
+    row = place
+    for i in range(n_tp):
+        inside = jnp.logical_and(place >= i * each, place < (i + 1) * each)
+        row = jnp.where(inside, place + (flag_ref[START + i] - i * each), row)
     col = lax.broadcasted_iota(jnp.int32, (rows, rows), 1)
     mask = jnp.concatenate([(row - col) >= flag_ref[EDGES + b] for b in range(4)], axis=1)
     attend(q2_ref, k2_ref, v2_ref, 4 * rows, None, None, m_ref, acc_ref, rows, heads, mask)
@@ -127,8 +146,8 @@
     attend_live(flag_ref, at, q2_ref, groups, k2_ref, v2_ref, m_in, acc_in, m_ref, acc_ref, rows, heads)
 
 
-def last_kernel(flag_ref, q2_ref, other_ref, m_in, acc_in, step_ref, w_hbm, out_ref, att_ref,
-                acc_ref, m_ref, k2_ref, v2_ref, w_ref, w_sem, *, rows, heads, n_tp):
+def last_kernel(flag_ref, q2_ref, other_ref, m_in, acc_in, step_ref, w_hbm, keep_ref, send_ref, g0_ref, g1_ref, g2_ref,
+                g3_ref, att_ref, acc_ref, m_ref, k2_ref, v2_ref, w_ref, token_ref, w_sem, *, rows, heads, n_tp):
     w_copy = pltpu.make_async_copy(w_hbm, w_ref, w_sem)
     w_copy.start()
     attend_live(flag_ref, (OTHER + 3,), q2_ref, [[other_ref]], k2_ref, v2_ref,
@@ -139,27 +158,54 @@
         att_ref[:rows, cols] = (acc[:, :HEAD] / acc[:, HEAD:]).astype(jnp.bfloat16)
         att_ref[rows:, cols] = jnp.broadcast_to(step_ref[h:h + 1, :], (STEP_ROWS, HEAD)).astype(jnp.bfloat16)
     w_copy.wait()
-    each, wide = rows // n_tp, w_ref.shape[1] // n_tp
+    each, wide, half = rows // n_tp, w_ref.shape[1] // n_tp, w_ref.shape[1] // 2
+    g_refs = (g0_ref, g1_ref, g2_ref, g3_ref)
     for g in range(n_tp):
         part = jnp.dot(att_ref[...], w_ref[:, g * wide:(g + 1) * wide], preferred_element_type=jnp.float32)
+        token_ref[:, g * wide:(g + 1) * wide] = part[rows:, :]
         part = part.astype(jnp.bfloat16)
-        for t in range(n_tp):
-            out_ref[t, g * each:(g + 1) * each, :] = part[t * each:(t + 1) * each, :]
-        out_ref[g, rows:, :] = part[rows:, :]
-
-
-def sum_kernel(parts_ref, out_ref, step_ref, *, n_tp):
-    each, wide = out_ref.shape[0], parts_ref.shape[2]
-    rows = parts_ref.shape[1] - STEP_ROWS
-    for g in range(n_tp):
-        total = parts_ref[0, g * each:(g + 1) * each, :].astype(jnp.float32)
-        for t in range(1, n_tp):
-            total = total + parts_ref[t, g * each:(g + 1) * each, :].astype(jnp.float32)
-        out_ref[:, g * wide:(g + 1) * wide] = total.astype(jnp.bfloat16)
-    total = parts_ref[0, rows:, :].astype(jnp.float32)
-    for t in range(1, n_tp):
-        total = total + parts_ref[t, rows:, :].astype(jnp.float32)
-    step_ref[...] = total[:1, :].astype(jnp.bfloat16)
+        if g * wide < half:
+            cols = slice(g * wide, (g + 1) * wide)
+            keep_ref[:, cols] = part[:rows // 2, :]
+            send_ref[:, cols] = part[rows // 2:rows, :]
+        else:
+            cols = slice(g * wide - half, (g + 1) * wide - half)
+            for dx, g_ref in enumerate(g_refs):
+                g_ref[:each, cols] = part[dx * each:(dx + 1) * each, :]
+                g_ref[each:2 * each, cols] = part[rows // 2 + dx * each:rows // 2 + (dx + 1) * each, :]
+    for g_ref in g_refs:
+        g_ref[:, half:] = jnp.zeros((2 * each, LANES), jnp.bfloat16)
+    for i in range(n_tp):
+        dy, dx = divmod(i, X)
+        start = pl.multiple_of(flag_ref[START + i] * (wide // each), wide)
+        for j in range(wide // LANES):
+            piece = token_ref[:1, pl.ds(start + j * LANES, LANES)].astype(jnp.bfloat16)
+            g_refs[dx][dy * each + j:dy * each + j + 1, half:] = piece
+
+
+def middle_kernel(keep_ref, recv_ref, g0_ref, g1_ref, g2_ref, g3_ref, f0_ref, f1_ref, f2_ref, f3_ref, mine_ref, give_ref):
+    each = f0_ref.shape[0]
+    for dx, f_ref in enumerate((f0_ref, f1_ref, f2_ref, f3_ref)):
+        part = slice(dx * each, (dx + 1) * each)
+        total = keep_ref[part, :].astype(jnp.float32) + recv_ref[part, :].astype(jnp.float32)
+        f_ref[...] = total.astype(f_ref.dtype)
+    for at, ref in ((0, mine_ref), (each, give_ref)):
+        total = g0_ref[at:at + each, :].astype(jnp.float32)
+        for g_ref in (g1_ref, g2_ref, g3_ref):
+            total = total + g_ref[at:at + each, :].astype(jnp.float32)
+        ref[...] = total.astype(ref.dtype)
+
+
+def sum_kernel(f0_ref, f1_ref, f2_ref, f3_ref, mine_ref, give_ref, out_ref, step_ref):
+    half = f0_ref.shape[1]
+    total = f0_ref[...]
+    for ref in (f1_ref, f2_ref, f3_ref):
+        total = total + ref[...].astype(jnp.float32)
+    out_ref[:, :half] = total.astype(jnp.bfloat16)
+    total = mine_ref[...] + give_ref[...].astype(jnp.float32)
+    out_ref[:, half:] = total[:, :half].astype(jnp.bfloat16)
+    for j in range(step_ref.shape[1] // LANES):
+        step_ref[:, j * LANES:(j + 1) * LANES] = total[j:j + 1, half:].astype(jnp.bfloat16)
 
 
 def decode_kernel(len_ref, q_ref, nk_ref, nv_ref, k_hbm, v_hbm, out_ref, k_ref, v_ref, k_sem, v_sem, *, heads):
@@ -250,7 +296,11 @@
     own_ring = [jnp.where(core == 0, z >= k, z + k >= Z) for k in range(1, 4)]
     other_ring = [jnp.where(core == 0, z + k >= Z, z >= k) for k in range(1, 4)]
     edges = [jnp.int32(0)] + [jnp.where(c == 1, -rows, rows) for c in (yh, core, yh)]
-    flags = jnp.stack([x.astype(jnp.int32) for x in edges + [z >= Z // 2] + own_ring + other_ring])
+    tp = lax.axis_index("tp")
+    starts = [
+        ((tp // YL + dx) % X * YL + (tp % YL + dy) % YL) * (rows // n_tp) for dy in range(YL) for dx in range(X)
+    ]
+    flags = jnp.stack([x.astype(jnp.int32) for x in edges + [z >= Z // 2] + own_ring + other_ring + starts])
 
     own = pl.pallas_call(
         pack_own_kernel,
@@ -290,7 +340,7 @@
         jax.ShapeDtypeStruct((heads * rows, 2 * HEAD), jnp.float32),
     )
     q2, m, acc = pl.pallas_call(
-        functools.partial(local_kernel, rows=rows, heads=heads),
+        functools.partial(local_kernel, rows=rows, heads=heads, n_tp=n_tp),
         in_specs=[smem, vmem, vmem],
         out_specs=[vmem] * 3,
         out_shape=(jax.ShapeDtypeStruct((heads * rows, 2 * HEAD), jnp.bfloat16),) + state,
@@ -325,11 +375,13 @@
     other_3 = send(ring_3, SWAP_CORE)
     m, acc = step("attend_3", (OTHER + 2, OWN + 3), [[other_2], [ring_3]], m, acc)
 
-    partial = pl.pallas_call(
+    each, half = rows // n_tp, width // 2
+    bf16 = functools.partial(jax.ShapeDtypeStruct, dtype=jnp.bfloat16)
+    keep, give_y, *over_x = pl.pallas_call(
         functools.partial(last_kernel, rows=rows, heads=heads, n_tp=n_tp),
         in_specs=[smem] + [vmem] * 5 + [anywhere],
-        out_specs=vmem,
-        out_shape=jax.ShapeDtypeStruct((n_tp, rows + STEP_ROWS, width // n_tp), jnp.bfloat16),
+        out_specs=[vmem] * 6,
+        out_shape=[bf16((rows // 2, half))] * 2 + [bf16((2 * each, half + LANES))] * X,
         scratch_shapes=[
             pltpu.VMEM((rows + STEP_ROWS, heads * HEAD), jnp.bfloat16),
             pltpu.VMEM(state[1].shape, jnp.float32),
@@ -337,24 +389,34 @@
             pltpu.VMEM((4 * rows, 2 * HEAD), jnp.bfloat16),
             pltpu.VMEM((4 * rows, 2 * HEAD), jnp.bfloat16),
             pltpu.VMEM(out_weight.shape, jnp.bfloat16),
+            pltpu.VMEM((STEP_ROWS, width), jnp.float32),
             pltpu.SemaphoreType.DMA,
         ],
         compiler_params=params(44),
         cost_estimate=cost(4 * rows, 2 * rows * heads * HEAD * width),
         name="attend_project",
     )(flags, q2, other_3, m, acc, step_attention, out_weight)
-    swapped = lax.all_to_all(partial, "tp", 0, 0)
+    from_y = lax.ppermute(give_y, "tp", OVER_Y)
+    from_x = [lax.ppermute(over_x[dx], "tp", over_x_pairs(dx)) for dx in (1, 2, 3)]
+    f0, *give_x, mine, give = pl.pallas_call(
+        middle_kernel,
+        in_specs=[vmem] * 6,
+        out_specs=[vmem] * 6,
+        out_shape=[jax.ShapeDtypeStruct((each, half), jnp.float32)] + [bf16((each, half))] * 3
+        + [jax.ShapeDtypeStruct((each, half + LANES), jnp.float32), bf16((each, half + LANES))],
+        compiler_params=params(24),
+        name="sum_first",
+    )(keep, from_y, over_x[0], *from_x)
+    given = lax.ppermute(give, "tp", OVER_Y)
+    given_x = [lax.ppermute(give_x[dx - 1], "tp", over_x_pairs(dx)) for dx in (1, 2, 3)]
     prefill_out, decode_out = pl.pallas_call(
-        functools.partial(sum_kernel, n_tp=n_tp),
-        in_specs=[vmem],
+        sum_kernel,
+        in_specs=[vmem] * 6,
         out_specs=[vmem] * 2,
-        out_shape=(
-            jax.ShapeDtypeStruct((rows // n_tp, width), jnp.bfloat16),
-            jax.ShapeDtypeStruct((1, width // n_tp), jnp.bfloat16),
-        ),
+        out_shape=[bf16((each, width)), bf16((1, width // n_tp))],
         compiler_params=params(24),
-        name="sum_parts",
-    )(swapped)
+        name="sum_last",
+    )(f0, *given_x, mine, given)
     return prefill_out, decode_out
 
 

time: 93.7 us -> 89.7 us (0.957)
  blocking collectives: 33.2 us -> 0 us
  waiting for transfers between devices: 16.1 us -> 32.1 us
  starting transfers between devices: 9.9 us -> 23.1 us
    all_to_all x1 -> x0, blocking collectives: 33.2 us -> none  [body(): swapped = lax.all_to_all(partial, 'tp', 0, 0)]
    ppermute x0 -> x8, waiting for transfers between devices: none -> 16 us  [the longest x3 11.6 us: body(): lax.ppermute(over_x[dx], 'tp', over_x_pairs(dx))]
    ppermute x0 -> x8, starting transfers between devices: none -> 13.1 us  [the longest x3 5.65 us: body(): lax.ppermute(over_x[dx], 'tp', over_x_pairs(dx))]
    pallas_call x2 -> x3, Pallas kernels: 5.31 us -> 5.37 us  [the longest x1 4.33 us: body(): pl.pallas_call(functools.partial(local_kernel, rows=rows, heads=heads, n_...]
  transfers between devices with their start and end apart: 13 -> 21, of which waited for: 4 -> 9; matrix products, arithmetic and copies ran while one was open for 0% -> 0% of each run, Pallas kernels for 24% -> 25%
where the time goes in v1:
time: 89.7 us; the launch traced here: 89.4 us
  Pallas kernels  32.1 us (36%)
  waiting for transfers between devices  32.1 us (36%)
  starting transfers between devices  23.1 us (26%)
  between operations  1.44 us (2%)
    ppermute x13, waiting for transfers between devices, send(): return lax.ppermute(block, 'seq', pairs)  16.1 us
    pallas_call x3, Pallas kernels, step(): pl.pallas_call(functools.partial(step_kernel, rows=rows, heads=heads, at=...  14.7 us
    ppermute x3, waiting for transfers between devices, body(): lax.ppermute(over_x[dx], 'tp', over_x_pairs(dx))  11.6 us
    ppermute x13, starting transfers between devices, send(): return lax.ppermute(block, 'seq', pairs)  9.9 us
    pallas_call x1, Pallas kernels, body(): pl.pallas_call(functools.partial(last_kernel, rows=rows, heads=heads, n_t...  6.43 us
    ppermute x3, starting transfers between devices, body(): lax.ppermute(over_x[dx], 'tp', over_x_pairs(dx))  5.65 us
    ppermute x3, starting transfers between devices, body(): lax.ppermute(give_x[dx - 1], 'tp', over_x_pairs(dx))  5.29 us
    ppermute x3, waiting for transfers between devices, body(): lax.ppermute(give_x[dx - 1], 'tp', over_x_pairs(dx))  4.41 us
  transfers between devices with their start and end apart: 21, of which 9 were waited for; matrix products, arithmetic and copies ran while one was open for 0% of the time, Pallas kernels for 25%

profile of v1, /device:TPU:128, one launch (start us, length us, event | category | flops | bytes accessed | tf_op | source)
XLA Modules:
  0.0 89.4 jit_solution(11133352302876431613)
XLA Ops:
  0.6 1.5 %pack_own.1.own_ref = bf16[512,128]{1,0:T(8,128)(2,1)} custom-call(bf16[256,128]{1,0:T(8,128)(2,1)} %k_hbm.2, bf16[256,128]{1,0:T(8,128)(2,1)} %v_hbm.2), custom_call_target="tpu_custom_call" | custom-call | tf_op jit(solution)/shard_map/pack_own/pallas_call | solution.py:305
  2.2 3.3 %collective-permute-start = (bf16[512,128]{1,0:T(8,128)(2,1)}, bf16[512,128]{1,0:T(8,128)(2,1)S(1)}, u32[]{:S(2)}, u32[]{:S(2)}) collective-permute-start(bf16[512,128]{1,0:T(8,128)(2,1)} %pack_own.1.own_ref), channel_id=1, source_target_pairs={{0,16},{8,24},{16,0},{24,8},{32,48},{40,56},{48,32},{56,40},{64,80... | collective-permute-start | bytes 393224 | tf_op jit(solution)/shard_map/ppermute | solution.py:294
  5.5 0.0 collective-permute-start.3
  5.5 0.0 collective-permute-start.2
  6.1 0.0 copy-start.3
  6.1 3.4 %decode.1.__1_.step_ref = f32[8,128]{1,0:T(8,128)} custom-call(s32[1]{0:T(128)S(6)} %copy.32.len_ref, bf16[1,1024]{1,0:T(2,128)(2,1)} %q_ref.2, bf16[1,128]{1,0:T(2,128)(2,1)} %nk_ref.1, bf16[1,128]{1,0:T(2,128)(2,1)} %nv_ref.1, bf16[1,4096,128]{2,1,0:T(8,128)(2,1)} %k_hbm.3, bf16[1,4096,128]{2,1,0:T(8,128)(2,1)} %v_hbm.3), custom_call_target="tpu_custom_call" | custom-call | flops 1000000000 | bytes 2097152 | tf_op jit(solution)/shard_map/decode/pallas_call | solution.py:315
  9.6 0.0 collective-permute-done.__0_
  9.6 0.7 copy-done.1
  10.3 0.5 collective-permute-start.1
  10.8 0.1 stack.100._.flag_ref
  10.9 5.7 %collective-permute-done.3.far_ref = bf16[512,128]{1,0:T(8,128)(2,1)S(1)} collective-permute-done((bf16[512,128]{1,0:T(8,128)(2,1)}, bf16[512,128]{1,0:T(8,128)(2,1)S(1)}, u32[]{:S(2)}, u32[]{:S(2)}) %collective-permute-start.3) | collective-permute-done | bytes 131104 | tf_op jit(solution)/shard_map/ppermute | solution.py:294
  16.6 0.0 collective-permute-done.1.both_ref
  16.6 0.6 pack_here.1
  17.2 1.8 %collective-permute-start.4 = (bf16[2048,128]{1,0:T(8,128)(2,1)S(1)}, bf16[2048,128]{1,0:T(8,128)(2,1)S(1)}, u32[]{:S(2)}, u32[]{:S(2)}) collective-permute-start(bf16[2048,128]{1,0:T(8,128)(2,1)S(1)} %get-tuple-element.25.kv_ref), channel_id=1, source_target_pairs={{0,32},{8,232},{16,48},{24,248},{32,64},{40,8},{48,80},{56,24},{64... | collective-permute-start | bytes 1572872 | tf_op jit(solution)/shard_map/ppermute | solution.py:294
  19.0 0.4 collective-permute-start.8
  19.4 0.6 collective-permute-start.7
  20.0 2.7 %collective-permute-start.6 = (bf16[512,128]{1,0:T(8,128)(2,1)S(1)}, bf16[512,128]{1,0:T(8,128)(2,1)S(1)}, u32[]{:S(2)}, u32[]{:S(2)}) collective-permute-start(bf16[512,128]{1,0:T(8,128)(2,1)S(1)} %get-tuple-element.28.refs_1_), channel_id=1, source_target_pairs={{0,8},{8,0},{16,24},{24,16},{32,40},{40,32},{48,56},{56,48},{64,72... | collective-permute-start | bytes 393224 | tf_op jit(solution)/shard_map/ppermute | solution.py:294
  22.7 4.3 %attend_local.1 = (bf16[2048,256]{1,0:T(8,128)(2,1)S(1)}, f32[2048,128]{1,0:T(8,128)S(1)}, f32[2048,256]{1,0:T(8,128)S(1)}) custom-call(s32[19]{0:T(128)S(1)} %stack.100._.flag_ref, bf16[256,1024]{1,0:T(8,128)(2,1)S(1)} %copy-done.3, bf16[2048,128]{1,0:T(8,128)(2,1)S(1)} %get-tuple-element.25.kv_ref), custom_call_target="tpu_custom_call" | custom-call | flops 2147483648 | bytes 1048576 | tf_op jit(solution)/shard_map/attend_local/pallas_call | solution.py:342
  27.0 0.7 collective-permute-done.4.__0_
  27.7 0.5 collective-permute-start.5
  28.2 0.1 collective-permute-start.10
  28.4 6.4 %attend_1.1 = (f32[2048,128]{1,0:T(8,128)S(1)}, f32[2048,256]{1,0:T(8,128)S(1)}) custom-call(s32[19]{0:T(128)S(1)} %stack.100._.flag_ref, bf16[2048,256]{1,0:T(8,128)(2,1)S(1)} %get-tuple-element.26.q2_ref, bf16[2048,128]{1,0:T(8,128)(2,1)S(1)} %gate.5.refs_0_, ...), custom_call_target="tpu_custom_call", output_to_operand_aliasing={{0}: (7, {}), {1}: (8, {})} | custom-call | flops 4294967296 | bytes 1048576 | tf_op jit(solution)/shard_map/attend_1/pallas_call | solution.py:356
  34.8 3.3 %collective-permute-done.5.__0_ = bf16[2048,128]{1,0:T(8,128)(2,1)S(1)} collective-permute-done((bf16[2048,128]{1,0:T(8,128)(2,1)S(1)}, bf16[2048,128]{1,0:T(8,128)(2,1)S(1)}, u32[]{:S(2)}, u32[]{:S(2)}) %collective-permute-start.5) | collective-permute-done | bytes 524320 | tf_op jit(solution)/shard_map/ppermute | solution.py:294
  38.1 0.0 collective-permute-start.9
  38.1 0.0 collective-permute-start.12
  38.1 0.0 collective-permute-done.10.refs_0_
  38.1 4.0 %attend_2.1 = (f32[2048,128]{1,0:T(8,128)S(1)}, f32[2048,256]{1,0:T(8,128)S(1)}) custom-call(s32[19]{0:T(128)S(1)} %stack.100._.flag_ref, bf16[2048,256]{1,0:T(8,128)(2,1)S(1)} %get-tuple-element.26.q2_ref, bf16[2048,128]{1,0:T(8,128)(2,1)S(1)} %collective-permute-done.10.refs_0_, ...), custom_call_target="tpu_custom_call", output_to_operand_aliasing={{0}: (4, {}), {1}: (5, {})} | custom-call | flops 4294967296 | bytes 1048576 | tf_op jit(solution)/shard_map/attend_2/pallas_call | solution.py:356
  42.2 6.3 %collective-permute-done.9.__0_ = bf16[2048,128]{1,0:T(8,128)(2,1)S(1)} collective-permute-done((bf16[2048,128]{1,0:T(8,128)(2,1)S(1)}, bf16[2048,128]{1,0:T(8,128)(2,1)S(1)}, u32[]{:S(2)}, u32[]{:S(2)}) %collective-permute-start.9) | collective-permute-done | bytes 524320 | tf_op jit(solution)/shard_map/ppermute | solution.py:294
  48.5 0.0 collective-permute-start.11
  48.5 0.0 collective-permute-done.12.refs_0_
  48.5 4.3 %attend_3.1 = (f32[2048,128]{1,0:T(8,128)S(1)}, f32[2048,256]{1,0:T(8,128)S(1)}) custom-call(s32[19]{0:T(128)S(1)} %stack.100._.flag_ref, bf16[2048,256]{1,0:T(8,128)(2,1)S(1)} %get-tuple-element.26.q2_ref, bf16[2048,128]{1,0:T(8,128)(2,1)S(1)} %collective-permute-done.12.refs_0_, ...), custom_call_target="tpu_custom_call", output_to_operand_aliasing={{0}: (4, {}), {1}: (5, {})} | custom-call | flops 4294967296 | bytes 1048576 | tf_op jit(solution)/shard_map/attend_3/pallas_call | solution.py:356
  52.8 6.4 %attend_project.1 = (bf16[128,2048]{1,0:T(8,128)(2,1)S(1)}, bf16[128,2048]{1,0:T(8,128)(2,1)S(1)}, bf16[64,2176]{1,0:T(8,128)(2,1)S(1)}, bf16[64,2176]{1,0:T(8,1...) custom-call(s32[19]{0:T(128)S(1)} %stack.100._.flag_ref, ...), custom_call_target="tpu_custom_call" | custom-call | flops 4294967296 | bytes 1048576 | tf_op jit(solution)/shard_map/attend_project/pallas_call | solution.py:380
  59.2 0.8 collective-permute-start.13
  60.0 1.5 %collective-permute-start.14 = (bf16[64,2176]{1,0:T(8,128)(2,1)S(1)}, bf16[64,2176]{1,0:T(8,128)(2,1)S(1)}, u32[]{:S(2)}, u32[]{:S(2)}) collective-permute-start(bf16[64,2176]{1,0:T(8,128)(2,1)S(1)} %get-tuple-element.39), channel_id=1, source_target_pairs={{0,2},{1,3},{2,4},{3,5},{4,6},{5,7},{6,0},{7,1},{8,10},{9,11},{10,... | collective-permute-start | bytes 835592 | tf_op jit(solution)/shard_map/ppermute | solution.py:400
  61.5 2.7 %collective-permute-start.15 = (bf16[64,2176]{1,0:T(8,128)(2,1)S(1)}, bf16[64,2176]{1,0:T(8,128)(2,1)S(1)}, u32[]{:S(2)}, u32[]{:S(2)}) collective-permute-start(bf16[64,2176]{1,0:T(8,128)(2,1)S(1)} %get-tuple-element.40), channel_id=1, source_target_pairs={{0,4},{1,5},{2,6},{3,7},{4,0},{5,1},{6,2},{7,3},{8,12},{9,13},{10,... | collective-permute-start | bytes 835592 | tf_op jit(solution)/shard_map/ppermute | solution.py:400
  64.2 1.4 %collective-permute-start.16 = (bf16[64,2176]{1,0:T(8,128)(2,1)S(1)}, bf16[64,2176]{1,0:T(8,128)(2,1)S(1)}, u32[]{:S(2)}, u32[]{:S(2)}) collective-permute-start(bf16[64,2176]{1,0:T(8,128)(2,1)S(1)} %get-tuple-element.41), channel_id=1, source_target_pairs={{0,6},{1,7},{2,0},{3,1},{4,2},{5,3},{6,4},{7,5},{8,14},{9,15},{10,... | collective-permute-start | bytes 835592 | tf_op jit(solution)/shard_map/ppermute | solution.py:400
  65.6 4.6 %collective-permute-done.14.g1_ref = bf16[64,2176]{1,0:T(8,128)(2,1)S(1)} collective-permute-done((bf16[64,2176]{1,0:T(8,128)(2,1)S(1)}, bf16[64,2176]{1,0:T(8,128)(2,1)S(1)}, u32[]{:S(2)}, u32[]{:S(2)}) %collective-permute-start.14) | collective-permute-done | bytes 278560 | tf_op jit(solution)/shard_map/ppermute | solution.py:400
  70.3 6.9 %collective-permute-done.15.g2_ref = bf16[64,2176]{1,0:T(8,128)(2,1)S(1)} collective-permute-done((bf16[64,2176]{1,0:T(8,128)(2,1)S(1)}, bf16[64,2176]{1,0:T(8,128)(2,1)S(1)}, u32[]{:S(2)}, u32[]{:S(2)}) %collective-permute-start.15) | collective-permute-done | bytes 278560 | tf_op jit(solution)/shard_map/ppermute | solution.py:400
  77.3 0.2 sum_first.1
  77.5 1.4 %collective-permute-start.20 = (bf16[32,2176]{1,0:T(8,128)(2,1)S(1)}, bf16[32,2176]{1,0:T(8,128)(2,1)S(1)}, u32[]{:S(2)}, u32[]{:S(2)}) collective-permute-start(bf16[32,2176]{1,0:T(8,128)(2,1)S(1)} %get-tuple-element.47), channel_id=1, source_target_pairs={{0,1},{1,0},{2,3},{3,2},{4,5},{5,4},{6,7},{7,6},{8,9},{9,8},{10,11... | collective-permute-start | bytes 417800 | tf_op jit(solution)/shard_map/ppermute | solution.py:410
  78.9 1.3 %collective-permute-start.17 = (bf16[32,2048]{1,0:T(8,128)(2,1)S(1)}, bf16[32,2048]{1,0:T(8,128)(2,1)S(1)}, u32[]{:S(2)}, u32[]{:S(2)}) collective-permute-start(bf16[32,2048]{1,0:T(8,128)(2,1)S(1)} %get-tuple-element.43), channel_id=1, source_target_pairs={{0,2},{1,3},{2,4},{3,5},{4,6},{5,7},{6,0},{7,1},{8,10},{9,11},{10,... | collective-permute-start | bytes 393224 | tf_op jit(solution)/shard_map/ppermute | solution.py:411
  80.3 2.4 %collective-permute-start.18 = (bf16[32,2048]{1,0:T(8,128)(2,1)S(1)}, bf16[32,2048]{1,0:T(8,128)(2,1)S(1)}, u32[]{:S(2)}, u32[]{:S(2)}) collective-permute-start(bf16[32,2048]{1,0:T(8,128)(2,1)S(1)} %get-tuple-element.44), channel_id=1, source_target_pairs={{0,4},{1,5},{2,6},{3,7},{4,0},{5,1},{6,2},{7,3},{8,12},{9,13},{10,... | collective-permute-start | bytes 393224 | tf_op jit(solution)/shard_map/ppermute | solution.py:411
  82.7 1.6 %collective-permute-start.19 = (bf16[32,2048]{1,0:T(8,128)(2,1)S(1)}, bf16[32,2048]{1,0:T(8,128)(2,1)S(1)}, u32[]{:S(2)}, u32[]{:S(2)}) collective-permute-start(bf16[32,2048]{1,0:T(8,128)(2,1)S(1)} %get-tuple-element.45), channel_id=1, source_target_pairs={{0,6},{1,7},{2,0},{3,1},{4,2},{5,3},{6,4},{7,5},{8,14},{9,15},{10,... | collective-permute-start | bytes 393224 | tf_op jit(solution)/shard_map/ppermute | solution.py:411
  84.2 1.5 %collective-permute-done.17.f1_ref = bf16[32,2048]{1,0:T(8,128)(2,1)S(1)} collective-permute-done((bf16[32,2048]{1,0:T(8,128)(2,1)S(1)}, bf16[32,2048]{1,0:T(8,128)(2,1)S(1)}, u32[]{:S(2)}, u32[]{:S(2)}) %collective-permute-start.17) | collective-permute-done | bytes 131104 | tf_op jit(solution)/shard_map/ppermute | solution.py:411
  85.7 2.9 %collective-permute-done.18.f2_ref = bf16[32,2048]{1,0:T(8,128)(2,1)S(1)} collective-permute-done((bf16[32,2048]{1,0:T(8,128)(2,1)S(1)}, bf16[32,2048]{1,0:T(8,128)(2,1)S(1)}, u32[]{:S(2)}, u32[]{:S(2)}) %collective-permute-start.18) | collective-permute-done | bytes 131104 | tf_op jit(solution)/shard_map/ppermute | solution.py:411
  88.6 0.1 collective-permute-done.19.f3_ref
  88.7 0.0 collective-permute-done.20.give_ref
  88.7 0.8 sum_last.1
  (17 shorter events, 0.0 us)
Async XLA Ops:
  2.2 7.4 %collective-permute-start = (bf16[512,128]{1,0:T(8,128)(2,1)}, bf16[512,128]{1,0:T(8,128)(2,1)S(1)}, u32[]{:S(2)}, u32[]{:S(2)}) collective-permute-start(bf16[512,128]{1,0:T(8,128)(2,1)} %pack_own.1.own_ref), channel_id=1, source_target_pairs={{0,16},{8,24},{16,0},{24,8},{32,48},{40,56},{48,32},{56,40},{64,80... | collective-permute-start | bytes 393224 | tf_op jit(solution)/shard_map/ppermute | solution.py:294
  5.5 11.2 %collective-permute-start.3 = (bf16[512,128]{1,0:T(8,128)(2,1)}, bf16[512,128]{1,0:T(8,128)(2,1)S(1)}, u32[]{:S(2)}, u32[]{:S(2)}) collective-permute-start(bf16[512,128]{1,0:T(8,128)(2,1)} %pack_own.1.own_ref), channel_id=1, source_target_pairs={{0,128},{8,136},{16,144},{24,152},{32,160},{40,168},{48,176},{56,1... | collective-permute-start | bytes 393224 | tf_op jit(solution)/shard_map/ppermute | solution.py:294
  5.5 11.2 %collective-permute-start.2 = (bf16[512,128]{1,0:T(8,128)(2,1)}, bf16[512,128]{1,0:T(8,128)(2,1)S(1)}, u32[]{:S(2)}, u32[]{:S(2)}) collective-permute-start(bf16[512,128]{1,0:T(8,128)(2,1)} %pack_own.1.own_ref), channel_id=1, source_target_pairs={{0,8},{8,0},{16,24},{24,16},{32,40},{40,32},{48,56},{56,48},{64,72... | collective-permute-start | bytes 393224 | tf_op jit(solution)/shard_map/ppermute | solution.py:294
  6.1 10.5 %copy-start = (bf16[512,128]{1,0:T(8,128)(2,1)S(1)}, bf16[512,128]{1,0:T(8,128)(2,1)}, u32[]{:S(2)}) copy-start(bf16[512,128]{1,0:T(8,128)(2,1)} %pack_own.1.own_ref) | copy-start | bytes 393220
  6.1 16.6 %copy-start.3 = (bf16[256,1024]{1,0:T(8,128)(2,1)S(1)}, bf16[256,1024]{1,0:T(8,128)(2,1)}, u32[]{:S(2)}) copy-start(bf16[256,1024]{1,0:T(8,128)(2,1)} %q_ref.3) | copy-start | bytes 1572868
  9.6 0.7 copy-start.1
  10.3 6.3 %collective-permute-start.1 = (bf16[512,128]{1,0:T(8,128)(2,1)S(1)}, bf16[512,128]{1,0:T(8,128)(2,1)S(1)}, u32[]{:S(2)}, u32[]{:S(2)}) collective-permute-start(bf16[512,128]{1,0:T(8,128)(2,1)S(1)} %gate.4.y_ref), channel_id=1, source_target_pairs={{0,8},{8,0},{16,24},{24,16},{32,40},{40,32},{48,56},{56,48},{64,72... | collective-permute-start | bytes 393224 | tf_op jit(solution)/shard_map/ppermute | solution.py:294
  17.2 10.5 %collective-permute-start.4 = (bf16[2048,128]{1,0:T(8,128)(2,1)S(1)}, bf16[2048,128]{1,0:T(8,128)(2,1)S(1)}, u32[]{:S(2)}, u32[]{:S(2)}) collective-permute-start(bf16[2048,128]{1,0:T(8,128)(2,1)S(1)} %get-tuple-element.25.kv_ref), channel_id=1, source_target_pairs={{0,32},{8,232},{16,48},{24,248},{32,64},{40,8},{48,80},{56,24},{64... | collective-permute-start | bytes 1572872 | tf_op jit(solution)/shard_map/ppermute | solution.py:294
  19.0 9.3 %collective-permute-start.8 = (bf16[512,128]{1,0:T(8,128)(2,1)S(1)}, bf16[512,128]{1,0:T(8,128)(2,1)S(1)}, u32[]{:S(2)}, u32[]{:S(2)}) collective-permute-start(bf16[512,128]{1,0:T(8,128)(2,1)S(1)} %get-tuple-element.28.refs_1_), channel_id=1, source_target_pairs={{0,16},{8,24},{16,0},{24,8},{32,48},{40,56},{48,32},{56,40},{64,80... | collective-permute-start | bytes 393224 | tf_op jit(solution)/shard_map/ppermute | solution.py:294
  19.4 8.9 %collective-permute-start.7 = (bf16[512,128]{1,0:T(8,128)(2,1)S(1)}, bf16[512,128]{1,0:T(8,128)(2,1)S(1)}, u32[]{:S(2)}, u32[]{:S(2)}) collective-permute-start(bf16[512,128]{1,0:T(8,128)(2,1)S(1)} %get-tuple-element.28.refs_1_), channel_id=1, source_target_pairs={{0,24},{8,16},{16,8},{24,0},{32,56},{40,48},{48,40},{56,32},{64,88... | collective-permute-start | bytes 393224 | tf_op jit(solution)/shard_map/ppermute | solution.py:294
  20.0 8.4 %collective-permute-start.6 = (bf16[512,128]{1,0:T(8,128)(2,1)S(1)}, bf16[512,128]{1,0:T(8,128)(2,1)S(1)}, u32[]{:S(2)}, u32[]{:S(2)}) collective-permute-start(bf16[512,128]{1,0:T(8,128)(2,1)S(1)} %get-tuple-element.28.refs_1_), channel_id=1, source_target_pairs={{0,8},{8,0},{16,24},{24,16},{32,40},{40,32},{48,56},{56,48},{64,72... | collective-permute-start | bytes 393224 | tf_op jit(solution)/shard_map/ppermute | solution.py:294
  27.7 10.4 %collective-permute-start.5 = (bf16[2048,128]{1,0:T(8,128)(2,1)S(1)}, bf16[2048,128]{1,0:T(8,128)(2,1)S(1)}, u32[]{:S(2)}, u32[]{:S(2)}) collective-permute-start(bf16[2048,128]{1,0:T(8,128)(2,1)S(1)} %gate.5.refs_0_), channel_id=1, source_target_pairs={{0,32},{8,232},{16,48},{24,248},{32,64},{40,8},{48,80},{56,24},{64... | collective-permute-start | bytes 1572872 | tf_op jit(solution)/shard_map/ppermute | solution.py:294
  28.2 9.9 %collective-permute-start.10 = (bf16[2048,128]{1,0:T(8,128)(2,1)S(1)}, bf16[2048,128]{1,0:T(8,128)(2,1)S(1)}, u32[]{:S(2)}, u32[]{:S(2)}) collective-permute-start(bf16[2048,128]{1,0:T(8,128)(2,1)S(1)} %gate.5.refs_0_), channel_id=1, source_target_pairs={{0,8},{8,0},{16,24},{24,16},{32,40},{40,32},{48,56},{56,48},{64,72... | collective-permute-start | bytes 1572872 | tf_op jit(solution)/shard_map/ppermute | solution.py:294
  38.1 10.4 %collective-permute-start.9 = (bf16[2048,128]{1,0:T(8,128)(2,1)S(1)}, bf16[2048,128]{1,0:T(8,128)(2,1)S(1)}, u32[]{:S(2)}, u32[]{:S(2)}) collective-permute-start(bf16[2048,128]{1,0:T(8,128)(2,1)S(1)} %gate.6.refs_1_), channel_id=1, source_target_pairs={{0,32},{8,232},{16,48},{24,248},{32,64},{40,8},{48,80},{56,24},{64... | collective-permute-start | bytes 1572872 | tf_op jit(solution)/shard_map/ppermute | solution.py:294
  38.1 10.4 %collective-permute-start.12 = (bf16[2048,128]{1,0:T(8,128)(2,1)S(1)}, bf16[2048,128]{1,0:T(8,128)(2,1)S(1)}, u32[]{:S(2)}, u32[]{:S(2)}) collective-permute-start(bf16[2048,128]{1,0:T(8,128)(2,1)S(1)} %gate.6.refs_1_), channel_id=1, source_target_pairs={{0,8},{8,0},{16,24},{24,16},{32,40},{40,32},{48,56},{56,48},{64,72... | collective-permute-start | bytes 1572872 | tf_op jit(solution)/shard_map/ppermute | solution.py:294
  48.5 4.3 %collective-permute-start.11 = (bf16[2048,128]{1,0:T(8,128)(2,1)S(1)}, bf16[2048,128]{1,0:T(8,128)(2,1)S(1)}, u32[]{:S(2)}, u32[]{:S(2)}) collective-permute-start(bf16[2048,128]{1,0:T(8,128)(2,1)S(1)} %gate.7.refs_1_), channel_id=1, source_target_pairs={{0,8},{8,0},{16,24},{24,16},{32,40},{40,32},{48,56},{56,48},{64,72... | collective-permute-start | bytes 1572872 | tf_op jit(solution)/shard_map/ppermute | solution.py:294
  48.5 4.3 %copy-start.2 = (f32[8,128]{1,0:T(8,128)S(1)}, f32[8,128]{1,0:T(8,128)}, u32[]{:S(2)}) copy-start(f32[8,128]{1,0:T(8,128)} %decode.1.__1_.step_ref) | copy-start | bytes 12292
  59.2 18.0 %collective-permute-start.13 = (bf16[128,2048]{1,0:T(8,128)(2,1)S(1)}, bf16[128,2048]{1,0:T(8,128)(2,1)S(1)}, u32[]{:S(2)}, u32[]{:S(2)}) collective-permute-start(bf16[128,2048]{1,0:T(8,128)(2,1)S(1)} %get-tuple-element.37), channel_id=1, source_target_pairs={{0,1},{1,0},{2,3},{3,2},{4,5},{5,4},{6,7},{7,6},{8,9},{9,8},{10,11... | collective-permute-start | bytes 1572872 | tf_op jit(solution)/shard_map/ppermute | solution.py:399
  60.0 10.3 %collective-permute-start.14 = (bf16[64,2176]{1,0:T(8,128)(2,1)S(1)}, bf16[64,2176]{1,0:T(8,128)(2,1)S(1)}, u32[]{:S(2)}, u32[]{:S(2)}) collective-permute-start(bf16[64,2176]{1,0:T(8,128)(2,1)S(1)} %get-tuple-element.39), channel_id=1, source_target_pairs={{0,2},{1,3},{2,4},{3,5},{4,6},{5,7},{6,0},{7,1},{8,10},{9,11},{10,... | collective-permute-start | bytes 835592 | tf_op jit(solution)/shard_map/ppermute | solution.py:400
  61.5 15.8 %collective-permute-start.15 = (bf16[64,2176]{1,0:T(8,128)(2,1)S(1)}, bf16[64,2176]{1,0:T(8,128)(2,1)S(1)}, u32[]{:S(2)}, u32[]{:S(2)}) collective-permute-start(bf16[64,2176]{1,0:T(8,128)(2,1)S(1)} %get-tuple-element.40), channel_id=1, source_target_pairs={{0,4},{1,5},{2,6},{3,7},{4,0},{5,1},{6,2},{7,3},{8,12},{9,13},{10,... | collective-permute-start | bytes 835592 | tf_op jit(solution)/shard_map/ppermute | solution.py:400
  64.2 13.0 %collective-permute-start.16 = (bf16[64,2176]{1,0:T(8,128)(2,1)S(1)}, bf16[64,2176]{1,0:T(8,128)(2,1)S(1)}, u32[]{:S(2)}, u32[]{:S(2)}) collective-permute-start(bf16[64,2176]{1,0:T(8,128)(2,1)S(1)} %get-tuple-element.41), channel_id=1, source_target_pairs={{0,6},{1,7},{2,0},{3,1},{4,2},{5,3},{6,4},{7,5},{8,14},{9,15},{10,... | collective-permute-start | bytes 835592 | tf_op jit(solution)/shard_map/ppermute | solution.py:400
  77.5 11.1 %collective-permute-start.20 = (bf16[32,2176]{1,0:T(8,128)(2,1)S(1)}, bf16[32,2176]{1,0:T(8,128)(2,1)S(1)}, u32[]{:S(2)}, u32[]{:S(2)}) collective-permute-start(bf16[32,2176]{1,0:T(8,128)(2,1)S(1)} %get-tuple-element.47), channel_id=1, source_target_pairs={{0,1},{1,0},{2,3},{3,2},{4,5},{5,4},{6,7},{7,6},{8,9},{9,8},{10,11... | collective-permute-start | bytes 417800 | tf_op jit(solution)/shard_map/ppermute | solution.py:410
  78.9 6.8 %collective-permute-start.17 = (bf16[32,2048]{1,0:T(8,128)(2,1)S(1)}, bf16[32,2048]{1,0:T(8,128)(2,1)S(1)}, u32[]{:S(2)}, u32[]{:S(2)}) collective-permute-start(bf16[32,2048]{1,0:T(8,128)(2,1)S(1)} %get-tuple-element.43), channel_id=1, source_target_pairs={{0,2},{1,3},{2,4},{3,5},{4,6},{5,7},{6,0},{7,1},{8,10},{9,11},{10,... | collective-permute-start | bytes 393224 | tf_op jit(solution)/shard_map/ppermute | solution.py:411
  80.3 8.3 %collective-permute-start.18 = (bf16[32,2048]{1,0:T(8,128)(2,1)S(1)}, bf16[32,2048]{1,0:T(8,128)(2,1)S(1)}, u32[]{:S(2)}, u32[]{:S(2)}) collective-permute-start(bf16[32,2048]{1,0:T(8,128)(2,1)S(1)} %get-tuple-element.44), channel_id=1, source_target_pairs={{0,4},{1,5},{2,6},{3,7},{4,0},{5,1},{6,2},{7,3},{8,12},{9,13},{10,... | collective-permute-start | bytes 393224 | tf_op jit(solution)/shard_map/ppermute | solution.py:411
  82.7 6.0 %collective-permute-start.19 = (bf16[32,2048]{1,0:T(8,128)(2,1)S(1)}, bf16[32,2048]{1,0:T(8,128)(2,1)S(1)}, u32[]{:S(2)}, u32[]{:S(2)}) collective-permute-start(bf16[32,2048]{1,0:T(8,128)(2,1)S(1)} %get-tuple-element.45), channel_id=1, source_target_pairs={{0,6},{1,7},{2,0},{3,1},{4,2},{5,3},{6,4},{7,5},{8,14},{9,15},{10,... | collective-permute-start | bytes 393224 | tf_op jit(solution)/shard_map/ppermute | solution.py:411

commit v2 on v1

--- a/solution.py
+++ b/solution.py
@@ -158,29 +158,28 @@
         att_ref[:rows, cols] = (acc[:, :HEAD] / acc[:, HEAD:]).astype(jnp.bfloat16)
         att_ref[rows:, cols] = jnp.broadcast_to(step_ref[h:h + 1, :], (STEP_ROWS, HEAD)).astype(jnp.bfloat16)
     w_copy.wait()
-    each, wide, half = rows // n_tp, w_ref.shape[1] // n_tp, w_ref.shape[1] // 2
+    each, wide, split, piece = rows // n_tp, w_ref.shape[1] // n_tp, keep_ref.shape[1], 256
     g_refs = (g0_ref, g1_ref, g2_ref, g3_ref)
-    for g in range(n_tp):
-        part = jnp.dot(att_ref[...], w_ref[:, g * wide:(g + 1) * wide], preferred_element_type=jnp.float32)
-        token_ref[:, g * wide:(g + 1) * wide] = part[rows:, :]
+    for c in range(0, w_ref.shape[1], piece):
+        part = jnp.dot(att_ref[...], w_ref[:, c:c + piece], preferred_element_type=jnp.float32)
+        token_ref[:, c:c + piece] = part[rows:, :]
         part = part.astype(jnp.bfloat16)
-        if g * wide < half:
-            cols = slice(g * wide, (g + 1) * wide)
-            keep_ref[:, cols] = part[:rows // 2, :]
-            send_ref[:, cols] = part[rows // 2:rows, :]
+        if c < split:
+            keep_ref[:, c:c + piece] = part[:rows // 2, :]
+            send_ref[:, c:c + piece] = part[rows // 2:rows, :]
         else:
-            cols = slice(g * wide - half, (g + 1) * wide - half)
+            cols = slice(c - split, c - split + piece)
             for dx, g_ref in enumerate(g_refs):
                 g_ref[:each, cols] = part[dx * each:(dx + 1) * each, :]
                 g_ref[each:2 * each, cols] = part[rows // 2 + dx * each:rows // 2 + (dx + 1) * each, :]
     for g_ref in g_refs:
-        g_ref[:, half:] = jnp.zeros((2 * each, LANES), jnp.bfloat16)
+        g_ref[:, -LANES:] = jnp.zeros((2 * each, LANES), jnp.bfloat16)
     for i in range(n_tp):
         dy, dx = divmod(i, X)
         start = pl.multiple_of(flag_ref[START + i] * (wide // each), wide)
         for j in range(wide // LANES):
-            piece = token_ref[:1, pl.ds(start + j * LANES, LANES)].astype(jnp.bfloat16)
-            g_refs[dx][dy * each + j:dy * each + j + 1, half:] = piece
+            chunk = token_ref[:1, pl.ds(start + j * LANES, LANES)].astype(jnp.bfloat16)
+            g_refs[dx][dy * each + j:dy * each + j + 1, -LANES:] = chunk
 
 
 def middle_kernel(keep_ref, recv_ref, g0_ref, g1_ref, g2_ref, g3_ref, f0_ref, f1_ref, f2_ref, f3_ref, mine_ref, give_ref):
@@ -197,15 +196,15 @@
 
 
 def sum_kernel(f0_ref, f1_ref, f2_ref, f3_ref, mine_ref, give_ref, out_ref, step_ref):
-    half = f0_ref.shape[1]
+    split, rest = f0_ref.shape[1], mine_ref.shape[1] - LANES
     total = f0_ref[...]
     for ref in (f1_ref, f2_ref, f3_ref):
         total = total + ref[...].astype(jnp.float32)
-    out_ref[:, :half] = total.astype(jnp.bfloat16)
+    out_ref[:, :split] = total.astype(jnp.bfloat16)
     total = mine_ref[...] + give_ref[...].astype(jnp.float32)
-    out_ref[:, half:] = total[:, :half].astype(jnp.bfloat16)
+    out_ref[:, split:] = total[:, :rest].astype(jnp.bfloat16)
     for j in range(step_ref.shape[1] // LANES):
-        step_ref[:, j * LANES:(j + 1) * LANES] = total[j:j + 1, half:].astype(jnp.bfloat16)
+        step_ref[:, j * LANES:(j + 1) * LANES] = total[j:j + 1, rest:].astype(jnp.bfloat16)
 
 
 def decode_kernel(len_ref, q_ref, nk_ref, nv_ref, k_hbm, v_hbm, out_ref, k_ref, v_ref, k_sem, v_sem, *, heads):
@@ -375,13 +374,13 @@
     other_3 = send(ring_3, SWAP_CORE)
     m, acc = step("attend_3", (OTHER + 2, OWN + 3), [[other_2], [ring_3]], m, acc)
 
-    each, half = rows // n_tp, width // 2
+    each, split = rows // n_tp, width * 9 // 16
     bf16 = functools.partial(jax.ShapeDtypeStruct, dtype=jnp.bfloat16)
     keep, give_y, *over_x = pl.pallas_call(
         functools.partial(last_kernel, rows=rows, heads=heads, n_tp=n_tp),
         in_specs=[smem] + [vmem] * 5 + [anywhere],
         out_specs=[vmem] * 6,
-        out_shape=[bf16((rows // 2, half))] * 2 + [bf16((2 * each, half + LANES))] * X,
+        out_shape=[bf16((rows // 2, split))] * 2 + [bf16((2 * each, width - split + LANES))] * X,
         scratch_shapes=[
             pltpu.VMEM((rows + STEP_ROWS, heads * HEAD), jnp.bfloat16),
             pltpu.VMEM(state[1].shape, jnp.float32),
@@ -402,8 +401,8 @@
         middle_kernel,
         in_specs=[vmem] * 6,
         out_specs=[vmem] * 6,
-        out_shape=[jax.ShapeDtypeStruct((each, half), jnp.float32)] + [bf16((each, half))] * 3
-        + [jax.ShapeDtypeStruct((each, half + LANES), jnp.float32), bf16((each, half + LANES))],
+        out_shape=[jax.ShapeDtypeStruct((each, split), jnp.float32)] + [bf16((each, split))] * 3
+        + [jax.ShapeDtypeStruct((each, width - split + LANES), jnp.float32), bf16((each, width - split + LANES))],
         compiler_params=params(24),
         name="sum_first",
     )(keep, from_y, over_x[0], *from_x)

time: 89.7 us -> 87.9 us (0.980)
  waiting for transfers between devices: 32.1 us -> 30.3 us
    ppermute x3, waiting for transfers between devices: 4.41 us -> 0.46 us  [body(): lax.ppermute(give_x[dx - 1], 'tp', over_x_pairs(dx))]
    ppermute x1, waiting for transfers between devices: 0.01 us -> 3.53 us  [body(): given = lax.ppermute(give, 'tp', OVER_Y)]
    ppermute x3, waiting for transfers between devices: 11.6 us -> 10.2 us  [body(): lax.ppermute(over_x[dx], 'tp', over_x_pairs(dx))]
  transfers between devices with their start and end apart: 21 -> 21, of which waited for: 9 -> 8; matrix products, arithmetic and copies ran while one was open for 0% -> 0% of each run, Pallas kernels for 25% -> 26%
where the time goes in v2:
time: 87.9 us; the launch traced here: 87.6 us
  Pallas kernels  32.1 us (37%)
  waiting for transfers between devices  30.3 us (34%)
  starting transfers between devices  23 us (26%)
  between operations  1.44 us (2%)
    ppermute x13, waiting for transfers between devices, send(): return lax.ppermute(block, 'seq', pairs)  16.1 us
    pallas_call x3, Pallas kernels, step(): pl.pallas_call(functools.partial(step_kernel, rows=rows, heads=heads, at=...  14.7 us
    ppermute x3, waiting for transfers between devices, body(): lax.ppermute(over_x[dx], 'tp', over_x_pairs(dx))  10.2 us
    ppermute x13, starting transfers between devices, send(): return lax.ppermute(block, 'seq', pairs)  9.9 us
    pallas_call x1, Pallas kernels, body(): pl.pallas_call(functools.partial(last_kernel, rows=rows, heads=heads, n_t...  6.43 us
    ppermute x3, starting transfers between devices, body(): lax.ppermute(over_x[dx], 'tp', over_x_pairs(dx))  5.65 us
    ppermute x3, starting transfers between devices, body(): lax.ppermute(give_x[dx - 1], 'tp', over_x_pairs(dx))  5.37 us
    pallas_call x1, Pallas kernels, body(): pl.pallas_call(functools.partial(local_kernel, rows=rows, heads=heads, n_...  4.33 us
  transfers between devices with their start and end apart: 21, of which 8 were waited for; matrix products, arithmetic and copies ran while one was open for 0% of the time, Pallas kernels for 26%

profile of v2, /device:TPU:128, one launch (start us, length us, event | category | flops | bytes accessed | tf_op | source)
XLA Modules:
  0.0 87.6 jit_solution(10613710371639556431)
XLA Ops:
  0.6 1.5 %pack_own.1.own_ref = bf16[512,128]{1,0:T(8,128)(2,1)} custom-call(bf16[256,128]{1,0:T(8,128)(2,1)} %k_hbm.2, bf16[256,128]{1,0:T(8,128)(2,1)} %v_hbm.2), custom_call_target="tpu_custom_call" | custom-call | tf_op jit(solution)/shard_map/pack_own/pallas_call | solution.py:304
  2.2 3.3 %collective-permute-start = (bf16[512,128]{1,0:T(8,128)(2,1)}, bf16[512,128]{1,0:T(8,128)(2,1)S(1)}, u32[]{:S(2)}, u32[]{:S(2)}) collective-permute-start(bf16[512,128]{1,0:T(8,128)(2,1)} %pack_own.1.own_ref), channel_id=1, source_target_pairs={{0,16},{8,24},{16,0},{24,8},{32,48},{40,56},{48,32},{56,40},{64,80... | collective-permute-start | bytes 393224 | tf_op jit(solution)/shard_map/ppermute | solution.py:293
  5.5 0.0 collective-permute-start.3
  5.5 0.0 collective-permute-start.2
  6.1 0.0 copy-start.3
  6.1 3.4 %decode.1.__1_.step_ref = f32[8,128]{1,0:T(8,128)} custom-call(s32[1]{0:T(128)S(6)} %copy.32.len_ref, bf16[1,1024]{1,0:T(2,128)(2,1)} %q_ref.2, bf16[1,128]{1,0:T(2,128)(2,1)} %nk_ref.1, bf16[1,128]{1,0:T(2,128)(2,1)} %nv_ref.1, bf16[1,4096,128]{2,1,0:T(8,128)(2,1)} %k_hbm.3, bf16[1,4096,128]{2,1,0:T(8,128)(2,1)} %v_hbm.3), custom_call_target="tpu_custom_call" | custom-call | flops 1000000000 | bytes 2097152 | tf_op jit(solution)/shard_map/decode/pallas_call | solution.py:314
  9.6 0.0 collective-permute-done.__0_
  9.6 0.7 copy-done.1
  10.3 0.5 collective-permute-start.1
  10.8 0.1 stack.100._.flag_ref
  10.9 5.7 %collective-permute-done.3.far_ref = bf16[512,128]{1,0:T(8,128)(2,1)S(1)} collective-permute-done((bf16[512,128]{1,0:T(8,128)(2,1)}, bf16[512,128]{1,0:T(8,128)(2,1)S(1)}, u32[]{:S(2)}, u32[]{:S(2)}) %collective-permute-start.3) | collective-permute-done | bytes 131104 | tf_op jit(solution)/shard_map/ppermute | solution.py:293
  16.6 0.0 collective-permute-done.2.core_ref
  16.6 0.0 collective-permute-done.1.both_ref
  16.6 0.6 pack_here.1
  17.2 1.8 %collective-permute-start.4 = (bf16[2048,128]{1,0:T(8,128)(2,1)S(1)}, bf16[2048,128]{1,0:T(8,128)(2,1)S(1)}, u32[]{:S(2)}, u32[]{:S(2)}) collective-permute-start(bf16[2048,128]{1,0:T(8,128)(2,1)S(1)} %get-tuple-element.25.kv_ref), channel_id=1, source_target_pairs={{0,32},{8,232},{16,48},{24,248},{32,64},{40,8},{48,80},{56,24},{64... | collective-permute-start | bytes 1572872 | tf_op jit(solution)/shard_map/ppermute | solution.py:293
  19.0 0.4 collective-permute-start.8
  19.4 0.6 collective-permute-start.7
  20.0 2.7 %collective-permute-start.6 = (bf16[512,128]{1,0:T(8,128)(2,1)S(1)}, bf16[512,128]{1,0:T(8,128)(2,1)S(1)}, u32[]{:S(2)}, u32[]{:S(2)}) collective-permute-start(bf16[512,128]{1,0:T(8,128)(2,1)S(1)} %get-tuple-element.28.refs_1_), channel_id=1, source_target_pairs={{0,8},{8,0},{16,24},{24,16},{32,40},{40,32},{48,56},{56,48},{64,72... | collective-permute-start | bytes 393224 | tf_op jit(solution)/shard_map/ppermute | solution.py:293
  22.7 4.3 %attend_local.1 = (bf16[2048,256]{1,0:T(8,128)(2,1)S(1)}, f32[2048,128]{1,0:T(8,128)S(1)}, f32[2048,256]{1,0:T(8,128)S(1)}) custom-call(s32[19]{0:T(128)S(1)} %stack.100._.flag_ref, bf16[256,1024]{1,0:T(8,128)(2,1)S(1)} %copy-done.3, bf16[2048,128]{1,0:T(8,128)(2,1)S(1)} %get-tuple-element.25.kv_ref), custom_call_target="tpu_custom_call" | custom-call | flops 2147483648 | bytes 1048576 | tf_op jit(solution)/shard_map/attend_local/pallas_call | solution.py:341
  27.0 0.7 collective-permute-done.4.__0_
  27.7 0.5 collective-permute-start.5
  28.2 0.1 collective-permute-start.10
  28.4 0.0 collective-permute-done.7.refs_3_
  28.4 0.0 collective-permute-done.6.refs_2_
  28.4 6.4 %attend_1.1 = (f32[2048,128]{1,0:T(8,128)S(1)}, f32[2048,256]{1,0:T(8,128)S(1)}) custom-call(s32[19]{0:T(128)S(1)} %stack.100._.flag_ref, bf16[2048,256]{1,0:T(8,128)(2,1)S(1)} %get-tuple-element.26.q2_ref, bf16[2048,128]{1,0:T(8,128)(2,1)S(1)} %gate.5.refs_0_, ...), custom_call_target="tpu_custom_call", output_to_operand_aliasing={{0}: (7, {}), {1}: (8, {})} | custom-call | flops 4294967296 | bytes 1048576 | tf_op jit(solution)/shard_map/attend_1/pallas_call | solution.py:355
  34.8 3.3 %collective-permute-done.5.__0_ = bf16[2048,128]{1,0:T(8,128)(2,1)S(1)} collective-permute-done((bf16[2048,128]{1,0:T(8,128)(2,1)S(1)}, bf16[2048,128]{1,0:T(8,128)(2,1)S(1)}, u32[]{:S(2)}, u32[]{:S(2)}) %collective-permute-start.5) | collective-permute-done | bytes 524320 | tf_op jit(solution)/shard_map/ppermute | solution.py:293
  38.1 0.0 collective-permute-start.9
  38.1 0.0 collective-permute-start.12
  38.1 4.0 %attend_2.1 = (f32[2048,128]{1,0:T(8,128)S(1)}, f32[2048,256]{1,0:T(8,128)S(1)}) custom-call(s32[19]{0:T(128)S(1)} %stack.100._.flag_ref, bf16[2048,256]{1,0:T(8,128)(2,1)S(1)} %get-tuple-element.26.q2_ref, bf16[2048,128]{1,0:T(8,128)(2,1)S(1)} %collective-permute-done.10.refs_0_, ...), custom_call_target="tpu_custom_call", output_to_operand_aliasing={{0}: (4, {}), {1}: (5, {})} | custom-call | flops 4294967296 | bytes 1048576 | tf_op jit(solution)/shard_map/attend_2/pallas_call | solution.py:355
  42.2 6.3 %collective-permute-done.9.__0_ = bf16[2048,128]{1,0:T(8,128)(2,1)S(1)} collective-permute-done((bf16[2048,128]{1,0:T(8,128)(2,1)S(1)}, bf16[2048,128]{1,0:T(8,128)(2,1)S(1)}, u32[]{:S(2)}, u32[]{:S(2)}) %collective-permute-start.9) | collective-permute-done | bytes 524320 | tf_op jit(solution)/shard_map/ppermute | solution.py:293
  48.5 0.0 collective-permute-start.11
  48.5 4.3 %attend_3.1 = (f32[2048,128]{1,0:T(8,128)S(1)}, f32[2048,256]{1,0:T(8,128)S(1)}) custom-call(s32[19]{0:T(128)S(1)} %stack.100._.flag_ref, bf16[2048,256]{1,0:T(8,128)(2,1)S(1)} %get-tuple-element.26.q2_ref, bf16[2048,128]{1,0:T(8,128)(2,1)S(1)} %collective-permute-done.12.refs_0_, ...), custom_call_target="tpu_custom_call", output_to_operand_aliasing={{0}: (4, {}), {1}: (5, {})} | custom-call | flops 4294967296 | bytes 1048576 | tf_op jit(solution)/shard_map/attend_3/pallas_call | solution.py:355
  52.8 0.0 collective-permute-done.11.other_ref
  52.8 6.4 %attend_project.1 = (bf16[128,2304]{1,0:T(8,128)(2,1)S(1)}, bf16[128,2304]{1,0:T(8,128)(2,1)S(1)}, bf16[64,1920]{1,0:T(8,128)(2,1)S(1)}, bf16[64,1920]{1,0:T(8,1...) custom-call(s32[19]{0:T(128)S(1)} %stack.100._.flag_ref, ...), custom_call_target="tpu_custom_call" | custom-call | flops 4294967296 | bytes 1048576 | tf_op jit(solution)/shard_map/attend_project/pallas_call | solution.py:379
  59.2 0.8 collective-permute-start.13
  60.0 1.5 %collective-permute-start.14 = (bf16[64,1920]{1,0:T(8,128)(2,1)S(1)}, bf16[64,1920]{1,0:T(8,128)(2,1)S(1)}, u32[]{:S(2)}, u32[]{:S(2)}) collective-permute-start(bf16[64,1920]{1,0:T(8,128)(2,1)S(1)} %get-tuple-element.39), channel_id=1, source_target_pairs={{0,2},{1,3},{2,4},{3,5},{4,6},{5,7},{6,0},{7,1},{8,10},{9,11},{10,... | collective-permute-start | bytes 737288 | tf_op jit(solution)/shard_map/ppermute | solution.py:399
  61.5 2.7 %collective-permute-start.15 = (bf16[64,1920]{1,0:T(8,128)(2,1)S(1)}, bf16[64,1920]{1,0:T(8,128)(2,1)S(1)}, u32[]{:S(2)}, u32[]{:S(2)}) collective-permute-start(bf16[64,1920]{1,0:T(8,128)(2,1)S(1)} %get-tuple-element.40), channel_id=1, source_target_pairs={{0,4},{1,5},{2,6},{3,7},{4,0},{5,1},{6,2},{7,3},{8,12},{9,13},{10,... | collective-permute-start | bytes 737288 | tf_op jit(solution)/shard_map/ppermute | solution.py:399
  64.2 1.4 %collective-permute-start.16 = (bf16[64,1920]{1,0:T(8,128)(2,1)S(1)}, bf16[64,1920]{1,0:T(8,128)(2,1)S(1)}, u32[]{:S(2)}, u32[]{:S(2)}) collective-permute-start(bf16[64,1920]{1,0:T(8,128)(2,1)S(1)} %get-tuple-element.41), channel_id=1, source_target_pairs={{0,6},{1,7},{2,0},{3,1},{4,2},{5,3},{6,4},{7,5},{8,14},{9,15},{10,... | collective-permute-start | bytes 737288 | tf_op jit(solution)/shard_map/ppermute | solution.py:399
  65.6 3.9 %collective-permute-done.14.g1_ref = bf16[64,1920]{1,0:T(8,128)(2,1)S(1)} collective-permute-done((bf16[64,1920]{1,0:T(8,128)(2,1)S(1)}, bf16[64,1920]{1,0:T(8,128)(2,1)S(1)}, u32[]{:S(2)}, u32[]{:S(2)}) %collective-permute-start.14) | collective-permute-done | bytes 245792 | tf_op jit(solution)/shard_map/ppermute | solution.py:399
  69.6 6.2 %collective-permute-done.15.g2_ref = bf16[64,1920]{1,0:T(8,128)(2,1)S(1)} collective-permute-done((bf16[64,1920]{1,0:T(8,128)(2,1)S(1)}, bf16[64,1920]{1,0:T(8,128)(2,1)S(1)}, u32[]{:S(2)}, u32[]{:S(2)}) %collective-permute-start.15) | collective-permute-done | bytes 245792 | tf_op jit(solution)/shard_map/ppermute | solution.py:399
  75.8 0.2 sum_first.1
  76.1 1.4 %collective-permute-start.17 = (bf16[32,2304]{1,0:T(8,128)(2,1)S(1)}, bf16[32,2304]{1,0:T(8,128)(2,1)S(1)}, u32[]{:S(2)}, u32[]{:S(2)}) collective-permute-start(bf16[32,2304]{1,0:T(8,128)(2,1)S(1)} %get-tuple-element.43), channel_id=1, source_target_pairs={{0,2},{1,3},{2,4},{3,5},{4,6},{5,7},{6,0},{7,1},{8,10},{9,11},{10,... | collective-permute-start | bytes 442376 | tf_op jit(solution)/shard_map/ppermute | solution.py:410
  77.5 2.4 %collective-permute-start.18 = (bf16[32,2304]{1,0:T(8,128)(2,1)S(1)}, bf16[32,2304]{1,0:T(8,128)(2,1)S(1)}, u32[]{:S(2)}, u32[]{:S(2)}) collective-permute-start(bf16[32,2304]{1,0:T(8,128)(2,1)S(1)} %get-tuple-element.44), channel_id=1, source_target_pairs={{0,4},{1,5},{2,6},{3,7},{4,0},{5,1},{6,2},{7,3},{8,12},{9,13},{10,... | collective-permute-start | bytes 442376 | tf_op jit(solution)/shard_map/ppermute | solution.py:410
  79.9 1.6 %collective-permute-start.19 = (bf16[32,2304]{1,0:T(8,128)(2,1)S(1)}, bf16[32,2304]{1,0:T(8,128)(2,1)S(1)}, u32[]{:S(2)}, u32[]{:S(2)}) collective-permute-start(bf16[32,2304]{1,0:T(8,128)(2,1)S(1)} %get-tuple-element.45), channel_id=1, source_target_pairs={{0,6},{1,7},{2,0},{3,1},{4,2},{5,3},{6,4},{7,5},{8,14},{9,15},{10,... | collective-permute-start | bytes 442376 | tf_op jit(solution)/shard_map/ppermute | solution.py:410
  81.5 1.3 %collective-permute-start.20 = (bf16[32,1920]{1,0:T(8,128)(2,1)S(1)}, bf16[32,1920]{1,0:T(8,128)(2,1)S(1)}, u32[]{:S(2)}, u32[]{:S(2)}) collective-permute-start(bf16[32,1920]{1,0:T(8,128)(2,1)S(1)} %get-tuple-element.47), channel_id=1, source_target_pairs={{0,1},{1,0},{2,3},{3,2},{4,5},{5,4},{6,7},{7,6},{8,9},{9,8},{10,11... | collective-permute-start | bytes 368648 | tf_op jit(solution)/shard_map/ppermute | solution.py:409
  82.8 3.5 %collective-permute-done.20.give_ref = bf16[32,1920]{1,0:T(8,128)(2,1)S(1)} collective-permute-done((bf16[32,1920]{1,0:T(8,128)(2,1)S(1)}, bf16[32,1920]{1,0:T(8,128)(2,1)S(1)}, u32[]{:S(2)}, u32[]{:S(2)}) %collective-permute-start.20) | collective-permute-done | bytes 122912 | tf_op jit(solution)/shard_map/ppermute | solution.py:409
  86.4 0.5 collective-permute-done.18.f2_ref
  86.8 0.8 sum_last.1
  (17 shorter events, 0.0 us)
Async XLA Ops:
  2.2 7.4 %collective-permute-start = (bf16[512,128]{1,0:T(8,128)(2,1)}, bf16[512,128]{1,0:T(8,128)(2,1)S(1)}, u32[]{:S(2)}, u32[]{:S(2)}) collective-permute-start(bf16[512,128]{1,0:T(8,128)(2,1)} %pack_own.1.own_ref), channel_id=1, source_target_pairs={{0,16},{8,24},{16,0},{24,8},{32,48},{40,56},{48,32},{56,40},{64,80... | collective-permute-start | bytes 393224 | tf_op jit(solution)/shard_map/ppermute | solution.py:293
  5.5 11.2 %collective-permute-start.3 = (bf16[512,128]{1,0:T(8,128)(2,1)}, bf16[512,128]{1,0:T(8,128)(2,1)S(1)}, u32[]{:S(2)}, u32[]{:S(2)}) collective-permute-start(bf16[512,128]{1,0:T(8,128)(2,1)} %pack_own.1.own_ref), channel_id=1, source_target_pairs={{0,128},{8,136},{16,144},{24,152},{32,160},{40,168},{48,176},{56,1... | collective-permute-start | bytes 393224 | tf_op jit(solution)/shard_map/ppermute | solution.py:293
  5.5 11.2 %collective-permute-start.2 = (bf16[512,128]{1,0:T(8,128)(2,1)}, bf16[512,128]{1,0:T(8,128)(2,1)S(1)}, u32[]{:S(2)}, u32[]{:S(2)}) collective-permute-start(bf16[512,128]{1,0:T(8,128)(2,1)} %pack_own.1.own_ref), channel_id=1, source_target_pairs={{0,8},{8,0},{16,24},{24,16},{32,40},{40,32},{48,56},{56,48},{64,72... | collective-permute-start | bytes 393224 | tf_op jit(solution)/shard_map/ppermute | solution.py:293
  6.1 10.5 %copy-start = (bf16[512,128]{1,0:T(8,128)(2,1)S(1)}, bf16[512,128]{1,0:T(8,128)(2,1)}, u32[]{:S(2)}) copy-start(bf16[512,128]{1,0:T(8,128)(2,1)} %pack_own.1.own_ref) | copy-start | bytes 393220
  6.1 16.6 %copy-start.3 = (bf16[256,1024]{1,0:T(8,128)(2,1)S(1)}, bf16[256,1024]{1,0:T(8,128)(2,1)}, u32[]{:S(2)}) copy-start(bf16[256,1024]{1,0:T(8,128)(2,1)} %q_ref.3) | copy-start | bytes 1572868
  9.6 0.7 copy-start.1
  10.3 6.3 %collective-permute-start.1 = (bf16[512,128]{1,0:T(8,128)(2,1)S(1)}, bf16[512,128]{1,0:T(8,128)(2,1)S(1)}, u32[]{:S(2)}, u32[]{:S(2)}) collective-permute-start(bf16[512,128]{1,0:T(8,128)(2,1)S(1)} %gate.4.y_ref), channel_id=1, source_target_pairs={{0,8},{8,0},{16,24},{24,16},{32,40},{40,32},{48,56},{56,48},{64,72... | collective-permute-start | bytes 393224 | tf_op jit(solution)/shard_map/ppermute | solution.py:293
  17.2 10.5 %collective-permute-start.4 = (bf16[2048,128]{1,0:T(8,128)(2,1)S(1)}, bf16[2048,128]{1,0:T(8,128)(2,1)S(1)}, u32[]{:S(2)}, u32[]{:S(2)}) collective-permute-start(bf16[2048,128]{1,0:T(8,128)(2,1)S(1)} %get-tuple-element.25.kv_ref), channel_id=1, source_target_pairs={{0,32},{8,232},{16,48},{24,248},{32,64},{40,8},{48,80},{56,24},{64... | collective-permute-start | bytes 1572872 | tf_op jit(solution)/shard_map/ppermute | solution.py:293
  19.0 9.3 %collective-permute-start.8 = (bf16[512,128]{1,0:T(8,128)(2,1)S(1)}, bf16[512,128]{1,0:T(8,128)(2,1)S(1)}, u32[]{:S(2)}, u32[]{:S(2)}) collective-permute-start(bf16[512,128]{1,0:T(8,128)(2,1)S(1)} %get-tuple-element.28.refs_1_), channel_id=1, source_target_pairs={{0,16},{8,24},{16,0},{24,8},{32,48},{40,56},{48,32},{56,40},{64,80... | collective-permute-start | bytes 393224 | tf_op jit(solution)/shard_map/ppermute | solution.py:293
  19.4 8.9 %collective-permute-start.7 = (bf16[512,128]{1,0:T(8,128)(2,1)S(1)}, bf16[512,128]{1,0:T(8,128)(2,1)S(1)}, u32[]{:S(2)}, u32[]{:S(2)}) collective-permute-start(bf16[512,128]{1,0:T(8,128)(2,1)S(1)} %get-tuple-element.28.refs_1_), channel_id=1, source_target_pairs={{0,24},{8,16},{16,8},{24,0},{32,56},{40,48},{48,40},{56,32},{64,88... | collective-permute-start | bytes 393224 | tf_op jit(solution)/shard_map/ppermute | solution.py:293
  20.0 8.4 %collective-permute-start.6 = (bf16[512,128]{1,0:T(8,128)(2,1)S(1)}, bf16[512,128]{1,0:T(8,128)(2,1)S(1)}, u32[]{:S(2)}, u32[]{:S(2)}) collective-permute-start(bf16[512,128]{1,0:T(8,128)(2,1)S(1)} %get-tuple-element.28.refs_1_), channel_id=1, source_target_pairs={{0,8},{8,0},{16,24},{24,16},{32,40},{40,32},{48,56},{56,48},{64,72... | collective-permute-start | bytes 393224 | tf_op jit(solution)/shard_map/ppermute | solution.py:293
  27.7 10.4 %collective-permute-start.5 = (bf16[2048,128]{1,0:T(8,128)(2,1)S(1)}, bf16[2048,128]{1,0:T(8,128)(2,1)S(1)}, u32[]{:S(2)}, u32[]{:S(2)}) collective-permute-start(bf16[2048,128]{1,0:T(8,128)(2,1)S(1)} %gate.5.refs_0_), channel_id=1, source_target_pairs={{0,32},{8,232},{16,48},{24,248},{32,64},{40,8},{48,80},{56,24},{64... | collective-permute-start | bytes 1572872 | tf_op jit(solution)/shard_map/ppermute | solution.py:293
  28.2 9.9 %collective-permute-start.10 = (bf16[2048,128]{1,0:T(8,128)(2,1)S(1)}, bf16[2048,128]{1,0:T(8,128)(2,1)S(1)}, u32[]{:S(2)}, u32[]{:S(2)}) collective-permute-start(bf16[2048,128]{1,0:T(8,128)(2,1)S(1)} %gate.5.refs_0_), channel_id=1, source_target_pairs={{0,8},{8,0},{16,24},{24,16},{32,40},{40,32},{48,56},{56,48},{64,72... | collective-permute-start | bytes 1572872 | tf_op jit(solution)/shard_map/ppermute | solution.py:293
  38.1 10.4 %collective-permute-start.9 = (bf16[2048,128]{1,0:T(8,128)(2,1)S(1)}, bf16[2048,128]{1,0:T(8,128)(2,1)S(1)}, u32[]{:S(2)}, u32[]{:S(2)}) collective-permute-start(bf16[2048,128]{1,0:T(8,128)(2,1)S(1)} %gate.6.refs_1_), channel_id=1, source_target_pairs={{0,32},{8,232},{16,48},{24,248},{32,64},{40,8},{48,80},{56,24},{64... | collective-permute-start | bytes 1572872 | tf_op jit(solution)/shard_map/ppermute | solution.py:293
  38.1 10.4 %collective-permute-start.12 = (bf16[2048,128]{1,0:T(8,128)(2,1)S(1)}, bf16[2048,128]{1,0:T(8,128)(2,1)S(1)}, u32[]{:S(2)}, u32[]{:S(2)}) collective-permute-start(bf16[2048,128]{1,0:T(8,128)(2,1)S(1)} %gate.6.refs_1_), channel_id=1, source_target_pairs={{0,8},{8,0},{16,24},{24,16},{32,40},{40,32},{48,56},{56,48},{64,72... | collective-permute-start | bytes 1572872 | tf_op jit(solution)/shard_map/ppermute | solution.py:293
  48.5 4.3 %collective-permute-start.11 = (bf16[2048,128]{1,0:T(8,128)(2,1)S(1)}, bf16[2048,128]{1,0:T(8,128)(2,1)S(1)}, u32[]{:S(2)}, u32[]{:S(2)}) collective-permute-start(bf16[2048,128]{1,0:T(8,128)(2,1)S(1)} %gate.7.refs_1_), channel_id=1, source_target_pairs={{0,8},{8,0},{16,24},{24,16},{32,40},{40,32},{48,56},{56,48},{64,72... | collective-permute-start | bytes 1572872 | tf_op jit(solution)/shard_map/ppermute | solution.py:293
  48.5 4.3 %copy-start.2 = (f32[8,128]{1,0:T(8,128)S(1)}, f32[8,128]{1,0:T(8,128)}, u32[]{:S(2)}) copy-start(f32[8,128]{1,0:T(8,128)} %decode.1.__1_.step_ref) | copy-start | bytes 12292
  59.2 16.6 %collective-permute-start.13 = (bf16[128,2304]{1,0:T(8,128)(2,1)S(1)}, bf16[128,2304]{1,0:T(8,128)(2,1)S(1)}, u32[]{:S(2)}, u32[]{:S(2)}) collective-permute-start(bf16[128,2304]{1,0:T(8,128)(2,1)S(1)} %get-tuple-element.37), channel_id=1, source_target_pairs={{0,1},{1,0},{2,3},{3,2},{4,5},{5,4},{6,7},{7,6},{8,9},{9,8},{10,11... | collective-permute-start | bytes 1769480 | tf_op jit(solution)/shard_map/ppermute | solution.py:398
  60.0 9.6 %collective-permute-start.14 = (bf16[64,1920]{1,0:T(8,128)(2,1)S(1)}, bf16[64,1920]{1,0:T(8,128)(2,1)S(1)}, u32[]{:S(2)}, u32[]{:S(2)}) collective-permute-start(bf16[64,1920]{1,0:T(8,128)(2,1)S(1)} %get-tuple-element.39), channel_id=1, source_target_pairs={{0,2},{1,3},{2,4},{3,5},{4,6},{5,7},{6,0},{7,1},{8,10},{9,11},{10,... | collective-permute-start | bytes 737288 | tf_op jit(solution)/shard_map/ppermute | solution.py:399
  61.5 14.4 %collective-permute-start.15 = (bf16[64,1920]{1,0:T(8,128)(2,1)S(1)}, bf16[64,1920]{1,0:T(8,128)(2,1)S(1)}, u32[]{:S(2)}, u32[]{:S(2)}) collective-permute-start(bf16[64,1920]{1,0:T(8,128)(2,1)S(1)} %get-tuple-element.40), channel_id=1, source_target_pairs={{0,4},{1,5},{2,6},{3,7},{4,0},{5,1},{6,2},{7,3},{8,12},{9,13},{10,... | collective-permute-start | bytes 737288 | tf_op jit(solution)/shard_map/ppermute | solution.py:399
  64.2 11.6 %collective-permute-start.16 = (bf16[64,1920]{1,0:T(8,128)(2,1)S(1)}, bf16[64,1920]{1,0:T(8,128)(2,1)S(1)}, u32[]{:S(2)}, u32[]{:S(2)}) collective-permute-start(bf16[64,1920]{1,0:T(8,128)(2,1)S(1)} %get-tuple-element.41), channel_id=1, source_target_pairs={{0,6},{1,7},{2,0},{3,1},{4,2},{5,3},{6,4},{7,5},{8,14},{9,15},{10,... | collective-permute-start | bytes 737288 | tf_op jit(solution)/shard_map/ppermute | solution.py:399
  76.1 10.3 %collective-permute-start.17 = (bf16[32,2304]{1,0:T(8,128)(2,1)S(1)}, bf16[32,2304]{1,0:T(8,128)(2,1)S(1)}, u32[]{:S(2)}, u32[]{:S(2)}) collective-permute-start(bf16[32,2304]{1,0:T(8,128)(2,1)S(1)} %get-tuple-element.43), channel_id=1, source_target_pairs={{0,2},{1,3},{2,4},{3,5},{4,6},{5,7},{6,0},{7,1},{8,10},{9,11},{10,... | collective-permute-start | bytes 442376 | tf_op jit(solution)/shard_map/ppermute | solution.py:410
  77.5 9.3 %collective-permute-start.18 = (bf16[32,2304]{1,0:T(8,128)(2,1)S(1)}, bf16[32,2304]{1,0:T(8,128)(2,1)S(1)}, u32[]{:S(2)}, u32[]{:S(2)}) collective-permute-start(bf16[32,2304]{1,0:T(8,128)(2,1)S(1)} %get-tuple-element.44), channel_id=1, source_target_pairs={{0,4},{1,5},{2,6},{3,7},{4,0},{5,1},{6,2},{7,3},{8,12},{9,13},{10,... | collective-permute-start | bytes 442376 | tf_op jit(solution)/shard_map/ppermute | solution.py:410
  79.9 6.9 %collective-permute-start.19 = (bf16[32,2304]{1,0:T(8,128)(2,1)S(1)}, bf16[32,2304]{1,0:T(8,128)(2,1)S(1)}, u32[]{:S(2)}, u32[]{:S(2)}) collective-permute-start(bf16[32,2304]{1,0:T(8,128)(2,1)S(1)} %get-tuple-element.45), channel_id=1, source_target_pairs={{0,6},{1,7},{2,0},{3,1},{4,2},{5,3},{6,4},{7,5},{8,14},{9,15},{10,... | collective-permute-start | bytes 442376 | tf_op jit(solution)/shard_map/ppermute | solution.py:410
  81.5 4.9 %collective-permute-start.20 = (bf16[32,1920]{1,0:T(8,128)(2,1)S(1)}, bf16[32,1920]{1,0:T(8,128)(2,1)S(1)}, u32[]{:S(2)}, u32[]{:S(2)}) collective-permute-start(bf16[32,1920]{1,0:T(8,128)(2,1)S(1)} %get-tuple-element.47), channel_id=1, source_target_pairs={{0,1},{1,0},{2,3},{3,2},{4,5},{5,4},{6,7},{7,6},{8,9},{9,8},{10,11... | collective-permute-start | bytes 368648 | tf_op jit(solution)/shard_map/ppermute | solution.py:409

commit v3 on v2

--- a/solution.py
+++ b/solution.py
@@ -33,7 +33,7 @@
 SWAP_Y = seq_pairs(lambda z, yh, c: (z, 1 - yh, c))
 SWAP_CORE = seq_pairs(lambda z, yh, c: (z, yh, 1 - c))
 SWAP_BOTH = seq_pairs(lambda z, yh, c: (z, 1 - yh, 1 - c))
-FAR = seq_pairs(lambda z, yh, c: (z + Z // 2, yh, c))
+FAR = seq_pairs(lambda z, yh, c: (z + Z // 2 if z < Z // 2 else Z - 1 - z, yh, c))
 RING = seq_pairs(lambda z, yh, c: (z + 1 if c == 0 else z - 1, yh, c))
 
 
@@ -172,14 +172,14 @@
             for dx, g_ref in enumerate(g_refs):
                 g_ref[:each, cols] = part[dx * each:(dx + 1) * each, :]
                 g_ref[each:2 * each, cols] = part[rows // 2 + dx * each:rows // 2 + (dx + 1) * each, :]
-    for g_ref in g_refs:
-        g_ref[:, -LANES:] = jnp.zeros((2 * each, LANES), jnp.bfloat16)
+    line = lax.broadcasted_iota(jnp.int32, (each, LANES), 0)
     for i in range(n_tp):
         dy, dx = divmod(i, X)
         start = pl.multiple_of(flag_ref[START + i] * (wide // each), wide)
+        tile = jnp.zeros((each, LANES), jnp.float32)
         for j in range(wide // LANES):
-            chunk = token_ref[:1, pl.ds(start + j * LANES, LANES)].astype(jnp.bfloat16)
-            g_refs[dx][dy * each + j:dy * each + j + 1, -LANES:] = chunk
+            tile = jnp.where(line == j, token_ref[:1, pl.ds(start + j * LANES, LANES)], tile)
+        g_refs[dx][dy * each:(dy + 1) * each, -LANES:] = tile.astype(jnp.bfloat16)
 
 
 def middle_kernel(keep_ref, recv_ref, g0_ref, g1_ref, g2_ref, g3_ref, f0_ref, f1_ref, f2_ref, f3_ref, mine_ref, give_ref):
@@ -396,7 +396,7 @@
         name="attend_project",
     )(flags, q2, other_3, m, acc, step_attention, out_weight)
     from_y = lax.ppermute(give_y, "tp", OVER_Y)
-    from_x = [lax.ppermute(over_x[dx], "tp", over_x_pairs(dx)) for dx in (1, 2, 3)]
+    from_x = [lax.ppermute(over_x[dx], "tp", over_x_pairs(dx)) for dx in (2, 1, 3)]
     f0, *give_x, mine, give = pl.pallas_call(
         middle_kernel,
         in_specs=[vmem] * 6,
@@ -407,7 +407,7 @@
         name="sum_first",
     )(keep, from_y, over_x[0], *from_x)
     given = lax.ppermute(give, "tp", OVER_Y)
-    given_x = [lax.ppermute(give_x[dx - 1], "tp", over_x_pairs(dx)) for dx in (1, 2, 3)]
+    given_x = [lax.ppermute(give_x[dx - 1], "tp", over_x_pairs(dx)) for dx in (2, 1, 3)]
     prefill_out, decode_out = pl.pallas_call(
         sum_kernel,
         in_specs=[vmem] * 6,

time: 87.9 us -> 87.7 us (level)
  waiting for transfers between devices: 30.3 us -> 28.5 us
  starting transfers between devices: 23 us -> 24.6 us
    ppermute x3, waiting for transfers between devices: 10.2 us -> 9.03 us  [body(): lax.ppermute(over_x[dx], 'tp', over_x_pairs(dx))]
    ppermute x3, starting transfers between devices: 5.37 us -> 6.34 us  [body(): lax.ppermute(give_x[dx - 1], 'tp', over_x_pairs(dx))]
  transfers between devices with their start and end apart: 21 -> 21, of which waited for: 8 -> 9; matrix products, arithmetic and copies ran while one was open for 0% -> 0% of each run, Pallas kernels for 26% -> 26%
where the time goes in v3:
time: 87.7 us; the launch traced here: 87.4 us
  Pallas kernels  32.1 us (37%)
  waiting for transfers between devices  28.5 us (32%)
  starting transfers between devices  24.6 us (28%)
  between operations  1.45 us (2%)
    ppermute x13, waiting for transfers between devices, send(): return lax.ppermute(block, 'seq', pairs)  15.2 us
    pallas_call x3, Pallas kernels, step(): pl.pallas_call(functools.partial(step_kernel, rows=rows, heads=heads, at=...  14.7 us
    ppermute x13, starting transfers between devices, send(): return lax.ppermute(block, 'seq', pairs)  10.5 us
    ppermute x3, waiting for transfers between devices, body(): lax.ppermute(over_x[dx], 'tp', over_x_pairs(dx))  9.03 us
    pallas_call x1, Pallas kernels, body(): pl.pallas_call(functools.partial(last_kernel, rows=rows, heads=heads, n_t...  6.42 us
    ppermute x3, starting transfers between devices, body(): lax.ppermute(give_x[dx - 1], 'tp', over_x_pairs(dx))  6.34 us
    ppermute x3, starting transfers between devices, body(): lax.ppermute(over_x[dx], 'tp', over_x_pairs(dx))  6.26 us
    pallas_call x1, Pallas kernels, body(): pl.pallas_call(functools.partial(local_kernel, rows=rows, heads=heads, n_...  4.33 us
  transfers between devices with their start and end apart: 21, of which 9 were waited for; matrix products, arithmetic and copies ran while one was open for 0% of the time, Pallas kernels for 26%

profile of v3, /device:TPU:128, one launch (start us, length us, event | category | flops | bytes accessed | tf_op | source)
XLA Modules:
  0.0 87.4 jit_solution(16846837069795327534)
XLA Ops:
  0.6 1.5 %pack_own.1.own_ref = bf16[512,128]{1,0:T(8,128)(2,1)} custom-call(bf16[256,128]{1,0:T(8,128)(2,1)} %k_hbm.2, bf16[256,128]{1,0:T(8,128)(2,1)} %v_hbm.2), custom_call_target="tpu_custom_call" | custom-call | tf_op jit(solution)/shard_map/pack_own/pallas_call | solution.py:304
  2.2 3.3 %collective-permute-start = (bf16[512,128]{1,0:T(8,128)(2,1)}, bf16[512,128]{1,0:T(8,128)(2,1)S(1)}, u32[]{:S(2)}, u32[]{:S(2)}) collective-permute-start(bf16[512,128]{1,0:T(8,128)(2,1)} %pack_own.1.own_ref), channel_id=1, source_target_pairs={{0,16},{8,24},{16,0},{24,8},{32,48},{40,56},{48,32},{56,40},{64,80... | collective-permute-start | bytes 393224 | tf_op jit(solution)/shard_map/ppermute | solution.py:293
  5.5 0.1 collective-permute-start.3
  6.2 0.0 copy-start.3
  6.2 3.4 %decode.1.__1_.step_ref = f32[8,128]{1,0:T(8,128)} custom-call(s32[1]{0:T(128)S(6)} %copy.32.len_ref, bf16[1,1024]{1,0:T(2,128)(2,1)} %q_ref.2, bf16[1,128]{1,0:T(2,128)(2,1)} %nk_ref.1, bf16[1,128]{1,0:T(2,128)(2,1)} %nv_ref.1, bf16[1,4096,128]{2,1,0:T(8,128)(2,1)} %k_hbm.3, bf16[1,4096,128]{2,1,0:T(8,128)(2,1)} %v_hbm.3), custom_call_target="tpu_custom_call" | custom-call | flops 1000000000 | bytes 2097152 | tf_op jit(solution)/shard_map/decode/pallas_call | solution.py:314
  9.7 0.0 collective-permute-done.__0_
  9.7 0.7 copy-done.1
  10.4 0.5 collective-permute-start.1
  10.9 0.1 stack.100._.flag_ref
  11.0 5.4 %collective-permute-done.3.far_ref = bf16[512,128]{1,0:T(8,128)(2,1)S(1)} collective-permute-done((bf16[512,128]{1,0:T(8,128)(2,1)}, bf16[512,128]{1,0:T(8,128)(2,1)S(1)}, u32[]{:S(2)}, u32[]{:S(2)}) %collective-permute-start.3) | collective-permute-done | bytes 131104 | tf_op jit(solution)/shard_map/ppermute | solution.py:293
  16.4 0.6 pack_here.1
  17.0 2.1 %collective-permute-start.4 = (bf16[2048,128]{1,0:T(8,128)(2,1)S(1)}, bf16[2048,128]{1,0:T(8,128)(2,1)S(1)}, u32[]{:S(2)}, u32[]{:S(2)}) collective-permute-start(bf16[2048,128]{1,0:T(8,128)(2,1)S(1)} %get-tuple-element.25.kv_ref), channel_id=1, source_target_pairs={{0,32},{8,232},{16,48},{24,248},{32,64},{40,8},{48,80},{56,24},{64... | collective-permute-start | bytes 1572872 | tf_op jit(solution)/shard_map/ppermute | solution.py:293
  19.1 0.3 collective-permute-start.8
  19.4 0.6 collective-permute-start.7
  20.0 2.8 %collective-permute-start.6 = (bf16[512,128]{1,0:T(8,128)(2,1)S(1)}, bf16[512,128]{1,0:T(8,128)(2,1)S(1)}, u32[]{:S(2)}, u32[]{:S(2)}) collective-permute-start(bf16[512,128]{1,0:T(8,128)(2,1)S(1)} %get-tuple-element.28.refs_1_), channel_id=1, source_target_pairs={{0,8},{8,0},{16,24},{24,16},{32,40},{40,32},{48,56},{56,48},{64,72... | collective-permute-start | bytes 393224 | tf_op jit(solution)/shard_map/ppermute | solution.py:293
  22.8 4.3 %attend_local.1 = (bf16[2048,256]{1,0:T(8,128)(2,1)S(1)}, f32[2048,128]{1,0:T(8,128)S(1)}, f32[2048,256]{1,0:T(8,128)S(1)}) custom-call(s32[19]{0:T(128)S(1)} %stack.100._.flag_ref, bf16[256,1024]{1,0:T(8,128)(2,1)S(1)} %copy-done.3, bf16[2048,128]{1,0:T(8,128)(2,1)S(1)} %get-tuple-element.25.kv_ref), custom_call_target="tpu_custom_call" | custom-call | flops 2147483648 | bytes 1048576 | tf_op jit(solution)/shard_map/attend_local/pallas_call | solution.py:341
  27.1 0.4 collective-permute-done.4.__0_
  27.5 0.8 collective-permute-start.5
  28.3 0.0 collective-permute-done.8.refs_4_
  28.3 0.0 collective-permute-done.7.refs_3_
  28.4 6.4 %attend_1.1 = (f32[2048,128]{1,0:T(8,128)S(1)}, f32[2048,256]{1,0:T(8,128)S(1)}) custom-call(s32[19]{0:T(128)S(1)} %stack.100._.flag_ref, bf16[2048,256]{1,0:T(8,128)(2,1)S(1)} %get-tuple-element.26.q2_ref, bf16[2048,128]{1,0:T(8,128)(2,1)S(1)} %gate.5.refs_0_, ...), custom_call_target="tpu_custom_call", output_to_operand_aliasing={{0}: (7, {}), {1}: (8, {})} | custom-call | flops 4294967296 | bytes 1048576 | tf_op jit(solution)/shard_map/attend_1/pallas_call | solution.py:355
  34.8 3.1 %collective-permute-done.5.__0_ = bf16[2048,128]{1,0:T(8,128)(2,1)S(1)} collective-permute-done((bf16[2048,128]{1,0:T(8,128)(2,1)S(1)}, bf16[2048,128]{1,0:T(8,128)(2,1)S(1)}, u32[]{:S(2)}, u32[]{:S(2)}) %collective-permute-start.5) | collective-permute-done | bytes 524320 | tf_op jit(solution)/shard_map/ppermute | solution.py:293
  37.9 0.0 collective-permute-start.9
  37.9 0.0 collective-permute-start.12
  37.9 0.0 collective-permute-done.10.refs_0_
  37.9 4.0 %attend_2.1 = (f32[2048,128]{1,0:T(8,128)S(1)}, f32[2048,256]{1,0:T(8,128)S(1)}) custom-call(s32[19]{0:T(128)S(1)} %stack.100._.flag_ref, bf16[2048,256]{1,0:T(8,128)(2,1)S(1)} %get-tuple-element.26.q2_ref, bf16[2048,128]{1,0:T(8,128)(2,1)S(1)} %collective-permute-done.10.refs_0_, ...), custom_call_target="tpu_custom_call", output_to_operand_aliasing={{0}: (4, {}), {1}: (5, {})} | custom-call | flops 4294967296 | bytes 1048576 | tf_op jit(solution)/shard_map/attend_2/pallas_call | solution.py:355
  41.9 6.3 %collective-permute-done.9.__0_ = bf16[2048,128]{1,0:T(8,128)(2,1)S(1)} collective-permute-done((bf16[2048,128]{1,0:T(8,128)(2,1)S(1)}, bf16[2048,128]{1,0:T(8,128)(2,1)S(1)}, u32[]{:S(2)}, u32[]{:S(2)}) %collective-permute-start.9) | collective-permute-done | bytes 524320 | tf_op jit(solution)/shard_map/ppermute | solution.py:293
  48.3 0.0 collective-permute-start.11
  48.3 0.0 collective-permute-done.12.refs_0_
  48.3 4.3 %attend_3.1 = (f32[2048,128]{1,0:T(8,128)S(1)}, f32[2048,256]{1,0:T(8,128)S(1)}) custom-call(s32[19]{0:T(128)S(1)} %stack.100._.flag_ref, bf16[2048,256]{1,0:T(8,128)(2,1)S(1)} %get-tuple-element.26.q2_ref, bf16[2048,128]{1,0:T(8,128)(2,1)S(1)} %collective-permute-done.12.refs_0_, ...), custom_call_target="tpu_custom_call", output_to_operand_aliasing={{0}: (4, {}), {1}: (5, {})} | custom-call | flops 4294967296 | bytes 1048576 | tf_op jit(solution)/shard_map/attend_3/pallas_call | solution.py:355
  52.6 0.0 collective-permute-done.11.other_ref
  52.6 6.4 %attend_project.1 = (bf16[128,2304]{1,0:T(8,128)(2,1)S(1)}, bf16[128,2304]{1,0:T(8,128)(2,1)S(1)}, bf16[64,1920]{1,0:T(8,128)(2,1)S(1)}, bf16[64,1920]{1,0:T(8,1...) custom-call(s32[19]{0:T(128)S(1)} %stack.100._.flag_ref, ...), custom_call_target="tpu_custom_call" | custom-call | flops 4294967296 | bytes 1048576 | tf_op jit(solution)/shard_map/attend_project/pallas_call | solution.py:379
  59.0 0.8 collective-permute-start.13
  59.8 3.0 %collective-permute-start.14 = (bf16[64,1920]{1,0:T(8,128)(2,1)S(1)}, bf16[64,1920]{1,0:T(8,128)(2,1)S(1)}, u32[]{:S(2)}, u32[]{:S(2)}) collective-permute-start(bf16[64,1920]{1,0:T(8,128)(2,1)S(1)} %get-tuple-element.39), channel_id=1, source_target_pairs={{0,4},{1,5},{2,6},{3,7},{4,0},{5,1},{6,2},{7,3},{8,12},{9,13},{10,... | collective-permute-start | bytes 737288 | tf_op jit(solution)/shard_map/ppermute | solution.py:399
  62.8 0.6 collective-permute-start.15
  63.4 2.6 %collective-permute-start.16 = (bf16[64,1920]{1,0:T(8,128)(2,1)S(1)}, bf16[64,1920]{1,0:T(8,128)(2,1)S(1)}, u32[]{:S(2)}, u32[]{:S(2)}) collective-permute-start(bf16[64,1920]{1,0:T(8,128)(2,1)S(1)} %get-tuple-element.41), channel_id=1, source_target_pairs={{0,6},{1,7},{2,0},{3,1},{4,2},{5,3},{6,4},{7,5},{8,14},{9,15},{10,... | collective-permute-start | bytes 737288 | tf_op jit(solution)/shard_map/ppermute | solution.py:399
  66.0 4.0 %collective-permute-done.14.g1_ref = bf16[64,1920]{1,0:T(8,128)(2,1)S(1)} collective-permute-done((bf16[64,1920]{1,0:T(8,128)(2,1)S(1)}, bf16[64,1920]{1,0:T(8,128)(2,1)S(1)}, u32[]{:S(2)}, u32[]{:S(2)}) %collective-permute-start.14) | collective-permute-done | bytes 245792 | tf_op jit(solution)/shard_map/ppermute | solution.py:399
  70.1 4.9 %collective-permute-done.15.g2_ref = bf16[64,1920]{1,0:T(8,128)(2,1)S(1)} collective-permute-done((bf16[64,1920]{1,0:T(8,128)(2,1)S(1)}, bf16[64,1920]{1,0:T(8,128)(2,1)S(1)}, u32[]{:S(2)}, u32[]{:S(2)}) %collective-permute-start.15) | collective-permute-done | bytes 245792 | tf_op jit(solution)/shard_map/ppermute | solution.py:399
  74.9 0.1 collective-permute-done.16.g3_ref
  75.1 0.1 collective-permute-done.13.recv_ref
  75.1 0.2 sum_first.1
  75.4 3.1 %collective-permute-start.17 = (bf16[32,2304]{1,0:T(8,128)(2,1)S(1)}, bf16[32,2304]{1,0:T(8,128)(2,1)S(1)}, u32[]{:S(2)}, u32[]{:S(2)}) collective-permute-start(bf16[32,2304]{1,0:T(8,128)(2,1)S(1)} %get-tuple-element.43), channel_id=1, source_target_pairs={{0,4},{1,5},{2,6},{3,7},{4,0},{5,1},{6,2},{7,3},{8,12},{9,13},{10,... | collective-permute-start | bytes 442376 | tf_op jit(solution)/shard_map/ppermute | solution.py:410
  78.5 0.6 collective-permute-start.18
  79.1 2.6 %collective-permute-start.19 = (bf16[32,2304]{1,0:T(8,128)(2,1)S(1)}, bf16[32,2304]{1,0:T(8,128)(2,1)S(1)}, u32[]{:S(2)}, u32[]{:S(2)}) collective-permute-start(bf16[32,2304]{1,0:T(8,128)(2,1)S(1)} %get-tuple-element.45), channel_id=1, source_target_pairs={{0,6},{1,7},{2,0},{3,1},{4,2},{5,3},{6,4},{7,5},{8,14},{9,15},{10,... | collective-permute-start | bytes 442376 | tf_op jit(solution)/shard_map/ppermute | solution.py:410
  81.7 0.7 collective-permute-start.20
  82.4 4.2 %collective-permute-done.20.give_ref = bf16[32,1920]{1,0:T(8,128)(2,1)S(1)} collective-permute-done((bf16[32,1920]{1,0:T(8,128)(2,1)S(1)}, bf16[32,1920]{1,0:T(8,128)(2,1)S(1)}, u32[]{:S(2)}, u32[]{:S(2)}) %collective-permute-start.20) | collective-permute-done | bytes 122912 | tf_op jit(solution)/shard_map/ppermute | solution.py:409
  86.6 0.0 collective-permute-done.17.f1_ref
  86.6 0.8 sum_last.1
  (17 shorter events, 0.0 us)
Async XLA Ops:
  2.2 7.5 %collective-permute-start = (bf16[512,128]{1,0:T(8,128)(2,1)}, bf16[512,128]{1,0:T(8,128)(2,1)S(1)}, u32[]{:S(2)}, u32[]{:S(2)}) collective-permute-start(bf16[512,128]{1,0:T(8,128)(2,1)} %pack_own.1.own_ref), channel_id=1, source_target_pairs={{0,16},{8,24},{16,0},{24,8},{32,48},{40,56},{48,32},{56,40},{64,80... | collective-permute-start | bytes 393224 | tf_op jit(solution)/shard_map/ppermute | solution.py:293
  5.5 11.0 %collective-permute-start.3 = (bf16[512,128]{1,0:T(8,128)(2,1)}, bf16[512,128]{1,0:T(8,128)(2,1)S(1)}, u32[]{:S(2)}, u32[]{:S(2)}) collective-permute-start(bf16[512,128]{1,0:T(8,128)(2,1)} %pack_own.1.own_ref), channel_id=1, source_target_pairs={{0,128},{8,136},{16,144},{24,152},{32,160},{40,168},{48,176},{56,1... | collective-permute-start | bytes 393224 | tf_op jit(solution)/shard_map/ppermute | solution.py:293
  5.6 10.8 %collective-permute-start.2 = (bf16[512,128]{1,0:T(8,128)(2,1)}, bf16[512,128]{1,0:T(8,128)(2,1)S(1)}, u32[]{:S(2)}, u32[]{:S(2)}) collective-permute-start(bf16[512,128]{1,0:T(8,128)(2,1)} %pack_own.1.own_ref), channel_id=1, source_target_pairs={{0,8},{8,0},{16,24},{24,16},{32,40},{40,32},{48,56},{56,48},{64,72... | collective-permute-start | bytes 393224 | tf_op jit(solution)/shard_map/ppermute | solution.py:293
  6.2 10.2 %copy-start = (bf16[512,128]{1,0:T(8,128)(2,1)S(1)}, bf16[512,128]{1,0:T(8,128)(2,1)}, u32[]{:S(2)}) copy-start(bf16[512,128]{1,0:T(8,128)(2,1)} %pack_own.1.own_ref) | copy-start | bytes 393220
  6.2 16.6 %copy-start.3 = (bf16[256,1024]{1,0:T(8,128)(2,1)S(1)}, bf16[256,1024]{1,0:T(8,128)(2,1)}, u32[]{:S(2)}) copy-start(bf16[256,1024]{1,0:T(8,128)(2,1)} %q_ref.3) | copy-start | bytes 1572868
  9.7 0.7 copy-start.1
  10.4 6.0 %collective-permute-start.1 = (bf16[512,128]{1,0:T(8,128)(2,1)S(1)}, bf16[512,128]{1,0:T(8,128)(2,1)S(1)}, u32[]{:S(2)}, u32[]{:S(2)}) collective-permute-start(bf16[512,128]{1,0:T(8,128)(2,1)S(1)} %gate.4.y_ref), channel_id=1, source_target_pairs={{0,8},{8,0},{16,24},{24,16},{32,40},{40,32},{48,56},{56,48},{64,72... | collective-permute-start | bytes 393224 | tf_op jit(solution)/shard_map/ppermute | solution.py:293
  17.0 10.5 %collective-permute-start.4 = (bf16[2048,128]{1,0:T(8,128)(2,1)S(1)}, bf16[2048,128]{1,0:T(8,128)(2,1)S(1)}, u32[]{:S(2)}, u32[]{:S(2)}) collective-permute-start(bf16[2048,128]{1,0:T(8,128)(2,1)S(1)} %get-tuple-element.25.kv_ref), channel_id=1, source_target_pairs={{0,32},{8,232},{16,48},{24,248},{32,64},{40,8},{48,80},{56,24},{64... | collective-permute-start | bytes 1572872 | tf_op jit(solution)/shard_map/ppermute | solution.py:293
  19.1 9.2 %collective-permute-start.8 = (bf16[512,128]{1,0:T(8,128)(2,1)S(1)}, bf16[512,128]{1,0:T(8,128)(2,1)S(1)}, u32[]{:S(2)}, u32[]{:S(2)}) collective-permute-start(bf16[512,128]{1,0:T(8,128)(2,1)S(1)} %get-tuple-element.28.refs_1_), channel_id=1, source_target_pairs={{0,16},{8,24},{16,0},{24,8},{32,48},{40,56},{48,32},{56,40},{64,80... | collective-permute-start | bytes 393224 | tf_op jit(solution)/shard_map/ppermute | solution.py:293
  19.4 8.9 %collective-permute-start.7 = (bf16[512,128]{1,0:T(8,128)(2,1)S(1)}, bf16[512,128]{1,0:T(8,128)(2,1)S(1)}, u32[]{:S(2)}, u32[]{:S(2)}) collective-permute-start(bf16[512,128]{1,0:T(8,128)(2,1)S(1)} %get-tuple-element.28.refs_1_), channel_id=1, source_target_pairs={{0,24},{8,16},{16,8},{24,0},{32,56},{40,48},{48,40},{56,32},{64,88... | collective-permute-start | bytes 393224 | tf_op jit(solution)/shard_map/ppermute | solution.py:293
  20.0 8.4 %collective-permute-start.6 = (bf16[512,128]{1,0:T(8,128)(2,1)S(1)}, bf16[512,128]{1,0:T(8,128)(2,1)S(1)}, u32[]{:S(2)}, u32[]{:S(2)}) collective-permute-start(bf16[512,128]{1,0:T(8,128)(2,1)S(1)} %get-tuple-element.28.refs_1_), channel_id=1, source_target_pairs={{0,8},{8,0},{16,24},{24,16},{32,40},{40,32},{48,56},{56,48},{64,72... | collective-permute-start | bytes 393224 | tf_op jit(solution)/shard_map/ppermute | solution.py:293
  27.5 10.4 %collective-permute-start.5 = (bf16[2048,128]{1,0:T(8,128)(2,1)S(1)}, bf16[2048,128]{1,0:T(8,128)(2,1)S(1)}, u32[]{:S(2)}, u32[]{:S(2)}) collective-permute-start(bf16[2048,128]{1,0:T(8,128)(2,1)S(1)} %gate.5.refs_0_), channel_id=1, source_target_pairs={{0,32},{8,232},{16,48},{24,248},{32,64},{40,8},{48,80},{56,24},{64... | collective-permute-start | bytes 1572872 | tf_op jit(solution)/shard_map/ppermute | solution.py:293
  28.3 9.6 %collective-permute-start.10 = (bf16[2048,128]{1,0:T(8,128)(2,1)S(1)}, bf16[2048,128]{1,0:T(8,128)(2,1)S(1)}, u32[]{:S(2)}, u32[]{:S(2)}) collective-permute-start(bf16[2048,128]{1,0:T(8,128)(2,1)S(1)} %gate.5.refs_0_), channel_id=1, source_target_pairs={{0,8},{8,0},{16,24},{24,16},{32,40},{40,32},{48,56},{56,48},{64,72... | collective-permute-start | bytes 1572872 | tf_op jit(solution)/shard_map/ppermute | solution.py:293
  37.9 10.4 %collective-permute-start.9 = (bf16[2048,128]{1,0:T(8,128)(2,1)S(1)}, bf16[2048,128]{1,0:T(8,128)(2,1)S(1)}, u32[]{:S(2)}, u32[]{:S(2)}) collective-permute-start(bf16[2048,128]{1,0:T(8,128)(2,1)S(1)} %gate.6.refs_1_), channel_id=1, source_target_pairs={{0,32},{8,232},{16,48},{24,248},{32,64},{40,8},{48,80},{56,24},{64... | collective-permute-start | bytes 1572872 | tf_op jit(solution)/shard_map/ppermute | solution.py:293
  37.9 10.4 %collective-permute-start.12 = (bf16[2048,128]{1,0:T(8,128)(2,1)S(1)}, bf16[2048,128]{1,0:T(8,128)(2,1)S(1)}, u32[]{:S(2)}, u32[]{:S(2)}) collective-permute-start(bf16[2048,128]{1,0:T(8,128)(2,1)S(1)} %gate.6.refs_1_), channel_id=1, source_target_pairs={{0,8},{8,0},{16,24},{24,16},{32,40},{40,32},{48,56},{56,48},{64,72... | collective-permute-start | bytes 1572872 | tf_op jit(solution)/shard_map/ppermute | solution.py:293
  48.3 4.3 %collective-permute-start.11 = (bf16[2048,128]{1,0:T(8,128)(2,1)S(1)}, bf16[2048,128]{1,0:T(8,128)(2,1)S(1)}, u32[]{:S(2)}, u32[]{:S(2)}) collective-permute-start(bf16[2048,128]{1,0:T(8,128)(2,1)S(1)} %gate.7.refs_1_), channel_id=1, source_target_pairs={{0,8},{8,0},{16,24},{24,16},{32,40},{40,32},{48,56},{56,48},{64,72... | collective-permute-start | bytes 1572872 | tf_op jit(solution)/shard_map/ppermute | solution.py:293
  48.3 4.3 %copy-start.2 = (f32[8,128]{1,0:T(8,128)S(1)}, f32[8,128]{1,0:T(8,128)}, u32[]{:S(2)}) copy-start(f32[8,128]{1,0:T(8,128)} %decode.1.__1_.step_ref) | copy-start | bytes 12292
  59.0 16.1 %collective-permute-start.13 = (bf16[128,2304]{1,0:T(8,128)(2,1)S(1)}, bf16[128,2304]{1,0:T(8,128)(2,1)S(1)}, u32[]{:S(2)}, u32[]{:S(2)}) collective-permute-start(bf16[128,2304]{1,0:T(8,128)(2,1)S(1)} %get-tuple-element.37), channel_id=1, source_target_pairs={{0,1},{1,0},{2,3},{3,2},{4,5},{5,4},{6,7},{7,6},{8,9},{9,8},{10,11... | collective-permute-start | bytes 1769480 | tf_op jit(solution)/shard_map/ppermute | solution.py:398
  59.8 10.3 %collective-permute-start.14 = (bf16[64,1920]{1,0:T(8,128)(2,1)S(1)}, bf16[64,1920]{1,0:T(8,128)(2,1)S(1)}, u32[]{:S(2)}, u32[]{:S(2)}) collective-permute-start(bf16[64,1920]{1,0:T(8,128)(2,1)S(1)} %get-tuple-element.39), channel_id=1, source_target_pairs={{0,4},{1,5},{2,6},{3,7},{4,0},{5,1},{6,2},{7,3},{8,12},{9,13},{10,... | collective-permute-start | bytes 737288 | tf_op jit(solution)/shard_map/ppermute | solution.py:399
  62.8 12.1 %collective-permute-start.15 = (bf16[64,1920]{1,0:T(8,128)(2,1)S(1)}, bf16[64,1920]{1,0:T(8,128)(2,1)S(1)}, u32[]{:S(2)}, u32[]{:S(2)}) collective-permute-start(bf16[64,1920]{1,0:T(8,128)(2,1)S(1)} %get-tuple-element.40), channel_id=1, source_target_pairs={{0,2},{1,3},{2,4},{3,5},{4,6},{5,7},{6,0},{7,1},{8,10},{9,11},{10,... | collective-permute-start | bytes 737288 | tf_op jit(solution)/shard_map/ppermute | solution.py:399
  63.4 11.7 %collective-permute-start.16 = (bf16[64,1920]{1,0:T(8,128)(2,1)S(1)}, bf16[64,1920]{1,0:T(8,128)(2,1)S(1)}, u32[]{:S(2)}, u32[]{:S(2)}) collective-permute-start(bf16[64,1920]{1,0:T(8,128)(2,1)S(1)} %get-tuple-element.41), channel_id=1, source_target_pairs={{0,6},{1,7},{2,0},{3,1},{4,2},{5,3},{6,4},{7,5},{8,14},{9,15},{10,... | collective-permute-start | bytes 737288 | tf_op jit(solution)/shard_map/ppermute | solution.py:399
  75.4 11.2 %collective-permute-start.17 = (bf16[32,2304]{1,0:T(8,128)(2,1)S(1)}, bf16[32,2304]{1,0:T(8,128)(2,1)S(1)}, u32[]{:S(2)}, u32[]{:S(2)}) collective-permute-start(bf16[32,2304]{1,0:T(8,128)(2,1)S(1)} %get-tuple-element.43), channel_id=1, source_target_pairs={{0,4},{1,5},{2,6},{3,7},{4,0},{5,1},{6,2},{7,3},{8,12},{9,13},{10,... | collective-permute-start | bytes 442376 | tf_op jit(solution)/shard_map/ppermute | solution.py:410
  78.5 8.1 %collective-permute-start.18 = (bf16[32,2304]{1,0:T(8,128)(2,1)S(1)}, bf16[32,2304]{1,0:T(8,128)(2,1)S(1)}, u32[]{:S(2)}, u32[]{:S(2)}) collective-permute-start(bf16[32,2304]{1,0:T(8,128)(2,1)S(1)} %get-tuple-element.44), channel_id=1, source_target_pairs={{0,2},{1,3},{2,4},{3,5},{4,6},{5,7},{6,0},{7,1},{8,10},{9,11},{10,... | collective-permute-start | bytes 442376 | tf_op jit(solution)/shard_map/ppermute | solution.py:410
  79.1 7.5 %collective-permute-start.19 = (bf16[32,2304]{1,0:T(8,128)(2,1)S(1)}, bf16[32,2304]{1,0:T(8,128)(2,1)S(1)}, u32[]{:S(2)}, u32[]{:S(2)}) collective-permute-start(bf16[32,2304]{1,0:T(8,128)(2,1)S(1)} %get-tuple-element.45), channel_id=1, source_target_pairs={{0,6},{1,7},{2,0},{3,1},{4,2},{5,3},{6,4},{7,5},{8,14},{9,15},{10,... | collective-permute-start | bytes 442376 | tf_op jit(solution)/shard_map/ppermute | solution.py:410
  81.7 4.9 %collective-permute-start.20 = (bf16[32,1920]{1,0:T(8,128)(2,1)S(1)}, bf16[32,1920]{1,0:T(8,128)(2,1)S(1)}, u32[]{:S(2)}, u32[]{:S(2)}) collective-permute-start(bf16[32,1920]{1,0:T(8,128)(2,1)S(1)} %get-tuple-element.47), channel_id=1, source_target_pairs={{0,1},{1,0},{2,3},{3,2},{4,5},{5,4},{6,7},{7,6},{8,9},{9,8},{10,11... | collective-permute-start | bytes 368648 | tf_op jit(solution)/shard_map/ppermute | solution.py:409

commit v4 on v3

--- a/solution.py
+++ b/solution.py
@@ -140,9 +140,13 @@
         acc_ref[...] = acc_in[...]
 
 
-def step_kernel(flag_ref, q2_ref, *refs, rows, heads, at, counts):
+def step_kernel(flag_ref, q2_ref, *refs, rows, heads, at, counts, passes):
     groups = [refs[:counts[0]], refs[counts[0]:sum(counts)]]
-    m_in, acc_in, m_ref, acc_ref, k2_ref, v2_ref = refs[sum(counts):]
+    if passes is None:
+        m_in, acc_in, m_ref, acc_ref, k2_ref, v2_ref = refs[sum(counts):]
+    else:
+        m_in, acc_in, m_ref, acc_ref, pass_ref, k2_ref, v2_ref = refs[sum(counts):]
+        pass_ref[...] = groups[passes][0][...]
     attend_live(flag_ref, at, q2_ref, groups, k2_ref, v2_ref, m_in, acc_in, m_ref, acc_ref, rows, heads)
 
 
@@ -349,14 +353,15 @@
         name="attend_local",
     )(flags, queries, here)
 
-    def step(name, at, groups, m, acc):
+    def step(name, at, groups, m, acc, passes=None):
         counts = [len(group) for group in groups]
         n = sum(counts)
+        passed = () if passes is None else (jax.ShapeDtypeStruct(groups[passes][0].shape, jnp.bfloat16),)
         return pl.pallas_call(
-            functools.partial(step_kernel, rows=rows, heads=heads, at=at, counts=counts),
+            functools.partial(step_kernel, rows=rows, heads=heads, at=at, counts=counts, passes=passes),
             in_specs=[smem] + [vmem] * (3 + n),
-            out_specs=[vmem] * 2,
-            out_shape=state,
+            out_specs=[vmem] * (2 if passes is None else 3),
+            out_shape=state + passed,
             input_output_aliases={2 + n: 0, 3 + n: 1},
             scratch_shapes=[pltpu.VMEM((8 * rows, 2 * HEAD), jnp.bfloat16)] * 2,
             compiler_params=params(36),
@@ -365,11 +370,13 @@
         )(flags, q2, *groups[0], *groups[1], m, acc)
 
     ring_1 = after(ring_1, m)
-    ring_2, other_1 = send(ring_1, RING), send(ring_1, SWAP_CORE)
-    m, acc = step("attend_1", (OWN + 1, HALF), [[ring_1], fars], m, acc)
+    ring_2 = send(ring_1, RING)
+    m, acc, other_1 = step("attend_1", (OWN + 1, HALF), [[ring_1], fars], m, acc, passes=0)
+    other_1 = send(other_1, SWAP_CORE)
     ring_2 = after(ring_2, m)
-    ring_3, other_2 = send(ring_2, RING), send(ring_2, SWAP_CORE)
-    m, acc = step("attend_2", (OTHER + 1, OWN + 2), [[other_1], [ring_2]], m, acc)
+    ring_3 = send(ring_2, RING)
+    m, acc, other_2 = step("attend_2", (OTHER + 1, OWN + 2), [[other_1], [ring_2]], m, acc, passes=1)
+    other_2 = send(other_2, SWAP_CORE)
     ring_3 = after(ring_3, m)
     other_3 = send(ring_3, SWAP_CORE)
     m, acc = step("attend_3", (OTHER + 2, OWN + 3), [[other_2], [ring_3]], m, acc)

time: 87.7 us -> 87.7 us (level)
  no operation moved by 1% of the time
where the time goes in v4:
time: 87.7 us; the launch traced here: 87.4 us
  Pallas kernels  32.2 us (37%)
  waiting for transfers between devices  28.3 us (32%)
  starting transfers between devices  24.8 us (28%)
  between operations  1.45 us (2%)
    ppermute x13, waiting for transfers between devices, send(): return lax.ppermute(block, 'seq', pairs)  15 us
    pallas_call x3, Pallas kernels, step(): pl.pallas_call(functools.partial(step_kernel, rows=rows, heads=heads, at=...  14.8 us
    ppermute x13, starting transfers between devices, send(): return lax.ppermute(block, 'seq', pairs)  10.7 us
    ppermute x3, waiting for transfers between devices, body(): lax.ppermute(over_x[dx], 'tp', over_x_pairs(dx))  9.03 us
    pallas_call x1, Pallas kernels, body(): pl.pallas_call(functools.partial(last_kernel, rows=rows, heads=heads, n_t...  6.42 us
    ppermute x3, starting transfers between devices, body(): lax.ppermute(give_x[dx - 1], 'tp', over_x_pairs(dx))  6.34 us
    ppermute x3, starting transfers between devices, body(): lax.ppermute(over_x[dx], 'tp', over_x_pairs(dx))  6.26 us
    pallas_call x1, Pallas kernels, body(): pl.pallas_call(functools.partial(local_kernel, rows=rows, heads=heads, n_...  4.33 us
  transfers between devices with their start and end apart: 21, of which 9 were waited for; matrix products, arithmetic and copies ran while one was open for 0% of the time, Pallas kernels for 26%

profile of v4, /device:TPU:128, one launch (start us, length us, event | category | flops | bytes accessed | tf_op | source)
XLA Modules:
  0.0 87.4 jit_solution(5315336579490590592)
XLA Ops:
  0.6 1.5 %pack_own.1.own_ref = bf16[512,128]{1,0:T(8,128)(2,1)} custom-call(bf16[256,128]{1,0:T(8,128)(2,1)} %k_hbm.2, bf16[256,128]{1,0:T(8,128)(2,1)} %v_hbm.2), custom_call_target="tpu_custom_call" | custom-call | tf_op jit(solution)/shard_map/pack_own/pallas_call | solution.py:308
  2.2 3.3 %collective-permute-start = (bf16[512,128]{1,0:T(8,128)(2,1)}, bf16[512,128]{1,0:T(8,128)(2,1)S(1)}, u32[]{:S(2)}, u32[]{:S(2)}) collective-permute-start(bf16[512,128]{1,0:T(8,128)(2,1)} %pack_own.1.own_ref), channel_id=1, source_target_pairs={{0,16},{8,24},{16,0},{24,8},{32,48},{40,56},{48,32},{56,40},{64,80... | collective-permute-start | bytes 393224 | tf_op jit(solution)/shard_map/ppermute | solution.py:297
  5.5 0.1 collective-permute-start.3
  6.2 0.0 copy-start.3
  6.2 3.4 %decode.1.__1_.step_ref = f32[8,128]{1,0:T(8,128)} custom-call(s32[1]{0:T(128)S(6)} %copy.32.len_ref, bf16[1,1024]{1,0:T(2,128)(2,1)} %q_ref.2, bf16[1,128]{1,0:T(2,128)(2,1)} %nk_ref.1, bf16[1,128]{1,0:T(2,128)(2,1)} %nv_ref.1, bf16[1,4096,128]{2,1,0:T(8,128)(2,1)} %k_hbm.3, bf16[1,4096,128]{2,1,0:T(8,128)(2,1)} %v_hbm.3), custom_call_target="tpu_custom_call" | custom-call | flops 1000000000 | bytes 2097152 | tf_op jit(solution)/shard_map/decode/pallas_call | solution.py:318
  9.7 0.0 collective-permute-done.__0_
  9.7 0.7 copy-done.1
  10.4 0.5 collective-permute-start.1
  10.9 0.1 stack.100._.flag_ref
  11.0 5.4 %collective-permute-done.3.far_ref = bf16[512,128]{1,0:T(8,128)(2,1)S(1)} collective-permute-done((bf16[512,128]{1,0:T(8,128)(2,1)}, bf16[512,128]{1,0:T(8,128)(2,1)S(1)}, u32[]{:S(2)}, u32[]{:S(2)}) %collective-permute-start.3) | collective-permute-done | bytes 131104 | tf_op jit(solution)/shard_map/ppermute | solution.py:297
  16.4 0.6 pack_here.1
  17.0 2.1 %collective-permute-start.4 = (bf16[2048,128]{1,0:T(8,128)(2,1)S(1)}, bf16[2048,128]{1,0:T(8,128)(2,1)S(1)}, u32[]{:S(2)}, u32[]{:S(2)}) collective-permute-start(bf16[2048,128]{1,0:T(8,128)(2,1)S(1)} %get-tuple-element.27.kv_ref), channel_id=1, source_target_pairs={{0,32},{8,232},{16,48},{24,248},{32,64},{40,8},{48,80},{56,24},{64... | collective-permute-start | bytes 1572872 | tf_op jit(solution)/shard_map/ppermute | solution.py:297
  19.1 0.3 collective-permute-start.8
  19.4 0.6 collective-permute-start.7
  20.0 2.8 %collective-permute-start.6 = (bf16[512,128]{1,0:T(8,128)(2,1)S(1)}, bf16[512,128]{1,0:T(8,128)(2,1)S(1)}, u32[]{:S(2)}, u32[]{:S(2)}) collective-permute-start(bf16[512,128]{1,0:T(8,128)(2,1)S(1)} %get-tuple-element.30.refs_1_), channel_id=1, source_target_pairs={{0,8},{8,0},{16,24},{24,16},{32,40},{40,32},{48,56},{56,48},{64,72... | collective-permute-start | bytes 393224 | tf_op jit(solution)/shard_map/ppermute | solution.py:297
  22.8 4.3 %attend_local.1 = (bf16[2048,256]{1,0:T(8,128)(2,1)S(1)}, f32[2048,128]{1,0:T(8,128)S(1)}, f32[2048,256]{1,0:T(8,128)S(1)}) custom-call(s32[19]{0:T(128)S(1)} %stack.100._.flag_ref, bf16[256,1024]{1,0:T(8,128)(2,1)S(1)} %copy-done.3, bf16[2048,128]{1,0:T(8,128)(2,1)S(1)} %get-tuple-element.27.kv_ref), custom_call_target="tpu_custom_call" | custom-call | flops 2147483648 | bytes 1048576 | tf_op jit(solution)/shard_map/attend_local/pallas_call | solution.py:345
  27.1 0.4 collective-permute-done.4.__0_
  27.5 0.8 collective-permute-start.5
  28.3 0.0 collective-permute-done.7.refs_3_
  28.3 0.0 collective-permute-done.6.refs_2_
  28.3 6.4 %attend_1.1 = (f32[2048,128]{1,0:T(8,128)S(1)}, f32[2048,256]{1,0:T(8,128)S(1)}, bf16[2048,128]{1,0:T(8,128)(2,1)S(1)}) custom-call(s32[19]{0:T(128)S(1)} %stack.100._.flag_ref, bf16[2048,256]{1,0:T(8,128)(2,1)S(1)} %get-tuple-element.28.q2_ref, bf16[2048,128]{1,0:T(8,128)(2,1)S(1)} %gate.5.refs_0_, ...), custom_call_target="tpu_custom_call", output_to_operand_aliasing={{0}: (7, {}), {1}: (8, {})} | custom-call | flops 4294967296 | bytes 1048576 | tf_op jit(solution)/shard_map/attend_1/pallas_call | solution.py:360
  34.8 0.1 collective-permute-start.10
  34.9 3.0 %collective-permute-done.5.__0_ = bf16[2048,128]{1,0:T(8,128)(2,1)S(1)} collective-permute-done((bf16[2048,128]{1,0:T(8,128)(2,1)S(1)}, bf16[2048,128]{1,0:T(8,128)(2,1)S(1)}, u32[]{:S(2)}, u32[]{:S(2)}) %collective-permute-start.5) | collective-permute-done | bytes 524320 | tf_op jit(solution)/shard_map/ppermute | solution.py:297
  37.9 0.0 collective-permute-start.9
  37.9 0.0 collective-permute-done.10.refs_0_
  37.9 4.1 %attend_2.1 = (f32[2048,128]{1,0:T(8,128)S(1)}, f32[2048,256]{1,0:T(8,128)S(1)}, bf16[2048,128]{1,0:T(8,128)(2,1)S(1)}) custom-call(s32[19]{0:T(128)S(1)} %stack.100._.flag_ref, bf16[2048,256]{1,0:T(8,128)(2,1)S(1)} %get-tuple-element.28.q2_ref, bf16[2048,128]{1,0:T(8,128)(2,1)S(1)} %collective-permute-done.10.refs_0_, ...), custom_call_target="tpu_custom_call", output_to_operand_aliasing={{0}: (4, {}), {1}: (5, {})} | custom-call | flops 4294967296 | bytes 1048576 | tf_op jit(solution)/shard_map/attend_2/pallas_call | solution.py:360
  42.0 0.1 collective-permute-start.12
  42.1 6.2 %collective-permute-done.9.__0_ = bf16[2048,128]{1,0:T(8,128)(2,1)S(1)} collective-permute-done((bf16[2048,128]{1,0:T(8,128)(2,1)S(1)}, bf16[2048,128]{1,0:T(8,128)(2,1)S(1)}, u32[]{:S(2)}, u32[]{:S(2)}) %collective-permute-start.9) | collective-permute-done | bytes 524320 | tf_op jit(solution)/shard_map/ppermute | solution.py:297
  48.3 0.0 collective-permute-start.11
  48.3 0.0 collective-permute-done.12.refs_0_
  48.3 4.3 %attend_3.1 = (f32[2048,128]{1,0:T(8,128)S(1)}, f32[2048,256]{1,0:T(8,128)S(1)}) custom-call(s32[19]{0:T(128)S(1)} %stack.100._.flag_ref, bf16[2048,256]{1,0:T(8,128)(2,1)S(1)} %get-tuple-element.28.q2_ref, bf16[2048,128]{1,0:T(8,128)(2,1)S(1)} %collective-permute-done.12.refs_0_, ...), custom_call_target="tpu_custom_call", output_to_operand_aliasing={{0}: (4, {}), {1}: (5, {})} | custom-call | flops 4294967296 | bytes 1048576 | tf_op jit(solution)/shard_map/attend_3/pallas_call | solution.py:360
  52.6 0.0 collective-permute-done.11.other_ref
  52.6 6.4 %attend_project.1 = (bf16[128,2304]{1,0:T(8,128)(2,1)S(1)}, bf16[128,2304]{1,0:T(8,128)(2,1)S(1)}, bf16[64,1920]{1,0:T(8,128)(2,1)S(1)}, bf16[64,1920]{1,0:T(8,1...) custom-call(s32[19]{0:T(128)S(1)} %stack.100._.flag_ref, ...), custom_call_target="tpu_custom_call" | custom-call | flops 4294967296 | bytes 1048576 | tf_op jit(solution)/shard_map/attend_project/pallas_call | solution.py:386
  59.0 0.8 collective-permute-start.13
  59.8 3.0 %collective-permute-start.14 = (bf16[64,1920]{1,0:T(8,128)(2,1)S(1)}, bf16[64,1920]{1,0:T(8,128)(2,1)S(1)}, u32[]{:S(2)}, u32[]{:S(2)}) collective-permute-start(bf16[64,1920]{1,0:T(8,128)(2,1)S(1)} %get-tuple-element.43), channel_id=1, source_target_pairs={{0,4},{1,5},{2,6},{3,7},{4,0},{5,1},{6,2},{7,3},{8,12},{9,13},{10,... | collective-permute-start | bytes 737288 | tf_op jit(solution)/shard_map/ppermute | solution.py:406
  62.8 0.6 collective-permute-start.15
  63.4 2.6 %collective-permute-start.16 = (bf16[64,1920]{1,0:T(8,128)(2,1)S(1)}, bf16[64,1920]{1,0:T(8,128)(2,1)S(1)}, u32[]{:S(2)}, u32[]{:S(2)}) collective-permute-start(bf16[64,1920]{1,0:T(8,128)(2,1)S(1)} %get-tuple-element.45), channel_id=1, source_target_pairs={{0,6},{1,7},{2,0},{3,1},{4,2},{5,3},{6,4},{7,5},{8,14},{9,15},{10,... | collective-permute-start | bytes 737288 | tf_op jit(solution)/shard_map/ppermute | solution.py:406
  66.0 4.0 %collective-permute-done.14.g1_ref = bf16[64,1920]{1,0:T(8,128)(2,1)S(1)} collective-permute-done((bf16[64,1920]{1,0:T(8,128)(2,1)S(1)}, bf16[64,1920]{1,0:T(8,128)(2,1)S(1)}, u32[]{:S(2)}, u32[]{:S(2)}) %collective-permute-start.14) | collective-permute-done | bytes 245792 | tf_op jit(solution)/shard_map/ppermute | solution.py:406
  70.1 4.9 %collective-permute-done.15.g2_ref = bf16[64,1920]{1,0:T(8,128)(2,1)S(1)} collective-permute-done((bf16[64,1920]{1,0:T(8,128)(2,1)S(1)}, bf16[64,1920]{1,0:T(8,128)(2,1)S(1)}, u32[]{:S(2)}, u32[]{:S(2)}) %collective-permute-start.15) | collective-permute-done | bytes 245792 | tf_op jit(solution)/shard_map/ppermute | solution.py:406
  74.9 0.1 collective-permute-done.16.g3_ref
  75.1 0.1 collective-permute-done.13.recv_ref
  75.1 0.2 sum_first.1
  75.4 3.1 %collective-permute-start.17 = (bf16[32,2304]{1,0:T(8,128)(2,1)S(1)}, bf16[32,2304]{1,0:T(8,128)(2,1)S(1)}, u32[]{:S(2)}, u32[]{:S(2)}) collective-permute-start(bf16[32,2304]{1,0:T(8,128)(2,1)S(1)} %get-tuple-element.47), channel_id=1, source_target_pairs={{0,4},{1,5},{2,6},{3,7},{4,0},{5,1},{6,2},{7,3},{8,12},{9,13},{10,... | collective-permute-start | bytes 442376 | tf_op jit(solution)/shard_map/ppermute | solution.py:417
  78.5 0.6 collective-permute-start.18
  79.1 2.6 %collective-permute-start.19 = (bf16[32,2304]{1,0:T(8,128)(2,1)S(1)}, bf16[32,2304]{1,0:T(8,128)(2,1)S(1)}, u32[]{:S(2)}, u32[]{:S(2)}) collective-permute-start(bf16[32,2304]{1,0:T(8,128)(2,1)S(1)} %get-tuple-element.49), channel_id=1, source_target_pairs={{0,6},{1,7},{2,0},{3,1},{4,2},{5,3},{6,4},{7,5},{8,14},{9,15},{10,... | collective-permute-start | bytes 442376 | tf_op jit(solution)/shard_map/ppermute | solution.py:417
  81.7 0.7 collective-permute-start.20
  82.4 4.2 %collective-permute-done.20.give_ref = bf16[32,1920]{1,0:T(8,128)(2,1)S(1)} collective-permute-done((bf16[32,1920]{1,0:T(8,128)(2,1)S(1)}, bf16[32,1920]{1,0:T(8,128)(2,1)S(1)}, u32[]{:S(2)}, u32[]{:S(2)}) %collective-permute-start.20) | collective-permute-done | bytes 122912 | tf_op jit(solution)/shard_map/ppermute | solution.py:416
  86.6 0.8 sum_last.1
  (17 shorter events, 0.0 us)
Async XLA Ops:
  2.2 7.5 %collective-permute-start = (bf16[512,128]{1,0:T(8,128)(2,1)}, bf16[512,128]{1,0:T(8,128)(2,1)S(1)}, u32[]{:S(2)}, u32[]{:S(2)}) collective-permute-start(bf16[512,128]{1,0:T(8,128)(2,1)} %pack_own.1.own_ref), channel_id=1, source_target_pairs={{0,16},{8,24},{16,0},{24,8},{32,48},{40,56},{48,32},{56,40},{64,80... | collective-permute-start | bytes 393224 | tf_op jit(solution)/shard_map/ppermute | solution.py:297
  5.5 11.0 %collective-permute-start.3 = (bf16[512,128]{1,0:T(8,128)(2,1)}, bf16[512,128]{1,0:T(8,128)(2,1)S(1)}, u32[]{:S(2)}, u32[]{:S(2)}) collective-permute-start(bf16[512,128]{1,0:T(8,128)(2,1)} %pack_own.1.own_ref), channel_id=1, source_target_pairs={{0,128},{8,136},{16,144},{24,152},{32,160},{40,168},{48,176},{56,1... | collective-permute-start | bytes 393224 | tf_op jit(solution)/shard_map/ppermute | solution.py:297
  5.6 10.8 %collective-permute-start.2 = (bf16[512,128]{1,0:T(8,128)(2,1)}, bf16[512,128]{1,0:T(8,128)(2,1)S(1)}, u32[]{:S(2)}, u32[]{:S(2)}) collective-permute-start(bf16[512,128]{1,0:T(8,128)(2,1)} %pack_own.1.own_ref), channel_id=1, source_target_pairs={{0,8},{8,0},{16,24},{24,16},{32,40},{40,32},{48,56},{56,48},{64,72... | collective-permute-start | bytes 393224 | tf_op jit(solution)/shard_map/ppermute | solution.py:297
  6.2 10.2 %copy-start = (bf16[512,128]{1,0:T(8,128)(2,1)S(1)}, bf16[512,128]{1,0:T(8,128)(2,1)}, u32[]{:S(2)}) copy-start(bf16[512,128]{1,0:T(8,128)(2,1)} %pack_own.1.own_ref) | copy-start | bytes 393220
  6.2 16.6 %copy-start.3 = (bf16[256,1024]{1,0:T(8,128)(2,1)S(1)}, bf16[256,1024]{1,0:T(8,128)(2,1)}, u32[]{:S(2)}) copy-start(bf16[256,1024]{1,0:T(8,128)(2,1)} %q_ref.3) | copy-start | bytes 1572868
  9.7 0.7 copy-start.1
  10.4 6.0 %collective-permute-start.1 = (bf16[512,128]{1,0:T(8,128)(2,1)S(1)}, bf16[512,128]{1,0:T(8,128)(2,1)S(1)}, u32[]{:S(2)}, u32[]{:S(2)}) collective-permute-start(bf16[512,128]{1,0:T(8,128)(2,1)S(1)} %gate.4.y_ref), channel_id=1, source_target_pairs={{0,8},{8,0},{16,24},{24,16},{32,40},{40,32},{48,56},{56,48},{64,72... | collective-permute-start | bytes 393224 | tf_op jit(solution)/shard_map/ppermute | solution.py:297
  17.0 10.5 %collective-permute-start.4 = (bf16[2048,128]{1,0:T(8,128)(2,1)S(1)}, bf16[2048,128]{1,0:T(8,128)(2,1)S(1)}, u32[]{:S(2)}, u32[]{:S(2)}) collective-permute-start(bf16[2048,128]{1,0:T(8,128)(2,1)S(1)} %get-tuple-element.27.kv_ref), channel_id=1, source_target_pairs={{0,32},{8,232},{16,48},{24,248},{32,64},{40,8},{48,80},{56,24},{64... | collective-permute-start | bytes 1572872 | tf_op jit(solution)/shard_map/ppermute | solution.py:297
  19.1 9.2 %collective-permute-start.8 = (bf16[512,128]{1,0:T(8,128)(2,1)S(1)}, bf16[512,128]{1,0:T(8,128)(2,1)S(1)}, u32[]{:S(2)}, u32[]{:S(2)}) collective-permute-start(bf16[512,128]{1,0:T(8,128)(2,1)S(1)} %get-tuple-element.30.refs_1_), channel_id=1, source_target_pairs={{0,16},{8,24},{16,0},{24,8},{32,48},{40,56},{48,32},{56,40},{64,80... | collective-permute-start | bytes 393224 | tf_op jit(solution)/shard_map/ppermute | solution.py:297
  19.4 8.9 %collective-permute-start.7 = (bf16[512,128]{1,0:T(8,128)(2,1)S(1)}, bf16[512,128]{1,0:T(8,128)(2,1)S(1)}, u32[]{:S(2)}, u32[]{:S(2)}) collective-permute-start(bf16[512,128]{1,0:T(8,128)(2,1)S(1)} %get-tuple-element.30.refs_1_), channel_id=1, source_target_pairs={{0,24},{8,16},{16,8},{24,0},{32,56},{40,48},{48,40},{56,32},{64,88... | collective-permute-start | bytes 393224 | tf_op jit(solution)/shard_map/ppermute | solution.py:297
  20.0 8.3 %collective-permute-start.6 = (bf16[512,128]{1,0:T(8,128)(2,1)S(1)}, bf16[512,128]{1,0:T(8,128)(2,1)S(1)}, u32[]{:S(2)}, u32[]{:S(2)}) collective-permute-start(bf16[512,128]{1,0:T(8,128)(2,1)S(1)} %get-tuple-element.30.refs_1_), channel_id=1, source_target_pairs={{0,8},{8,0},{16,24},{24,16},{32,40},{40,32},{48,56},{56,48},{64,72... | collective-permute-start | bytes 393224 | tf_op jit(solution)/shard_map/ppermute | solution.py:297
  27.5 10.4 %collective-permute-start.5 = (bf16[2048,128]{1,0:T(8,128)(2,1)S(1)}, bf16[2048,128]{1,0:T(8,128)(2,1)S(1)}, u32[]{:S(2)}, u32[]{:S(2)}) collective-permute-start(bf16[2048,128]{1,0:T(8,128)(2,1)S(1)} %gate.5.refs_0_), channel_id=1, source_target_pairs={{0,32},{8,232},{16,48},{24,248},{32,64},{40,8},{48,80},{56,24},{64... | collective-permute-start | bytes 1572872 | tf_op jit(solution)/shard_map/ppermute | solution.py:297
  34.8 3.1 %collective-permute-start.10 = (bf16[2048,128]{1,0:T(8,128)(2,1)S(1)}, bf16[2048,128]{1,0:T(8,128)(2,1)S(1)}, u32[]{:S(2)}, u32[]{:S(2)}) collective-permute-start(bf16[2048,128]{1,0:T(8,128)(2,1)S(1)} %get-tuple-element.33), channel_id=1, source_target_pairs={{0,8},{8,0},{16,24},{24,16},{32,40},{40,32},{48,56},{56,48},{64,72... | collective-permute-start | bytes 1572872 | tf_op jit(solution)/shard_map/ppermute | solution.py:297
  37.9 10.4 %collective-permute-start.9 = (bf16[2048,128]{1,0:T(8,128)(2,1)S(1)}, bf16[2048,128]{1,0:T(8,128)(2,1)S(1)}, u32[]{:S(2)}, u32[]{:S(2)}) collective-permute-start(bf16[2048,128]{1,0:T(8,128)(2,1)S(1)} %gate.6.refs_1_), channel_id=1, source_target_pairs={{0,32},{8,232},{16,48},{24,248},{32,64},{40,8},{48,80},{56,24},{64... | collective-permute-start | bytes 1572872 | tf_op jit(solution)/shard_map/ppermute | solution.py:297
  42.0 6.3 %collective-permute-start.12 = (bf16[2048,128]{1,0:T(8,128)(2,1)S(1)}, bf16[2048,128]{1,0:T(8,128)(2,1)S(1)}, u32[]{:S(2)}, u32[]{:S(2)}) collective-permute-start(bf16[2048,128]{1,0:T(8,128)(2,1)S(1)} %get-tuple-element.36), channel_id=1, source_target_pairs={{0,8},{8,0},{16,24},{24,16},{32,40},{40,32},{48,56},{56,48},{64,72... | collective-permute-start | bytes 1572872 | tf_op jit(solution)/shard_map/ppermute | solution.py:297
  48.3 4.3 %collective-permute-start.11 = (bf16[2048,128]{1,0:T(8,128)(2,1)S(1)}, bf16[2048,128]{1,0:T(8,128)(2,1)S(1)}, u32[]{:S(2)}, u32[]{:S(2)}) collective-permute-start(bf16[2048,128]{1,0:T(8,128)(2,1)S(1)} %gate.7.refs_1_), channel_id=1, source_target_pairs={{0,8},{8,0},{16,24},{24,16},{32,40},{40,32},{48,56},{56,48},{64,72... | collective-permute-start | bytes 1572872 | tf_op jit(solution)/shard_map/ppermute | solution.py:297
  48.3 4.3 %copy-start.2 = (f32[8,128]{1,0:T(8,128)S(1)}, f32[8,128]{1,0:T(8,128)}, u32[]{:S(2)}) copy-start(f32[8,128]{1,0:T(8,128)} %decode.1.__1_.step_ref) | copy-start | bytes 12292
  59.0 16.1 %collective-permute-start.13 = (bf16[128,2304]{1,0:T(8,128)(2,1)S(1)}, bf16[128,2304]{1,0:T(8,128)(2,1)S(1)}, u32[]{:S(2)}, u32[]{:S(2)}) collective-permute-start(bf16[128,2304]{1,0:T(8,128)(2,1)S(1)} %get-tuple-element.41), channel_id=1, source_target_pairs={{0,1},{1,0},{2,3},{3,2},{4,5},{5,4},{6,7},{7,6},{8,9},{9,8},{10,11... | collective-permute-start | bytes 1769480 | tf_op jit(solution)/shard_map/ppermute | solution.py:405
  59.8 10.3 %collective-permute-start.14 = (bf16[64,1920]{1,0:T(8,128)(2,1)S(1)}, bf16[64,1920]{1,0:T(8,128)(2,1)S(1)}, u32[]{:S(2)}, u32[]{:S(2)}) collective-permute-start(bf16[64,1920]{1,0:T(8,128)(2,1)S(1)} %get-tuple-element.43), channel_id=1, source_target_pairs={{0,4},{1,5},{2,6},{3,7},{4,0},{5,1},{6,2},{7,3},{8,12},{9,13},{10,... | collective-permute-start | bytes 737288 | tf_op jit(solution)/shard_map/ppermute | solution.py:406
  62.8 12.1 %collective-permute-start.15 = (bf16[64,1920]{1,0:T(8,128)(2,1)S(1)}, bf16[64,1920]{1,0:T(8,128)(2,1)S(1)}, u32[]{:S(2)}, u32[]{:S(2)}) collective-permute-start(bf16[64,1920]{1,0:T(8,128)(2,1)S(1)} %get-tuple-element.44), channel_id=1, source_target_pairs={{0,2},{1,3},{2,4},{3,5},{4,6},{5,7},{6,0},{7,1},{8,10},{9,11},{10,... | collective-permute-start | bytes 737288 | tf_op jit(solution)/shard_map/ppermute | solution.py:406
  63.4 11.7 %collective-permute-start.16 = (bf16[64,1920]{1,0:T(8,128)(2,1)S(1)}, bf16[64,1920]{1,0:T(8,128)(2,1)S(1)}, u32[]{:S(2)}, u32[]{:S(2)}) collective-permute-start(bf16[64,1920]{1,0:T(8,128)(2,1)S(1)} %get-tuple-element.45), channel_id=1, source_target_pairs={{0,6},{1,7},{2,0},{3,1},{4,2},{5,3},{6,4},{7,5},{8,14},{9,15},{10,... | collective-permute-start | bytes 737288 | tf_op jit(solution)/shard_map/ppermute | solution.py:406
  75.4 11.2 %collective-permute-start.17 = (bf16[32,2304]{1,0:T(8,128)(2,1)S(1)}, bf16[32,2304]{1,0:T(8,128)(2,1)S(1)}, u32[]{:S(2)}, u32[]{:S(2)}) collective-permute-start(bf16[32,2304]{1,0:T(8,128)(2,1)S(1)} %get-tuple-element.47), channel_id=1, source_target_pairs={{0,4},{1,5},{2,6},{3,7},{4,0},{5,1},{6,2},{7,3},{8,12},{9,13},{10,... | collective-permute-start | bytes 442376 | tf_op jit(solution)/shard_map/ppermute | solution.py:417
  78.5 8.1 %collective-permute-start.18 = (bf16[32,2304]{1,0:T(8,128)(2,1)S(1)}, bf16[32,2304]{1,0:T(8,128)(2,1)S(1)}, u32[]{:S(2)}, u32[]{:S(2)}) collective-permute-start(bf16[32,2304]{1,0:T(8,128)(2,1)S(1)} %get-tuple-element.48), channel_id=1, source_target_pairs={{0,2},{1,3},{2,4},{3,5},{4,6},{5,7},{6,0},{7,1},{8,10},{9,11},{10,... | collective-permute-start | bytes 442376 | tf_op jit(solution)/shard_map/ppermute | solution.py:417
  79.1 7.5 %collective-permute-start.19 = (bf16[32,2304]{1,0:T(8,128)(2,1)S(1)}, bf16[32,2304]{1,0:T(8,128)(2,1)S(1)}, u32[]{:S(2)}, u32[]{:S(2)}) collective-permute-start(bf16[32,2304]{1,0:T(8,128)(2,1)S(1)} %get-tuple-element.49), channel_id=1, source_target_pairs={{0,6},{1,7},{2,0},{3,1},{4,2},{5,3},{6,4},{7,5},{8,14},{9,15},{10,... | collective-permute-start | bytes 442376 | tf_op jit(solution)/shard_map/ppermute | solution.py:417
  81.7 4.9 %collective-permute-start.20 = (bf16[32,1920]{1,0:T(8,128)(2,1)S(1)}, bf16[32,1920]{1,0:T(8,128)(2,1)S(1)}, u32[]{:S(2)}, u32[]{:S(2)}) collective-permute-start(bf16[32,1920]{1,0:T(8,128)(2,1)S(1)} %get-tuple-element.51), channel_id=1, source_target_pairs={{0,1},{1,0},{2,3},{3,2},{4,5},{5,4},{6,7},{7,6},{8,9},{9,8},{10,11... | collective-permute-start | bytes 368648 | tf_op jit(solution)/shard_map/ppermute | solution.py:416

commit v5 on v3

--- a/solution.py
+++ b/solution.py
@@ -321,7 +321,7 @@
         cost_estimate=pl.CostEstimate(flops=10**9, bytes_accessed=2 * 2**20, transcendentals=heads * key_cache.shape[1]),
         name="decode",
     )(cache_lens, step_queries, new_keys, new_values, key_cache, value_cache)
-    by_y = after(by_y, step_attention)
+    far = after(far, step_attention)
     by_both = send(by_y, SWAP_CORE)
     here, far = pl.pallas_call(
         pack_here_kernel,

time: 87.7 us -> 88.4 us (level)
  waiting for transfers between devices: 28.5 us -> 29.9 us
    ppermute x13, waiting for transfers between devices: 15.2 us -> 16.6 us  [send(): return lax.ppermute(block, 'seq', pairs)]
  transfers between devices with their start and end apart: 21 -> 21, of which waited for: 9 -> 10; matrix products, arithmetic and copies ran while one was open for 0% -> 0% of each run, Pallas kernels for 26% -> 26%
where the time goes in v5:
time: 88.4 us; the launch traced here: 88.1 us
  Pallas kernels  32.1 us (36%)
  waiting for transfers between devices  29.9 us (34%)
  starting transfers between devices  23.9 us (27%)
  between operations  1.46 us (2%)
    ppermute x13, waiting for transfers between devices, send(): return lax.ppermute(block, 'seq', pairs)  16.6 us
    pallas_call x3, Pallas kernels, step(): pl.pallas_call(functools.partial(step_kernel, rows=rows, heads=heads, at=...  14.7 us
    ppermute x13, starting transfers between devices, send(): return lax.ppermute(block, 'seq', pairs)  9.82 us
    ppermute x3, waiting for transfers between devices, body(): lax.ppermute(over_x[dx], 'tp', over_x_pairs(dx))  9.03 us
    pallas_call x1, Pallas kernels, body(): pl.pallas_call(functools.partial(last_kernel, rows=rows, heads=heads, n_t...  6.42 us
    ppermute x3, starting transfers between devices, body(): lax.ppermute(give_x[dx - 1], 'tp', over_x_pairs(dx))  6.34 us
    ppermute x3, starting transfers between devices, body(): lax.ppermute(over_x[dx], 'tp', over_x_pairs(dx))  6.26 us
    pallas_call x1, Pallas kernels, body(): pl.pallas_call(functools.partial(local_kernel, rows=rows, heads=heads, n_...  4.33 us
  transfers between devices with their start and end apart: 21, of which 10 were waited for; matrix products, arithmetic and copies ran while one was open for 0% of the time, Pallas kernels for 26%

profile of v5, /device:TPU:128, one launch (start us, length us, event | category | flops | bytes accessed | tf_op | source)
XLA Modules:
  0.0 88.1 jit_solution(3090111041982113261)
XLA Ops:
  0.6 1.5 %pack_own.1.own_ref = bf16[512,128]{1,0:T(8,128)(2,1)} custom-call(bf16[256,128]{1,0:T(8,128)(2,1)} %k_hbm.2, bf16[256,128]{1,0:T(8,128)(2,1)} %v_hbm.2), custom_call_target="tpu_custom_call" | custom-call | tf_op jit(solution)/shard_map/pack_own/pallas_call | solution.py:304
  2.2 3.3 %collective-permute-start = (bf16[512,128]{1,0:T(8,128)(2,1)}, bf16[512,128]{1,0:T(8,128)(2,1)S(1)}, u32[]{:S(2)}, u32[]{:S(2)}) collective-permute-start(bf16[512,128]{1,0:T(8,128)(2,1)} %pack_own.1.own_ref), channel_id=1, source_target_pairs={{0,16},{8,24},{16,0},{24,8},{32,48},{40,56},{48,32},{56,40},{64,80... | collective-permute-start | bytes 393224 | tf_op jit(solution)/shard_map/ppermute | solution.py:293
  5.5 0.1 collective-permute-start.3
  5.6 0.0 collective-permute-start.2
  5.6 3.6 %collective-permute-done.y_ref = bf16[512,128]{1,0:T(8,128)(2,1)S(1)} collective-permute-done((bf16[512,128]{1,0:T(8,128)(2,1)}, bf16[512,128]{1,0:T(8,128)(2,1)S(1)}, u32[]{:S(2)}, u32[]{:S(2)}) %collective-permute-start) | collective-permute-done | bytes 131104 | tf_op jit(solution)/shard_map/ppermute | solution.py:293
  9.9 0.1 stack.100._.flag_ref
  10.0 0.0 copy-start.3
  10.0 3.4 %decode.1.__1_.step_ref = f32[8,128]{1,0:T(8,128)} custom-call(s32[1]{0:T(128)S(6)} %copy.32.len_ref, bf16[1,1024]{1,0:T(2,128)(2,1)} %q_ref.2, bf16[1,128]{1,0:T(2,128)(2,1)} %nk_ref.1, bf16[1,128]{1,0:T(2,128)(2,1)} %nv_ref.1, bf16[1,4096,128]{2,1,0:T(8,128)(2,1)} %k_hbm.3, bf16[1,4096,128]{2,1,0:T(8,128)(2,1)} %v_hbm.3), custom_call_target="tpu_custom_call" | custom-call | flops 1000000000 | bytes 2097152 | tf_op jit(solution)/shard_map/decode/pallas_call | solution.py:314
  13.5 2.9 %collective-permute-done.3.__0_ = bf16[512,128]{1,0:T(8,128)(2,1)S(1)} collective-permute-done((bf16[512,128]{1,0:T(8,128)(2,1)}, bf16[512,128]{1,0:T(8,128)(2,1)S(1)}, u32[]{:S(2)}, u32[]{:S(2)}) %collective-permute-start.3) | collective-permute-done | bytes 131104 | tf_op jit(solution)/shard_map/ppermute | solution.py:293
  16.4 0.7 copy-done.1
  17.1 0.0 collective-permute-done.2.core_ref
  17.1 0.0 collective-permute-done.1.both_ref
  17.1 0.6 pack_here.1
  17.7 2.0 %collective-permute-start.4 = (bf16[2048,128]{1,0:T(8,128)(2,1)S(1)}, bf16[2048,128]{1,0:T(8,128)(2,1)S(1)}, u32[]{:S(2)}, u32[]{:S(2)}) collective-permute-start(bf16[2048,128]{1,0:T(8,128)(2,1)S(1)} %get-tuple-element.25.kv_ref), channel_id=1, source_target_pairs={{0,32},{8,232},{16,48},{24,248},{32,64},{40,8},{48,80},{56,24},{64... | collective-permute-start | bytes 1572872 | tf_op jit(solution)/shard_map/ppermute | solution.py:293
  19.7 0.4 collective-permute-start.8
  20.1 0.6 collective-permute-start.7
  20.7 2.7 %collective-permute-start.6 = (bf16[512,128]{1,0:T(8,128)(2,1)S(1)}, bf16[512,128]{1,0:T(8,128)(2,1)S(1)}, u32[]{:S(2)}, u32[]{:S(2)}) collective-permute-start(bf16[512,128]{1,0:T(8,128)(2,1)S(1)} %get-tuple-element.28.refs_1_), channel_id=1, source_target_pairs={{0,8},{8,0},{16,24},{24,16},{32,40},{40,32},{48,56},{56,48},{64,72... | collective-permute-start | bytes 393224 | tf_op jit(solution)/shard_map/ppermute | solution.py:293
  23.4 4.3 %attend_local.1 = (bf16[2048,256]{1,0:T(8,128)(2,1)S(1)}, f32[2048,128]{1,0:T(8,128)S(1)}, f32[2048,256]{1,0:T(8,128)S(1)}) custom-call(s32[19]{0:T(128)S(1)} %stack.100._.flag_ref, bf16[256,1024]{1,0:T(8,128)(2,1)S(1)} %copy-done.3, bf16[2048,128]{1,0:T(8,128)(2,1)S(1)} %get-tuple-element.25.kv_ref), custom_call_target="tpu_custom_call" | custom-call | flops 2147483648 | bytes 1048576 | tf_op jit(solution)/shard_map/attend_local/pallas_call | solution.py:341
  27.7 0.5 collective-permute-done.4.__0_
  28.2 0.7 collective-permute-start.5
  28.9 0.0 collective-permute-done.7.refs_3_
  28.9 0.0 collective-permute-done.6.refs_2_
  28.9 6.4 %attend_1.1 = (f32[2048,128]{1,0:T(8,128)S(1)}, f32[2048,256]{1,0:T(8,128)S(1)}) custom-call(s32[19]{0:T(128)S(1)} %stack.100._.flag_ref, bf16[2048,256]{1,0:T(8,128)(2,1)S(1)} %get-tuple-element.26.q2_ref, bf16[2048,128]{1,0:T(8,128)(2,1)S(1)} %gate.5.refs_0_, ...), custom_call_target="tpu_custom_call", output_to_operand_aliasing={{0}: (7, {}), {1}: (8, {})} | custom-call | flops 4294967296 | bytes 1048576 | tf_op jit(solution)/shard_map/attend_1/pallas_call | solution.py:355
  35.4 3.2 %collective-permute-done.5.__0_ = bf16[2048,128]{1,0:T(8,128)(2,1)S(1)} collective-permute-done((bf16[2048,128]{1,0:T(8,128)(2,1)S(1)}, bf16[2048,128]{1,0:T(8,128)(2,1)S(1)}, u32[]{:S(2)}, u32[]{:S(2)}) %collective-permute-start.5) | collective-permute-done | bytes 524320 | tf_op jit(solution)/shard_map/ppermute | solution.py:293
  38.6 0.0 collective-permute-start.12
  38.6 0.0 collective-permute-done.10.refs_0_
  38.6 4.0 %attend_2.1 = (f32[2048,128]{1,0:T(8,128)S(1)}, f32[2048,256]{1,0:T(8,128)S(1)}) custom-call(s32[19]{0:T(128)S(1)} %stack.100._.flag_ref, bf16[2048,256]{1,0:T(8,128)(2,1)S(1)} %get-tuple-element.26.q2_ref, bf16[2048,128]{1,0:T(8,128)(2,1)S(1)} %collective-permute-done.10.refs_0_, ...), custom_call_target="tpu_custom_call", output_to_operand_aliasing={{0}: (4, {}), {1}: (5, {})} | custom-call | flops 4294967296 | bytes 1048576 | tf_op jit(solution)/shard_map/attend_2/pallas_call | solution.py:355
  42.6 6.3 %collective-permute-done.9.__0_ = bf16[2048,128]{1,0:T(8,128)(2,1)S(1)} collective-permute-done((bf16[2048,128]{1,0:T(8,128)(2,1)S(1)}, bf16[2048,128]{1,0:T(8,128)(2,1)S(1)}, u32[]{:S(2)}, u32[]{:S(2)}) %collective-permute-start.9) | collective-permute-done | bytes 524320 | tf_op jit(solution)/shard_map/ppermute | solution.py:293
  49.0 0.0 collective-permute-start.11
  49.0 0.0 collective-permute-done.12.refs_0_
  49.0 4.3 %attend_3.1 = (f32[2048,128]{1,0:T(8,128)S(1)}, f32[2048,256]{1,0:T(8,128)S(1)}) custom-call(s32[19]{0:T(128)S(1)} %stack.100._.flag_ref, bf16[2048,256]{1,0:T(8,128)(2,1)S(1)} %get-tuple-element.26.q2_ref, bf16[2048,128]{1,0:T(8,128)(2,1)S(1)} %collective-permute-done.12.refs_0_, ...), custom_call_target="tpu_custom_call", output_to_operand_aliasing={{0}: (4, {}), {1}: (5, {})} | custom-call | flops 4294967296 | bytes 1048576 | tf_op jit(solution)/shard_map/attend_3/pallas_call | solution.py:355
  53.3 6.4 %attend_project.1 = (bf16[128,2304]{1,0:T(8,128)(2,1)S(1)}, bf16[128,2304]{1,0:T(8,128)(2,1)S(1)}, bf16[64,1920]{1,0:T(8,128)(2,1)S(1)}, bf16[64,1920]{1,0:T(8,1...) custom-call(s32[19]{0:T(128)S(1)} %stack.100._.flag_ref, ...), custom_call_target="tpu_custom_call" | custom-call | flops 4294967296 | bytes 1048576 | tf_op jit(solution)/shard_map/attend_project/pallas_call | solution.py:379
  59.7 0.8 collective-permute-start.13
  60.5 3.0 %collective-permute-start.14 = (bf16[64,1920]{1,0:T(8,128)(2,1)S(1)}, bf16[64,1920]{1,0:T(8,128)(2,1)S(1)}, u32[]{:S(2)}, u32[]{:S(2)}) collective-permute-start(bf16[64,1920]{1,0:T(8,128)(2,1)S(1)} %get-tuple-element.39), channel_id=1, source_target_pairs={{0,4},{1,5},{2,6},{3,7},{4,0},{5,1},{6,2},{7,3},{8,12},{9,13},{10,... | collective-permute-start | bytes 737288 | tf_op jit(solution)/shard_map/ppermute | solution.py:399
  63.5 0.6 collective-permute-start.15
  64.1 2.6 %collective-permute-start.16 = (bf16[64,1920]{1,0:T(8,128)(2,1)S(1)}, bf16[64,1920]{1,0:T(8,128)(2,1)S(1)}, u32[]{:S(2)}, u32[]{:S(2)}) collective-permute-start(bf16[64,1920]{1,0:T(8,128)(2,1)S(1)} %get-tuple-element.41), channel_id=1, source_target_pairs={{0,6},{1,7},{2,0},{3,1},{4,2},{5,3},{6,4},{7,5},{8,14},{9,15},{10,... | collective-permute-start | bytes 737288 | tf_op jit(solution)/shard_map/ppermute | solution.py:399
  66.7 4.0 %collective-permute-done.14.g1_ref = bf16[64,1920]{1,0:T(8,128)(2,1)S(1)} collective-permute-done((bf16[64,1920]{1,0:T(8,128)(2,1)S(1)}, bf16[64,1920]{1,0:T(8,128)(2,1)S(1)}, u32[]{:S(2)}, u32[]{:S(2)}) %collective-permute-start.14) | collective-permute-done | bytes 245792 | tf_op jit(solution)/shard_map/ppermute | solution.py:399
  70.8 4.9 %collective-permute-done.15.g2_ref = bf16[64,1920]{1,0:T(8,128)(2,1)S(1)} collective-permute-done((bf16[64,1920]{1,0:T(8,128)(2,1)S(1)}, bf16[64,1920]{1,0:T(8,128)(2,1)S(1)}, u32[]{:S(2)}, u32[]{:S(2)}) %collective-permute-start.15) | collective-permute-done | bytes 245792 | tf_op jit(solution)/shard_map/ppermute | solution.py:399
  75.6 0.1 collective-permute-done.16.g3_ref
  75.7 0.1 collective-permute-done.13.recv_ref
  75.8 0.2 sum_first.1
  76.1 3.1 %collective-permute-start.17 = (bf16[32,2304]{1,0:T(8,128)(2,1)S(1)}, bf16[32,2304]{1,0:T(8,128)(2,1)S(1)}, u32[]{:S(2)}, u32[]{:S(2)}) collective-permute-start(bf16[32,2304]{1,0:T(8,128)(2,1)S(1)} %get-tuple-element.43), channel_id=1, source_target_pairs={{0,4},{1,5},{2,6},{3,7},{4,0},{5,1},{6,2},{7,3},{8,12},{9,13},{10,... | collective-permute-start | bytes 442376 | tf_op jit(solution)/shard_map/ppermute | solution.py:410
  79.2 0.6 collective-permute-start.18
  79.8 2.6 %collective-permute-start.19 = (bf16[32,2304]{1,0:T(8,128)(2,1)S(1)}, bf16[32,2304]{1,0:T(8,128)(2,1)S(1)}, u32[]{:S(2)}, u32[]{:S(2)}) collective-permute-start(bf16[32,2304]{1,0:T(8,128)(2,1)S(1)} %get-tuple-element.45), channel_id=1, source_target_pairs={{0,6},{1,7},{2,0},{3,1},{4,2},{5,3},{6,4},{7,5},{8,14},{9,15},{10,... | collective-permute-start | bytes 442376 | tf_op jit(solution)/shard_map/ppermute | solution.py:410
  82.4 0.7 collective-permute-start.20
  83.1 4.2 %collective-permute-done.20.give_ref = bf16[32,1920]{1,0:T(8,128)(2,1)S(1)} collective-permute-done((bf16[32,1920]{1,0:T(8,128)(2,1)S(1)}, bf16[32,1920]{1,0:T(8,128)(2,1)S(1)}, u32[]{:S(2)}, u32[]{:S(2)}) %collective-permute-start.20) | collective-permute-done | bytes 122912 | tf_op jit(solution)/shard_map/ppermute | solution.py:409
  87.3 0.0 collective-permute-done.17.f1_ref
  87.3 0.8 sum_last.1
  (17 shorter events, 0.0 us)
Async XLA Ops:
  2.2 7.0 %collective-permute-start = (bf16[512,128]{1,0:T(8,128)(2,1)}, bf16[512,128]{1,0:T(8,128)(2,1)S(1)}, u32[]{:S(2)}, u32[]{:S(2)}) collective-permute-start(bf16[512,128]{1,0:T(8,128)(2,1)} %pack_own.1.own_ref), channel_id=1, source_target_pairs={{0,16},{8,24},{16,0},{24,8},{32,48},{40,56},{48,32},{56,40},{64,80... | collective-permute-start | bytes 393224 | tf_op jit(solution)/shard_map/ppermute | solution.py:293
  5.5 11.0 %collective-permute-start.3 = (bf16[512,128]{1,0:T(8,128)(2,1)}, bf16[512,128]{1,0:T(8,128)(2,1)S(1)}, u32[]{:S(2)}, u32[]{:S(2)}) collective-permute-start(bf16[512,128]{1,0:T(8,128)(2,1)} %pack_own.1.own_ref), channel_id=1, source_target_pairs={{0,128},{8,136},{16,144},{24,152},{32,160},{40,168},{48,176},{56,1... | collective-permute-start | bytes 393224 | tf_op jit(solution)/shard_map/ppermute | solution.py:293
  5.6 11.5 %collective-permute-start.2 = (bf16[512,128]{1,0:T(8,128)(2,1)}, bf16[512,128]{1,0:T(8,128)(2,1)S(1)}, u32[]{:S(2)}, u32[]{:S(2)}) collective-permute-start(bf16[512,128]{1,0:T(8,128)(2,1)} %pack_own.1.own_ref), channel_id=1, source_target_pairs={{0,8},{8,0},{16,24},{24,16},{32,40},{40,32},{48,56},{56,48},{64,72... | collective-permute-start | bytes 393224 | tf_op jit(solution)/shard_map/ppermute | solution.py:293
  9.2 7.9 %collective-permute-start.1 = (bf16[512,128]{1,0:T(8,128)(2,1)S(1)}, bf16[512,128]{1,0:T(8,128)(2,1)S(1)}, u32[]{:S(2)}, u32[]{:S(2)}) collective-permute-start(bf16[512,128]{1,0:T(8,128)(2,1)S(1)} %collective-permute-done.y_ref), channel_id=1, source_target_pairs={{0,8},{8,0},{16,24},{24,16},{32,40},{40,32},{48,56},{56,48},{64,72... | collective-permute-start | bytes 393224 | tf_op jit(solution)/shard_map/ppermute | solution.py:293
  9.2 7.9 %copy-start = (bf16[512,128]{1,0:T(8,128)(2,1)S(1)}, bf16[512,128]{1,0:T(8,128)(2,1)}, u32[]{:S(2)}) copy-start(bf16[512,128]{1,0:T(8,128)(2,1)} %pack_own.1.own_ref) | copy-start | bytes 393220
  10.0 13.4 %copy-start.3 = (bf16[256,1024]{1,0:T(8,128)(2,1)S(1)}, bf16[256,1024]{1,0:T(8,128)(2,1)}, u32[]{:S(2)}) copy-start(bf16[256,1024]{1,0:T(8,128)(2,1)} %q_ref.3) | copy-start | bytes 1572868
  16.4 0.7 copy-start.1
  17.7 10.5 %collective-permute-start.4 = (bf16[2048,128]{1,0:T(8,128)(2,1)S(1)}, bf16[2048,128]{1,0:T(8,128)(2,1)S(1)}, u32[]{:S(2)}, u32[]{:S(2)}) collective-permute-start(bf16[2048,128]{1,0:T(8,128)(2,1)S(1)} %get-tuple-element.25.kv_ref), channel_id=1, source_target_pairs={{0,32},{8,232},{16,48},{24,248},{32,64},{40,8},{48,80},{56,24},{64... | collective-permute-start | bytes 1572872 | tf_op jit(solution)/shard_map/ppermute | solution.py:293
  19.7 9.2 %collective-permute-start.8 = (bf16[512,128]{1,0:T(8,128)(2,1)S(1)}, bf16[512,128]{1,0:T(8,128)(2,1)S(1)}, u32[]{:S(2)}, u32[]{:S(2)}) collective-permute-start(bf16[512,128]{1,0:T(8,128)(2,1)S(1)} %get-tuple-element.28.refs_1_), channel_id=1, source_target_pairs={{0,16},{8,24},{16,0},{24,8},{32,48},{40,56},{48,32},{56,40},{64,80... | collective-permute-start | bytes 393224 | tf_op jit(solution)/shard_map/ppermute | solution.py:293
  20.1 8.8 %collective-permute-start.7 = (bf16[512,128]{1,0:T(8,128)(2,1)S(1)}, bf16[512,128]{1,0:T(8,128)(2,1)S(1)}, u32[]{:S(2)}, u32[]{:S(2)}) collective-permute-start(bf16[512,128]{1,0:T(8,128)(2,1)S(1)} %get-tuple-element.28.refs_1_), channel_id=1, source_target_pairs={{0,24},{8,16},{16,8},{24,0},{32,56},{40,48},{48,40},{56,32},{64,88... | collective-permute-start | bytes 393224 | tf_op jit(solution)/shard_map/ppermute | solution.py:293
  20.7 8.3 %collective-permute-start.6 = (bf16[512,128]{1,0:T(8,128)(2,1)S(1)}, bf16[512,128]{1,0:T(8,128)(2,1)S(1)}, u32[]{:S(2)}, u32[]{:S(2)}) collective-permute-start(bf16[512,128]{1,0:T(8,128)(2,1)S(1)} %get-tuple-element.28.refs_1_), channel_id=1, source_target_pairs={{0,8},{8,0},{16,24},{24,16},{32,40},{40,32},{48,56},{56,48},{64,72... | collective-permute-start | bytes 393224 | tf_op jit(solution)/shard_map/ppermute | solution.py:293
  28.2 10.4 %collective-permute-start.5 = (bf16[2048,128]{1,0:T(8,128)(2,1)S(1)}, bf16[2048,128]{1,0:T(8,128)(2,1)S(1)}, u32[]{:S(2)}, u32[]{:S(2)}) collective-permute-start(bf16[2048,128]{1,0:T(8,128)(2,1)S(1)} %gate.5.refs_0_), channel_id=1, source_target_pairs={{0,32},{8,232},{16,48},{24,248},{32,64},{40,8},{48,80},{56,24},{64... | collective-permute-start | bytes 1572872 | tf_op jit(solution)/shard_map/ppermute | solution.py:293
  28.9 9.7 %collective-permute-start.10 = (bf16[2048,128]{1,0:T(8,128)(2,1)S(1)}, bf16[2048,128]{1,0:T(8,128)(2,1)S(1)}, u32[]{:S(2)}, u32[]{:S(2)}) collective-permute-start(bf16[2048,128]{1,0:T(8,128)(2,1)S(1)} %gate.5.refs_0_), channel_id=1, source_target_pairs={{0,8},{8,0},{16,24},{24,16},{32,40},{40,32},{48,56},{56,48},{64,72... | collective-permute-start | bytes 1572872 | tf_op jit(solution)/shard_map/ppermute | solution.py:293
  38.6 10.4 %collective-permute-start.9 = (bf16[2048,128]{1,0:T(8,128)(2,1)S(1)}, bf16[2048,128]{1,0:T(8,128)(2,1)S(1)}, u32[]{:S(2)}, u32[]{:S(2)}) collective-permute-start(bf16[2048,128]{1,0:T(8,128)(2,1)S(1)} %gate.6.refs_1_), channel_id=1, source_target_pairs={{0,32},{8,232},{16,48},{24,248},{32,64},{40,8},{48,80},{56,24},{64... | collective-permute-start | bytes 1572872 | tf_op jit(solution)/shard_map/ppermute | solution.py:293
  38.6 10.4 %collective-permute-start.12 = (bf16[2048,128]{1,0:T(8,128)(2,1)S(1)}, bf16[2048,128]{1,0:T(8,128)(2,1)S(1)}, u32[]{:S(2)}, u32[]{:S(2)}) collective-permute-start(bf16[2048,128]{1,0:T(8,128)(2,1)S(1)} %gate.6.refs_1_), channel_id=1, source_target_pairs={{0,8},{8,0},{16,24},{24,16},{32,40},{40,32},{48,56},{56,48},{64,72... | collective-permute-start | bytes 1572872 | tf_op jit(solution)/shard_map/ppermute | solution.py:293
  49.0 4.3 %collective-permute-start.11 = (bf16[2048,128]{1,0:T(8,128)(2,1)S(1)}, bf16[2048,128]{1,0:T(8,128)(2,1)S(1)}, u32[]{:S(2)}, u32[]{:S(2)}) collective-permute-start(bf16[2048,128]{1,0:T(8,128)(2,1)S(1)} %gate.7.refs_1_), channel_id=1, source_target_pairs={{0,8},{8,0},{16,24},{24,16},{32,40},{40,32},{48,56},{56,48},{64,72... | collective-permute-start | bytes 1572872 | tf_op jit(solution)/shard_map/ppermute | solution.py:293
  49.0 4.3 %copy-start.2 = (f32[8,128]{1,0:T(8,128)S(1)}, f32[8,128]{1,0:T(8,128)}, u32[]{:S(2)}) copy-start(f32[8,128]{1,0:T(8,128)} %decode.1.__1_.step_ref) | copy-start | bytes 12292
  59.7 16.1 %collective-permute-start.13 = (bf16[128,2304]{1,0:T(8,128)(2,1)S(1)}, bf16[128,2304]{1,0:T(8,128)(2,1)S(1)}, u32[]{:S(2)}, u32[]{:S(2)}) collective-permute-start(bf16[128,2304]{1,0:T(8,128)(2,1)S(1)} %get-tuple-element.37), channel_id=1, source_target_pairs={{0,1},{1,0},{2,3},{3,2},{4,5},{5,4},{6,7},{7,6},{8,9},{9,8},{10,11... | collective-permute-start | bytes 1769480 | tf_op jit(solution)/shard_map/ppermute | solution.py:398
  60.5 10.3 %collective-permute-start.14 = (bf16[64,1920]{1,0:T(8,128)(2,1)S(1)}, bf16[64,1920]{1,0:T(8,128)(2,1)S(1)}, u32[]{:S(2)}, u32[]{:S(2)}) collective-permute-start(bf16[64,1920]{1,0:T(8,128)(2,1)S(1)} %get-tuple-element.39), channel_id=1, source_target_pairs={{0,4},{1,5},{2,6},{3,7},{4,0},{5,1},{6,2},{7,3},{8,12},{9,13},{10,... | collective-permute-start | bytes 737288 | tf_op jit(solution)/shard_map/ppermute | solution.py:399
  63.5 12.1 %collective-permute-start.15 = (bf16[64,1920]{1,0:T(8,128)(2,1)S(1)}, bf16[64,1920]{1,0:T(8,128)(2,1)S(1)}, u32[]{:S(2)}, u32[]{:S(2)}) collective-permute-start(bf16[64,1920]{1,0:T(8,128)(2,1)S(1)} %get-tuple-element.40), channel_id=1, source_target_pairs={{0,2},{1,3},{2,4},{3,5},{4,6},{5,7},{6,0},{7,1},{8,10},{9,11},{10,... | collective-permute-start | bytes 737288 | tf_op jit(solution)/shard_map/ppermute | solution.py:399
  64.1 11.7 %collective-permute-start.16 = (bf16[64,1920]{1,0:T(8,128)(2,1)S(1)}, bf16[64,1920]{1,0:T(8,128)(2,1)S(1)}, u32[]{:S(2)}, u32[]{:S(2)}) collective-permute-start(bf16[64,1920]{1,0:T(8,128)(2,1)S(1)} %get-tuple-element.41), channel_id=1, source_target_pairs={{0,6},{1,7},{2,0},{3,1},{4,2},{5,3},{6,4},{7,5},{8,14},{9,15},{10,... | collective-permute-start | bytes 737288 | tf_op jit(solution)/shard_map/ppermute | solution.py:399
  76.1 11.2 %collective-permute-start.17 = (bf16[32,2304]{1,0:T(8,128)(2,1)S(1)}, bf16[32,2304]{1,0:T(8,128)(2,1)S(1)}, u32[]{:S(2)}, u32[]{:S(2)}) collective-permute-start(bf16[32,2304]{1,0:T(8,128)(2,1)S(1)} %get-tuple-element.43), channel_id=1, source_target_pairs={{0,4},{1,5},{2,6},{3,7},{4,0},{5,1},{6,2},{7,3},{8,12},{9,13},{10,... | collective-permute-start | bytes 442376 | tf_op jit(solution)/shard_map/ppermute | solution.py:410
  79.2 8.1 %collective-permute-start.18 = (bf16[32,2304]{1,0:T(8,128)(2,1)S(1)}, bf16[32,2304]{1,0:T(8,128)(2,1)S(1)}, u32[]{:S(2)}, u32[]{:S(2)}) collective-permute-start(bf16[32,2304]{1,0:T(8,128)(2,1)S(1)} %get-tuple-element.44), channel_id=1, source_target_pairs={{0,2},{1,3},{2,4},{3,5},{4,6},{5,7},{6,0},{7,1},{8,10},{9,11},{10,... | collective-permute-start | bytes 442376 | tf_op jit(solution)/shard_map/ppermute | solution.py:410
  79.8 7.5 %collective-permute-start.19 = (bf16[32,2304]{1,0:T(8,128)(2,1)S(1)}, bf16[32,2304]{1,0:T(8,128)(2,1)S(1)}, u32[]{:S(2)}, u32[]{:S(2)}) collective-permute-start(bf16[32,2304]{1,0:T(8,128)(2,1)S(1)} %get-tuple-element.45), channel_id=1, source_target_pairs={{0,6},{1,7},{2,0},{3,1},{4,2},{5,3},{6,4},{7,5},{8,14},{9,15},{10,... | collective-permute-start | bytes 442376 | tf_op jit(solution)/shard_map/ppermute | solution.py:410
  82.4 4.9 %collective-permute-start.20 = (bf16[32,1920]{1,0:T(8,128)(2,1)S(1)}, bf16[32,1920]{1,0:T(8,128)(2,1)S(1)}, u32[]{:S(2)}, u32[]{:S(2)}) collective-permute-start(bf16[32,1920]{1,0:T(8,128)(2,1)S(1)} %get-tuple-element.47), channel_id=1, source_target_pairs={{0,1},{1,0},{2,3},{3,2},{4,5},{5,4},{6,7},{7,6},{8,9},{9,8},{10,11... | collective-permute-start | bytes 368648 | tf_op jit(solution)/shard_map/ppermute | solution.py:409
